TPU v7x, 32 devices: a whole 2x2x4 slice. The times are simulated.
32 devices in a mesh: ctx: 4 (over x, core), tp: 4 (over z), fsdp: 2 (over y).
Axes of the slice: x: 2, y: 2, z: 4, core: 2. Of those that a mesh axis runs over, the one named last changes fastest.
Arguments:
- tokens: bfloat16 [8192, 8192], P(('ctx', 'fsdp'), 'tp'), may hold values from -6 to 6
- weight: bfloat16 [8192, 3, 4096], P('fsdp', None, 'tp'), may hold values from -0.0625 to 0.0625
- rate: float32 [4096, 16], P(('tp', 'fsdp')), may hold values from 1.2207031e-06 to 0.1
- residue: float32 [4096, 16], P(('tp', 'fsdp')), may hold values from -3 to 3
- skip: float32 [4096], P(('tp', 'fsdp')), may hold values from 0.5 to 1.5
- order: int32 [8], replicated, may hold values from 0 to 7, each once
Outputs:
- gated: bfloat16 [4096, 8192], P(('tp', 'fsdp'), 'ctx')
Inputs may be any that keep to these rules, and one draw needn't show every extreme that they name: order is a permutation: every segment number appears once.
All inputs are finite; a program needn't handle non-finite values.
Results may differ from a plain program's by a relative error of at most 0.006.
Values may be sent and summed in bfloat16 or wider, within the bound.
No kernel may reach another device: no remote copies, remote signals or barrier semaphores. Data moves between devices by JAX's collectives and lax.ppermute only.
A program may use at most 256 MiB of HBM per device.

v0:
```python
import functools
from typing import NamedTuple

import jax
import jax.numpy as jnp
from jax import lax
from jax.experimental import pallas as pl
from jax.experimental.pallas import tpu as pltpu
from jax.sharding import PartitionSpec as P

MIB = 1 << 20
DEPTH = 256
CHUNKS = (256, 256, 256, 256)
PASSED = (512, 512)
T = {'y_y': True, 'y3_c0': True, 'y2_A': False, 'x_x': [0, False, True, False], 'x_c': [0, 0, 1, 1], 'Ka': 'c3', 'x2_A': False, 'c_A': 9, 'c_P': [3], 'x_P': [], 'c_ser': [1, 0, 0, 0], 'E': [], 'FK': True, 'CH': [256, 256, 256, 256], 'S': {}, 'Kb': 'c3', 'cost': {'part_a': 0, 'part_b': 0, 'part_c': 0, 'project': 0}}
FREE = pl.CostEstimate(flops=0, bytes_accessed=0, transcendentals=0)


class Plan(NamedTuple):
    half_blocks: int
    part_blocks: int
    n_parts: int


def exchanged(block, axis, mask):
    count = lax.axis_size(axis)
    return lax.ppermute(block, axis, [(i, i ^ mask) for i in range(count)])


def after(value, *others):
    return lax.optimization_barrier((value, *others))[0]


def pole_gain(rate, residue, length):
    return residue * jnp.sqrt(jnp.maximum(-jnp.expm1(-2.0 * rate), 1.0 / length))


def choose(low, high, number, act):
    if high - low == 1:
        act(low)
        return
    middle = (low + high) // 2

    @pl.when(number < middle)
    def _():
        choose(low, middle, number, act)

    @pl.when(number >= middle)
    def _():
        choose(middle, high, number, act)


def fetch_weights(plan, place, p, block, own, pieces, first, target, sem):
    pair, ctx = place[0], place[1]
    local = lax.rem(block, plan.half_blocks)
    here = lax.div(block, plan.half_blocks) == pair

    @pl.when(here)
    def _():
        row = pl.multiple_of(local * DEPTH, DEPTH)
        pltpu.make_async_copy(own.at[p, pl.ds(row, DEPTH), :], target, sem).start()

    @pl.when(jnp.logical_not(here))
    def _():
        stride = len(pieces) // plan.n_parts
        number = jnp.bitwise_xor(lax.div(local, plan.part_blocks), ctx) * stride
        number = number + lax.rem(local, plan.part_blocks) - first

        def act(n):
            pltpu.make_async_copy(pieces[n].at[p], target, sem).start()

        choose(0, len(pieces), number, act)


def project_kernel(plan, n_inputs, n_pieces, first, base, final, blocks, x_plan, place, *refs):
    refs = list(refs)
    inputs = [refs.pop(0) for _ in range(n_inputs)]
    own = refs.pop(0)
    pieces = [refs.pop(0) for _ in range(n_pieces)]
    init = refs.pop(0) if base is not None else None
    outs = [refs.pop(0) for _ in range(2 if final else 1)]
    x_buf, w_buf, x_sem, w_sem = refs[:4]
    refs = refs[4:]
    if final:
        i_buf, i_sem = refs if init is not None else (None, None)
    else:
        o_buf, o_sem, i_sem = refs
        i_buf = o_buf
    pair, tp = place[0], place[2]
    rows, depth = x_buf.shape
    spans = (slice(0, depth // 2), slice(depth // 2, depth))

    def fetch(p):
        if init is not None:
            pltpu.make_async_copy(
                init.at[p, pl.ds(base, rows), :], i_buf.at[p], i_sem.at[p]
            ).start()
        for part in (0, 1):

            def one(step, carry):
                where = pl.ds(pl.multiple_of(step * DEPTH, DEPTH), DEPTH)
                block = x_plan(tp, step, inputs, x_buf.at[:, where], x_sem.at[part], p == 0)
                target = w_buf.at[p, where, :]
                fetch_weights(
                    plan, place, p, block, own, pieces, first, target, w_sem.at[p, part]
                )
                return carry

            lax.fori_loop(part * blocks // 2, (part + 1) * blocks // 2, one, 0)

    def await_part(p, part):
        if p == 0:
            target = x_buf.at[:, spans[part]]
            pltpu.make_async_copy(target, target, x_sem.at[part]).wait()
        target = w_buf.at[p, spans[part], :]
        pltpu.make_async_copy(target, target, w_sem.at[p, part]).wait()

    fetch(0)
    fetch(1)
    for p in range(3):
        if init is not None:
            pltpu.make_async_copy(i_buf.at[p], i_buf.at[p], i_sem.at[p]).wait()
        await_part(p, 0)
        if p:
            await_part(p, 1)
        if not final:
            chunk = min(rows, 256)

            def multiply(span, add, m, carry):
                some = pl.ds(pl.multiple_of(m * chunk, chunk), chunk)
                new = jnp.dot(
                    x_buf[some, span], w_buf[p, span, :], preferred_element_type=jnp.float32
                )
                if add or init is not None:
                    new = o_buf[p, some, :] + new
                o_buf[p, some, :] = new
                return carry

            if p == 0:
                lax.fori_loop(0, rows // chunk, functools.partial(multiply, spans[0], False), 0)
                await_part(0, 1)
                fetch(2)
                lax.fori_loop(0, rows // chunk, functools.partial(multiply, spans[1], True), 0)
            else:
                whole = slice(0, depth)
                lax.fori_loop(0, rows // chunk, functools.partial(multiply, whole, False), 0)
            pltpu.make_async_copy(o_buf.at[p], outs[0].at[p], o_sem.at[p]).start()
            continue
        kept, given = outs
        half = kept.shape[2]
        lanes = [pl.ds(pl.multiple_of(x * half, 128), half) for x in (pair, 1 - pair)]

        def product(span, n):
            return jnp.dot(
                x_buf[:, span], w_buf[p, span, lanes[n]], preferred_element_type=jnp.float32
            )

        if p == 0:
            early = [product(spans[0], n) for n in (0, 1)]
            await_part(0, 1)
            fetch(2)
            sums = [early[n] + product(spans[1], n) for n in (0, 1)]
        else:
            sums = [product(slice(0, depth), n) for n in (0, 1)]
        for n in (0, 1):
            new = sums[n]
            if init is not None:
                new = i_buf[p, :, lanes[n]] + new
            new = new.astype(jnp.bfloat16)
            if n == 0 or p == 0:
                outs[n][p] = new
            elif p == 1:
                given[1] = new
            else:
                both = given[1].astype(jnp.float32) * new.astype(jnp.float32)
                given[1] = both.astype(jnp.bfloat16)
    if not final:
        for p in range(3):
            pltpu.make_async_copy(o_buf.at[p], outs[0].at[p], o_sem.at[p]).wait()


def project(plan, place, inputs, own, pieces, first, init, base, rows, blocks, x_plan, name):
    final = name == "project"
    width = own.shape[2]
    anywhere = pl.BlockSpec(memory_space=pl.ANY)
    local = pl.BlockSpec(memory_space=pltpu.VMEM)
    operands = list(inputs) + [own] + list(pieces) + ([] if init is None else [init])
    depth = blocks * DEPTH
    total = (3, rows, width)
    scratch = [
        pltpu.VMEM((rows, depth), jnp.bfloat16),
        pltpu.VMEM((3, depth, width), jnp.bfloat16),
        pltpu.SemaphoreType.DMA((2,)),
        pltpu.SemaphoreType.DMA((3, 2)),
    ]
    if final:
        if init is not None:
            scratch += [pltpu.VMEM(total, jnp.float32), pltpu.SemaphoreType.DMA((3,))]
        out_shape = [
            jax.ShapeDtypeStruct((n, rows, width // 2), jnp.bfloat16) for n in (3, 2)
        ]
    else:
        scratch += [pltpu.VMEM(total, jnp.float32)] + [pltpu.SemaphoreType.DMA((3,))] * 2
        out_shape = jax.ShapeDtypeStruct(total, jnp.float32)
    return pl.pallas_call(
        functools.partial(
            project_kernel, plan, len(inputs), len(pieces), first,
            None if init is None else base, final, blocks, x_plan,
        ),
        grid_spec=pltpu.PrefetchScalarGridSpec(
            num_scalar_prefetch=1,
            grid=(),
            in_specs=[anywhere] * len(operands),
            out_specs=[local, local] if final else anywhere,
            scratch_shapes=scratch,
        ),
        out_shape=out_shape,
        compiler_params=pltpu.CompilerParams(vmem_limit_bytes=56 * MIB),
        cost_estimate=pl.CostEstimate(
            flops=T["cost"][name], bytes_accessed=0, transcendentals=0
        ),
        name=name,
    )(place, *operands)


def columns(quarter_block):
    return pl.ds(pl.multiple_of(quarter_block * DEPTH, DEPTH), DEPTH)


def gathered_plan(per_quarter):
    def plan(tp, step, inputs, target, sem, copy):
        source = inputs[0].at[lax.div(step, per_quarter), :, columns(lax.rem(step, per_quarter))]
        if copy:
            pltpu.make_async_copy(source, target, sem).start()
        return step

    return plan


def line_ends(tp):
    return (tp == 0) | (tp == 3)


def near_block(plan, tp, step, subs, base, inputs, target, sem, copy):
    span = plan.half_blocks // 2 // plan.part_blocks
    place = lax.div(step, len(subs))
    sub = subs[0] + lax.rem(step, len(subs))
    mine = place < span
    side = jnp.where(mine, lax.rem(tp, 2), 1 - lax.rem(tp, 2))
    within = lax.rem(place, span) * plan.part_blocks + sub
    block = lax.div(tp, 2) * plan.half_blocks + side * span * plan.part_blocks + within
    if not copy:
        return block
    where = columns(within)
    for at, source in ((True, inputs[0]), (False, inputs[1])):
        @pl.when(mine == at)
        def _():
            rows = pl.ds(base, target.shape[0])
            pltpu.make_async_copy(source.at[rows, where], target, sem).start()

    return block


def near_plan(plan, subs, base):
    def x_plan(tp, step, inputs, target, sem, copy):
        return near_block(plan, tp, step, subs, base, inputs, target, sem, copy)

    return x_plan


def middle_plan(plan, subs, late_subs):
    span = plan.half_blocks // plan.part_blocks * len(subs)
    per_quarter = plan.half_blocks // 2

    def x_plan(tp, step, inputs, target, sem, copy):
        middle, ends = inputs[2:]
        late = step - span
        early = jnp.minimum(step, span - 1)
        near = near_block(plan, tp, early, subs, 0, inputs, target, sem, False)
        part, sub = lax.div(late, len(late_subs)), lax.rem(late, len(late_subs))
        within = jnp.maximum(part * plan.part_blocks + late_subs[0] + sub, 0)
        block = jnp.where(late < 0, near, (2 - lax.div(tp, 2)) * per_quarter + within)
        if not copy:
            return block
        where = columns(within)

        @pl.when(late < 0)
        def _():
            near_block(plan, tp, early, subs, 0, inputs, target, sem, True)

        for at_end, source in ((False, middle), (True, ends)):
            @pl.when((late >= 0) & (line_ends(tp) == at_end))
            def _():
                pltpu.make_async_copy(source.at[:, where], target, sem).start()

        return block

    return x_plan


def last_plan(per_quarter, row, rows):
    def plan(tp, step, inputs, target, sem, copy):
        block = jnp.where(tp < 2, 3, 0) * per_quarter + step
        if not copy:
            return block
        middle, ends = inputs
        where = columns(step)

        @pl.when(line_ends(tp))
        def _():
            pltpu.make_async_copy(ends.at[:, where], target, sem).start()

        @pl.when(jnp.logical_not(line_ends(tp)))
        def _():
            pltpu.make_async_copy(middle.at[pl.ds(row, rows), where], target, sem).start()

        return block

    return plan


def scan_kernel(kept, given, decay, gain, skip, state_in, local_ref, state_out, prod):
    poles = decay.shape[0]
    rows = kept.shape[1]
    groups = kept.shape[2] // 128
    for side, ref in enumerate((kept, given)):
        for g in range(groups):
            lanes = slice(g * 128, (g + 1) * 128)
            product = ref[1, :, lanes].astype(jnp.float32)
            if side == 0:
                product = product * ref[2, :, lanes].astype(jnp.float32)
            prod[:, side * groups + g, :] = product
    direct = skip[...]
    factors = [decay[r] for r in range(poles)]
    gains = [gain[r] for r in range(poles)]

    def step(t, states):
        p = prod[t]
        new = [factors[r] * states[r] + gains[r] * p for r in range(poles)]
        total = list(new)
        while len(total) > 1:
            total = [a + b for a, b in zip(total[::2], total[1::2])]
        local_ref[t] = total[0] + direct * p
        return tuple(new)

    states = lax.fori_loop(0, rows, step, tuple(state_in[r] for r in range(poles)), unroll=8)
    for r in range(poles):
        state_out[r] = states[r]


def scan(kept, given, decay, gain, skip, state):
    rows = kept.shape[1]
    local = pl.BlockSpec(memory_space=pltpu.VMEM)
    lanes = decay.shape[1:]
    return pl.pallas_call(
        scan_kernel,
        in_specs=[local] * 6,
        out_specs=[local] * 2,
        out_shape=[
            jax.ShapeDtypeStruct((rows,) + lanes, jnp.float32),
            jax.ShapeDtypeStruct(decay.shape, jnp.float32),
        ],
        scratch_shapes=[pltpu.VMEM((rows,) + lanes, jnp.float32)],
        compiler_params=pltpu.CompilerParams(vmem_limit_bytes=24 * MIB),
        cost_estimate=FREE,
        name="scan",
    )(kept, given, decay, gain, skip, state)


def carry_kernel(n_ctx, seg_len, place, order, rate, weights):
    poles, sublanes, _ = rate.shape
    pair, ctx = place[0], place[1]
    upper = lax.broadcasted_iota(jnp.int32, rate.shape[1:], 0) < sublanes // 2
    targets = (order[2 * ctx + pair], order[2 * ctx + 1 - pair])
    for mask in range(n_ctx):
        origin = jnp.bitwise_xor(ctx, mask)
        sources = (order[2 * origin + pair], order[2 * origin + 1 - pair])
        for cross in (0, 1):
            gaps = [targets[s] - 1 - sources[s ^ cross] for s in (0, 1)]
            gap = jnp.where(upper, gaps[0], gaps[1])
            span = jnp.maximum(gap, 0).astype(jnp.float32) * seg_len
            for r in range(poles):
                weights[mask, cross, r] = jnp.where(gap >= 0, jnp.exp(-rate[r] * span), 0.0)


def carry(place, order, rate, n_ctx, seg_len):
    local = pl.BlockSpec(memory_space=pltpu.VMEM)
    return pl.pallas_call(
        functools.partial(carry_kernel, n_ctx, seg_len),
        grid_spec=pltpu.PrefetchScalarGridSpec(
            num_scalar_prefetch=2, grid=(), in_specs=[local], out_specs=local
        ),
        out_shape=jax.ShapeDtypeStruct((n_ctx, 2) + rate.shape, jnp.float32),
        cost_estimate=FREE,
        name="carry",
    )(place, order, rate)


def finish_kernel(n_ctx, n_chunks, seg_len, place, *refs):
    refs = list(refs)
    ends = [refs.pop(0) for _ in range(n_ctx)]
    weights = refs.pop(0)
    decay = refs.pop(0)
    locals_ = [refs.pop(0) for _ in range(n_chunks)]
    kept = [refs.pop(0) for _ in range(n_chunks)]
    given = [refs.pop(0) for _ in range(n_chunks)]
    out = refs.pop(0)
    conv = refs.pop(0)
    poles, sublanes, _ = decay.shape
    groups = sublanes // 2
    pair = place[0]
    states = [jnp.zeros(decay.shape[1:], jnp.float32) for _ in range(poles)]
    for mask in range(n_ctx):
        for r in range(poles):
            end = ends[mask][r]
            turned = jnp.concatenate([end[groups:], end[:groups]], axis=0)
            states[r] = states[r] + weights[mask, 0, r] * end + weights[mask, 1, r] * turned
    factors = [decay[r] for r in range(poles)]
    states = tuple(states)
    base = 0
    for k in range(n_chunks):
        rows = locals_[k].shape[0]

        def step(t, states):
            new = [factors[r] * states[r] for r in range(poles)]
            total = list(new)
            while len(total) > 1:
                total = [a + b for a, b in zip(total[::2], total[1::2])]
            conv[t] = total[0] + locals_[k][t]
            return tuple(new)

        states = lax.fori_loop(0, rows, step, states, unroll=8)
        for side, ref in enumerate((kept[k], given[k])):
            segment = pair if side == 0 else 1 - pair
            column = pl.multiple_of(segment * seg_len + base, 128)
            for g in range(groups):
                lanes = slice(g * 128, (g + 1) * 128)
                query = ref[0, :, lanes].astype(jnp.float32)
                gated = query * conv[:rows, side * groups + g, :]
                out[lanes, pl.ds(column, rows)] = gated.astype(jnp.bfloat16).T
        base += rows


def finish(place, ends, weights, decay, locals_, kept, given, seg_len):
    n_chunks = len(locals_)
    local = pl.BlockSpec(memory_space=pltpu.VMEM)
    operands = list(ends) + [weights, decay] + list(locals_) + list(kept) + list(given)
    lanes = decay.shape[1:]
    channels = kept[0].shape[2]
    longest = max(k.shape[1] for k in kept)
    return pl.pallas_call(
        functools.partial(finish_kernel, len(ends), n_chunks, seg_len),
        grid_spec=pltpu.PrefetchScalarGridSpec(
            num_scalar_prefetch=1,
            grid=(),
            in_specs=[local] * len(operands),
            out_specs=local,
            scratch_shapes=[pltpu.VMEM((longest,) + lanes, jnp.float32)],
        ),
        out_shape=jax.ShapeDtypeStruct((channels, 2 * seg_len), jnp.bfloat16),
        compiler_params=pltpu.CompilerParams(vmem_limit_bytes=40 * MIB),
        cost_estimate=pl.CostEstimate(
            flops=32 * seg_len * lanes[0] * lanes[1],
            bytes_accessed=seg_len * lanes[0] * lanes[1] * 8,
            transcendentals=0,
        ),
        name="finish",
    )(place, *operands)


def per_device(tokens, weight, rate, residue, skip, order):
    seg_len = tokens.shape[0]
    n_ctx = lax.axis_size("ctx")
    seq_len = 2 * n_ctx * seg_len
    pair_index = lax.axis_index("fsdp")
    ctx_index = lax.axis_index("ctx")
    place = jnp.stack([pair_index, ctx_index, lax.axis_index("tp")]).astype(jnp.int32)

    starts = [sum(CHUNKS[:k]) for k in range(len(CHUNKS))]
    on_line = lax.axis_size("tp") == 4 and n_ctx == 4
    passed = []
    if on_line:
        near = lax.ppermute(tokens, "tp", [(0, 1), (1, 0), (2, 3), (3, 2)])
        middle = lax.ppermute(tokens, "tp", [(1, 2), (2, 1)])
        ends = lax.ppermute(middle, "tp", [(1, 0), (2, 3)])
        block = lax.slice_in_dim(near, 0, PASSED[0], axis=0)
        far_middle = [lax.ppermute(block, "tp", [(1, 2), (2, 1)])]
        passed = [ends] + far_middle

    own = weight.transpose(1, 0, 2)
    part = own.shape[1] // n_ctx
    piece_len = DEPTH
    per_part = part // piece_len
    plan = Plan(own.shape[1] // DEPTH, part // DEPTH, n_ctx)
    per_quarter = tokens.shape[1] // DEPTH
    partials = [None]

    def add_part(subs, late_subs, name):
        known = range(max(late_subs) + 1) if subs[0] < per_part - 1 else subs
        some = [pieces[m, n] for m in range(n_ctx) for n in known]
        sources, x_plan = [tokens, near], near_plan(plan, subs, 0)
        if name != "part_a":
            sources, x_plan = sources + [middle, ends], middle_plan(plan, subs, late_subs)
        units = n_ctx * len(subs) + (n_ctx // 2 * len(late_subs) if name != "part_a" else 0)
        return project(
            plan, place, sources, own, some, known[0], partials[-1], 0, seg_len, units, x_plan, name
        )

    pieces = {}
    bits = []
    while 1 << len(bits) < n_ctx:
        bits.insert(0, 1 << len(bits))
    first = []
    for sub in range(per_part):
        piece = lax.dynamic_slice_in_dim(own, ctx_index * part + sub * piece_len, piece_len, 1)
        if sub >= 2 and T["y_y"]:
            piece = after(piece, first[sub - 2])
        if sub == 3 and T["y3_c0"]:
            piece = after(piece, *[pieces[m, 0] for m in range(n_ctx)])
        if sub == 2 and T["y2_A"] and on_line:
            piece = after(piece, near, middle)
        first.append(exchanged(piece, "fsdp", 1))
        held = {0: first[sub]}
        for bit in bits:
            for mask in list(held):
                block = held[mask]
                if bit == bits[0] and sub and T["x_x"][sub]:
                    block = after(block, pieces[bit, sub - 1])
                if bit == bits[0] and sub >= 2 and T["x_c"][sub]:
                    block = after(block, *[pieces[m, sub - 2] for m in range(n_ctx)])
                if on_line:
                    if bit == bits[0] and sub == 3 and T["Ka"] == "x3":
                        block = after(block, partials[1])
                    if bit == bits[-1] and T["Ka"] == "c%d" % sub:
                        block = after(block, partials[1])
                    if bit == bits[0] and sub == 3 and T["Kb"] == "x3":
                        block = after(block, partials[2])
                    if bit == bits[-1] and sub == 3 and T["Kb"] == "c3":
                        block = after(block, partials[2])
                    if bit == bits[0] and sub == 2 and T["x2_A"]:
                        block = after(block, near, middle)
                    if bit == bits[-1] and T["c_A"] == sub:
                        block = after(block, near, middle)
                    if bit == bits[-1] and sub in T["c_P"]:
                        block = after(block, *passed)
                    if bit == bits[0] and sub in T["x_P"]:
                        block = after(block, *passed)
                if bit == bits[-1] and mask and T["c_ser"][sub]:
                    block = after(block, latest)
                latest = exchanged(block, "ctx", bit)
                held[mask | bit] = latest
        for mask in range(n_ctx):
            pieces[mask, sub] = held[mask]
        if sub == 1 and on_line:
            partials.append(add_part((0, 1), (0, 1), "part_a"))
            block = lax.slice_in_dim(near, PASSED[0], seg_len, axis=0)
            if T["FK"]:
                block = after(block, partials[1])
            far_middle.append(lax.ppermute(block, "tp", [(1, 2), (2, 1)]))
        if sub == 2 and on_line:
            partials.append(add_part((2,), (0, 1, 2), "part_b"))
    ordered = [pieces[mask, sub] for mask in range(n_ctx) for sub in range(per_part)]

    channels = rate.shape[0]
    groups = channels // 128

    def spread(values):
        lanes = values.T.reshape(-1, groups, 128)
        return jnp.concatenate([lanes, lanes], axis=1)

    rates = spread(rate)
    decay = jnp.exp(-rates)
    gain = spread(pole_gain(rate, residue, float(seq_len)))
    direct = spread(skip[:, None])[0]

    if on_line:
        most = add_part((3,), (3,), "part_c")

    weights = carry(place, order, rates, n_ctx, seg_len)
    kept, given, locals_ = [], [], []
    state = jnp.zeros_like(decay)
    states = []
    for k, (base, rows) in enumerate(zip(starts, CHUNKS)):
        if on_line:
            n, row = 0, base
            while row >= PASSED[n]:
                row -= PASSED[n]
                n += 1
            block = lax.slice_in_dim(far_middle[n], row, row + rows, axis=0)
            if k in T["E"]:
                block = after(block, most)
            last = lax.ppermute(block, "tp", [(1, 0), (2, 3)])
            if k == 0:
                last = after(last, weights)
            if k in T["S"]:
                last = after(last, states[T["S"][k]])
            keep, give = project(
                plan, place, [far_middle[n], last], own, ordered, 0, most, base, rows,
                per_quarter, last_plan(per_quarter, row, rows), "project",
            )
        else:
            block = lax.slice_in_dim(tokens, base, base + rows, axis=0)
            whole = lax.all_gather(block, "tp", axis=0, tiled=False)
            keep, give = project(
                plan, place, [whole], own, ordered, 0, None, 0, rows,
                2 * plan.half_blocks, gathered_plan(per_quarter), "project",
            )
        got = exchanged(give, "fsdp", 1)
        local, state = scan(keep, got, decay, gain, direct, state)
        states.append(state)
        kept.append(keep)
        given.append(got)
        locals_.append(local)

    ends = [state] + [exchanged(state, "ctx", mask) for mask in range(1, n_ctx)]
    return finish(place, ends, weights, decay, locals_, kept, given, seg_len)


def solution(mesh):
    placed = (
        P(("ctx", "fsdp"), "tp"),
        P("fsdp", None, "tp"),
        P(("tp", "fsdp"), None),
        P(("tp", "fsdp"), None),
        P(("tp", "fsdp")),
        P(),
    )
    return jax.shard_map(
        per_device, mesh=mesh, in_specs=placed, out_specs=P(("tp", "fsdp"), "ctx"), check_vma=False
    )
```

profile of v0, /device:TPU:9, one launch (start us, length us, event | category | flops | bytes accessed | tf_op | source)
XLA Modules:
  0.0 332.0 jit_solution(1899411479624435551)
XLA Ops:
  0.0 4.5 %collective-permute-start.14 = (bf16[1024,2048]{1,0:T(8,128)(2,1)}, bf16[1024,2048]{1,0:T(8,128)(2,1)}, u32[]{:S(2)}, u32[]{:S(2)}) collective-permute-start(bf16[1024,2048]{1,0:T(8,128)(2,1)} %refs_0_.5), channel_id=1, source_target_pairs={{2,4},{4,2},{3,5},{5,3},{10,12},{12,10},{11,13},{13,11},{18,20},{2... | collective-permute-start | bytes 12582920 | tf_op jit(solution)/shard_map/ppermute | solution.py:484
  4.5 4.8 %dynamic-slice_bitcast_fusion = (bf16[3,256,1024]{2,1,0:T(8,128)(2,1)}, bf16[3,256,1024]{2,1,0:T(8,128)(2,1)S(1)}, bf16[3,256,1024]{2,1,0:T(8,128)(2,1)S(1)}, bf16[3,256,1024]{2,1,0:T(8,128)(2,1)S(1)}) fusion(bf16[4096,3,1024]{2,0,1:T(8,128)(2,1)} %param.7, s32[]{:T(128)S(6)} %select_n.15, s32[]{:T(128)S(6)} %select_n.13, s32[]{:T(128)S(6)} %select_n.12, ...), kind=kLoop, calls=%fused_computation | loop fusion | bytes 12582928 | tf_op jit(solution)/shard_map/dynamic_slice | solution.py:515
  9.3 1.2 collective-permute-start.1
  10.7 33.3 %collective-permute-done.1.refs_3_.refs_5_ = bf16[3,256,1024]{2,1,0:T(8,128)(2,1)S(1)} collective-permute-done((bf16[3,256,1024]{2,1,0:T(8,128)(2,1)S(1)}, bf16[3,256,1024]{2,1,0:T(8,128)(2,1)S(1)}, u32[]{:S(2)}, u32[]{:S(2)}) %collective-permute-start.1) | collective-permute-done | bytes 1572896 | tf_op jit(solution)/shard_map/ppermute | solution.py:27
  44.0 3.8 %collective-permute-start.3 = (bf16[3,256,1024]{2,1,0:T(8,128)(2,1)S(1)}, bf16[3,256,1024]{2,1,0:T(8,128)(2,1)S(1)}, u32[]{:S(2)}, u32[]{:S(2)}) collective-permute-start(bf16[3,256,1024]{2,1,0:T(8,128)(2,1)S(1)} %collective-permute-done.1.refs_3_.refs_5_), channel_id=1, source_target_pairs={{0,8},{8,0},{16,24},{24,16},{1,9},{9,1},{17,25},{25,17},{2,10},{10... | collective-permute-start | bytes 4718600 | tf_op jit(solution)/shard_map/ppermute | solution.py:27
  47.8 1.2 collective-permute-start.5
  49.1 28.7 %collective-permute-done.2.refs_4_.refs_6_ = bf16[3,256,1024]{2,1,0:T(8,128)(2,1)S(1)} collective-permute-done((bf16[3,256,1024]{2,1,0:T(8,128)(2,1)S(1)}, bf16[3,256,1024]{2,1,0:T(8,128)(2,1)S(1)}, u32[]{:S(2)}, u32[]{:S(2)}) %collective-permute-start.2) | collective-permute-done | bytes 1572896 | tf_op jit(solution)/shard_map/ppermute | solution.py:27
  77.7 1.2 collective-permute-start.6
  79.0 5.0 %collective-permute-done.5.refs_7_.refs_11_ = bf16[3,256,1024]{2,1,0:T(8,128)(2,1)S(1)} collective-permute-done((bf16[3,256,1024]{2,1,0:T(8,128)(2,1)S(1)}, bf16[3,256,1024]{2,1,0:T(8,128)(2,1)S(1)}, u32[]{:S(2)}, u32[]{:S(2)}) %collective-permute-start.5) | collective-permute-done | bytes 1572896 | tf_op jit(solution)/shard_map/ppermute | solution.py:27
  85.0 1.2 collective-permute-start.11
  86.3 5.5 %collective-permute-done.refs_1_ = bf16[1024,2048]{1,0:T(8,128)(2,1)} collective-permute-done((bf16[1024,2048]{1,0:T(8,128)(2,1)}, bf16[1024,2048]{1,0:T(8,128)(2,1)}, u32[]{:S(2)}, u32[]{:S(2)}) %collective-permute-start) | collective-permute-done | bytes 4194336 | tf_op jit(solution)/shard_map/ppermute | solution.py:483
  91.8 1.5 collective-permute-start.4
  93.3 1.5 collective-permute-done.14.refs_2_
  94.8 3.4 %collective-permute-start.15 = (bf16[1024,2048]{1,0:T(8,128)(2,1)}, bf16[1024,2048]{1,0:T(8,128)(2,1)}, u32[]{:S(2)}, u32[]{:S(2)}) collective-permute-start(bf16[1024,2048]{1,0:T(8,128)(2,1)} %collective-permute-done.14.refs_2_), channel_id=1, source_target_pairs={{2,0},{4,6},{3,1},{5,7},{10,8},{12,14},{11,9},{13,15},{18,16},{20,... | collective-permute-start | bytes 12582920 | tf_op jit(solution)/shard_map/ppermute | solution.py:485
  98.1 4.8 %fusion = (bf16[512,2048]{1,0:T(8,128)(2,1)}, bf16[512,2048]{1,0:T(8,128)(2,1)}) fusion(bf16[1024,2048]{1,0:T(8,128)(2,1)} %collective-permute-done.refs_1_), kind=kLoop, calls=%fused_computation.10 | loop fusion | bytes 8388608 | tf_op jit(solution)/shard_map/slice | solution.py:486
  103.0 14.7 %collective-permute-done.6.refs_8_.refs_12_ = bf16[3,256,1024]{2,1,0:T(8,128)(2,1)} collective-permute-done((bf16[3,256,1024]{2,1,0:T(8,128)(2,1)S(1)}, bf16[3,256,1024]{2,1,0:T(8,128)(2,1)}, u32[]{:S(2)}, u32[]{:S(2)}) %collective-permute-start.6) | collective-permute-done | bytes 1572896 | tf_op jit(solution)/shard_map/ppermute | solution.py:27
  117.7 1.9 collective-permute-start.18
  121.2 1.2 collective-permute-start.12
  126.6 20.9 %part_a.1.refs_17_ = f32[3,1024,1024]{2,1,0:T(8,128)} custom-call(s32[3]{0:T(128)} %pad_add_fusion.place, bf16[1024,2048]{1,0:T(8,128)(2,1)} %refs_0_.5, bf16[1024,2048]{1,0:T(8,128)(2,1)} %collective-permute-done.refs_1_, bf16[3,4096,1024]{2,1,0:T(8,128)(2,1)} %bitcast.18, bf16[3,256,1024]{2,1,0:T(8,128)(2,1)} %copy-done.6, ...), custom_call_target="tpu_custom_call" | custom-call | tf_op jit(solution)/shard_map/part_a/pallas_call | solution.py:205
  147.6 3.1 collective-permute-start.9
  150.7 5.9 %collective-permute-done.12.refs_5_.refs_6_ = bf16[3,256,1024]{2,1,0:T(8,128)(2,1)} collective-permute-done((bf16[3,256,1024]{2,1,0:T(8,128)(2,1)}, bf16[3,256,1024]{2,1,0:T(8,128)(2,1)}, u32[]{:S(2)}, u32[]{:S(2)}) %collective-permute-start.12) | collective-permute-done | bytes 1572896 | tf_op jit(solution)/shard_map/ppermute | solution.py:27
  157.8 8.4 %collective-permute-done.18.refs_0_ = bf16[512,2048]{1,0:T(8,128)(2,1)} collective-permute-done((bf16[512,2048]{1,0:T(8,128)(2,1)}, bf16[512,2048]{1,0:T(8,128)(2,1)}, u32[]{:S(2)}, u32[]{:S(2)}) %collective-permute-start.18) | collective-permute-done | bytes 2097184 | tf_op jit(solution)/shard_map/ppermute | solution.py:487
  166.3 2.9 collective-permute-start.13
  169.2 3.1 fusion.1
  172.3 20.0 %collective-permute-done.20.refs_7_.refs_14_ = bf16[3,256,1024]{2,1,0:T(8,128)(2,1)S(1)} collective-permute-done((bf16[3,256,1024]{2,1,0:T(8,128)(2,1)}, bf16[3,256,1024]{2,1,0:T(8,128)(2,1)S(1)}, u32[]{:S(2)}, u32[]{:S(2)}) %collective-permute-start.20) | collective-permute-done | bytes 1572896 | tf_op jit(solution)/shard_map/ppermute | solution.py:27
  192.4 2.3 collective-permute-start.27
  194.6 2.3 collective-permute-start.25
  198.1 26.0 %part_b.1.refs_9_ = f32[3,1024,1024]{2,1,0:T(8,128)} custom-call(s32[3]{0:T(128)} %pad_add_fusion.place, bf16[1024,2048]{1,0:T(8,128)(2,1)} %refs_0_.5, bf16[1024,2048]{1,0:T(8,128)(2,1)} %collective-permute-done.refs_1_, bf16[1024,2048]{1,0:T(8,128)(2,1)} %collective-permute-done.14.refs_2_, bf16[1024,2048]{1,0:T(8,128)(2,1)} %collective-permute-done.15.refs_3_, ...), custom_call_target="tpu_custom_call" | custom-call | tf_op jit(solution)/shard_map/part_b/pallas_call | solution.py:205
  224.1 2.1 collective-permute-start.19
  226.4 1.8 fusion.2
  228.4 2.3 collective-permute-start.23
  230.6 2.3 collective-permute-start.10
  233.6 2.4 carry.1.refs_4_
  236.0 18.6 %part_c.1.refs_19_ = f32[3,1024,1024]{2,1,0:T(8,128)} custom-call(s32[3]{0:T(128)} %pad_add_fusion.place, bf16[1024,2048]{1,0:T(8,128)(2,1)} %refs_0_.5, bf16[1024,2048]{1,0:T(8,128)(2,1)} %collective-permute-done.refs_1_, bf16[1024,2048]{1,0:T(8,128)(2,1)} %collective-permute-done.14.refs_2_, bf16[1024,2048]{1,0:T(8,128)(2,1)} %collective-permute-done.15.refs_3_, ...), custom_call_target="tpu_custom_call" | custom-call | tf_op jit(solution)/shard_map/part_c/pallas_call | solution.py:205
  254.6 8.8 %project.7 = (bf16[3,256,512]{2,1,0:T(8,128)(2,1)}, bf16[2,256,512]{2,1,0:T(8,128)(2,1)}) custom-call(s32[3]{0:T(128)} %pad_add_fusion.place, bf16[512,2048]{1,0:T(8,128)(2,1)} %collective-permute-done.18.refs_0_, bf16[256,2048]{1,0:T(8,128)(2,1)} %collective-permute-done.27.refs_1_, bf16[3,4096,1024]{2,1,0:T(8,128)(2,1)} %bitcast.21, ...), custom_call_target="tpu_custom_call" | custom-call | tf_op jit(solution)/shard_map/project/pallas_call | solution.py:205
  264.0 8.8 %project.6 = (bf16[3,256,512]{2,1,0:T(8,128)(2,1)}, bf16[2,256,512]{2,1,0:T(8,128)(2,1)}) custom-call(s32[3]{0:T(128)} %pad_add_fusion.place, bf16[512,2048]{1,0:T(8,128)(2,1)} %collective-permute-done.18.refs_0_, bf16[256,2048]{1,0:T(8,128)(2,1)} %collective-permute-done.25.refs_1_, bf16[3,4096,1024]{2,1,0:T(8,128)(2,1)} %bitcast.22, ...), custom_call_target="tpu_custom_call" | custom-call | tf_op jit(solution)/shard_map/project/pallas_call | solution.py:205
  273.8 8.8 %project.5 = (bf16[3,256,512]{2,1,0:T(8,128)(2,1)}, bf16[2,256,512]{2,1,0:T(8,128)(2,1)}) custom-call(s32[3]{0:T(128)} %pad_add_fusion.place, bf16[512,2048]{1,0:T(8,128)(2,1)} %copy-done.16, bf16[256,2048]{1,0:T(8,128)(2,1)} %collective-permute-done.23.refs_1_, bf16[3,4096,1024]{2,1,0:T(8,128)(2,1)} %bitcast.23, bf16[3,256,1024]{2,1,0:T(8,128)(2,1)} %copy-done.6, ...), custom_call_target="tpu_custom_call" | custom-call | tf_op jit(solution)/shard_map/project/pallas_call | solution.py:205
  283.3 8.8 %project.4 = (bf16[3,256,512]{2,1,0:T(8,128)(2,1)}, bf16[2,256,512]{2,1,0:T(8,128)(2,1)}) custom-call(s32[3]{0:T(128)} %pad_add_fusion.place, bf16[512,2048]{1,0:T(8,128)(2,1)} %copy-done.16, bf16[256,2048]{1,0:T(8,128)(2,1)} %collective-permute-done.10.refs_1_, bf16[3,4096,1024]{2,1,0:T(8,128)(2,1)} %bitcast.24, bf16[3,256,1024]{2,1,0:T(8,128)(2,1)} %copy-done.6, ...), custom_call_target="tpu_custom_call" | custom-call | tf_op jit(solution)/shard_map/project/pallas_call | solution.py:205
  293.3 3.1 scan.4
  296.4 3.1 scan.5
  299.5 3.1 scan.6
  302.6 8.0 %collective-permute-done.22.given.refs_17_ = bf16[2,256,512]{2,1,0:T(8,128)(2,1)} collective-permute-done((bf16[2,256,512]{2,1,0:T(8,128)(2,1)}, bf16[2,256,512]{2,1,0:T(8,128)(2,1)}, u32[]{:S(2)}, u32[]{:S(2)}) %collective-permute-start.22) | collective-permute-done | bytes 524320 | tf_op jit(solution)/shard_map/ppermute | solution.py:27
  310.6 4.1 %scan.7 = (f32[256,8,128]{2,1,0:T(8,128)S(1)}, f32[16,8,128]{2,1,0:T(8,128)S(1)}) custom-call(bf16[3,256,512]{2,1,0:T(8,128)(2,1)S(1)} %copy-done.3, bf16[2,256,512]{2,1,0:T(8,128)(2,1)} %collective-permute-done.22.given.refs_17_, f32[16,8,128]{2,1,0:T(8,128)S(1)} %get-tuple-element.78.decay.refs_5_, f32[16,8,128]{2,1,0:T(8,128)S(1)} %pad_maximum_fusion.1.gain, ...), custom_call_target="tpu_custom_call" | custom-call | tf_op jit(solution)/shard_map/scan/pallas_call | solution.py:355
  314.7 1.3 collective-permute-start.29
  316.0 1.2 collective-permute-start.30
  317.7 2.0 collective-permute-done.30.refs_2_
  319.7 1.6 collective-permute-done.31.refs_3_
  321.3 10.7 %finish.1 = bf16[512,2048]{1,0:T(8,128)(2,1)} custom-call(s32[3]{0:T(128)S(1)} %copy-done.5, f32[16,8,128]{2,1,0:T(8,128)S(1)} %get-tuple-element.62.refs_0_, f32[16,8,128]{2,1,0:T(8,128)S(1)} %collective-permute-done.29.refs_1_, f32[16,8,128]{2,1,0:T(8,128)S(1)} %collective-permute-done.30.refs_2_, f32[16,8,128]{2,1,0:T(8,128)S(1)} %collective-permute-done.31.refs_3_, ...), custom_call_target="tpu_custom_call" | custom-call | flops 33554432 | bytes 8388608 | tf_op jit(solution)/shard_map/finish/pallas_call | solution.py:451
  (81 shorter events, 14.3 us)
Async XLA Ops:
  0.0 91.8 %collective-permute-start = (bf16[1024,2048]{1,0:T(8,128)(2,1)}, bf16[1024,2048]{1,0:T(8,128)(2,1)}, u32[]{:S(2)}, u32[]{:S(2)}) collective-permute-start(bf16[1024,2048]{1,0:T(8,128)(2,1)} %refs_0_.5), channel_id=1, source_target_pairs={{0,2},{2,0},{4,6},{6,4},{1,3},{3,1},{5,7},{7,5},{8,10},{10,8},{12,... | collective-permute-start | bytes 12582920 | tf_op jit(solution)/shard_map/ppermute | solution.py:483
  0.0 94.8 %collective-permute-start.14 = (bf16[1024,2048]{1,0:T(8,128)(2,1)}, bf16[1024,2048]{1,0:T(8,128)(2,1)}, u32[]{:S(2)}, u32[]{:S(2)}) collective-permute-start(bf16[1024,2048]{1,0:T(8,128)(2,1)} %refs_0_.5), channel_id=1, source_target_pairs={{2,4},{4,2},{3,5},{5,3},{10,12},{12,10},{11,13},{13,11},{18,20},{2... | collective-permute-start | bytes 12582920 | tf_op jit(solution)/shard_map/ppermute | solution.py:484
  9.3 34.8 %collective-permute-start.1 = (bf16[3,256,1024]{2,1,0:T(8,128)(2,1)S(1)}, bf16[3,256,1024]{2,1,0:T(8,128)(2,1)S(1)}, u32[]{:S(2)}, u32[]{:S(2)}) collective-permute-start(bf16[3,256,1024]{2,1,0:T(8,128)(2,1)S(1)} %get-tuple-element.69), channel_id=1, source_target_pairs={{0,1},{1,0},{2,3},{3,2},{4,5},{5,4},{6,7},{7,6},{8,9},{9,8},{10,11... | collective-permute-start | bytes 4718600 | tf_op jit(solution)/shard_map/ppermute | solution.py:27
  10.5 67.2 %collective-permute-start.2 = (bf16[3,256,1024]{2,1,0:T(8,128)(2,1)S(1)}, bf16[3,256,1024]{2,1,0:T(8,128)(2,1)S(1)}, u32[]{:S(2)}, u32[]{:S(2)}) collective-permute-start(bf16[3,256,1024]{2,1,0:T(8,128)(2,1)S(1)} %get-tuple-element.68), channel_id=1, source_target_pairs={{0,1},{1,0},{2,3},{3,2},{4,5},{5,4},{6,7},{7,6},{8,9},{9,8},{10,11... | collective-permute-start | bytes 4718600 | tf_op jit(solution)/shard_map/ppermute | solution.py:27
  44.0 59.0 %copy-start.6 = (bf16[3,256,1024]{2,1,0:T(8,128)(2,1)}, bf16[3,256,1024]{2,1,0:T(8,128)(2,1)S(1)}, u32[]{:S(2)}) copy-start(bf16[3,256,1024]{2,1,0:T(8,128)(2,1)S(1)} %collective-permute-done.1.refs_3_.refs_5_) | copy-start | bytes 4718596
  44.0 34.9 %collective-permute-start.3 = (bf16[3,256,1024]{2,1,0:T(8,128)(2,1)S(1)}, bf16[3,256,1024]{2,1,0:T(8,128)(2,1)S(1)}, u32[]{:S(2)}, u32[]{:S(2)}) collective-permute-start(bf16[3,256,1024]{2,1,0:T(8,128)(2,1)S(1)} %collective-permute-done.1.refs_3_.refs_5_), channel_id=1, source_target_pairs={{0,8},{8,0},{16,24},{24,16},{1,9},{9,1},{17,25},{25,17},{2,10},{10... | collective-permute-start | bytes 4718600 | tf_op jit(solution)/shard_map/ppermute | solution.py:27
  47.8 36.1 %collective-permute-start.5 = (bf16[3,256,1024]{2,1,0:T(8,128)(2,1)S(1)}, bf16[3,256,1024]{2,1,0:T(8,128)(2,1)S(1)}, u32[]{:S(2)}, u32[]{:S(2)}) collective-permute-start(bf16[3,256,1024]{2,1,0:T(8,128)(2,1)S(1)} %collective-permute-done.1.refs_3_.refs_5_), channel_id=1, source_target_pairs={{0,16},{8,24},{16,0},{24,8},{1,17},{9,25},{17,1},{25,9},{2,18},{10... | collective-permute-start | bytes 4718600 | tf_op jit(solution)/shard_map/ppermute | solution.py:27
  77.7 25.3 %copy-start.7 = (bf16[3,256,1024]{2,1,0:T(8,128)(2,1)}, bf16[3,256,1024]{2,1,0:T(8,128)(2,1)S(1)}, u32[]{:S(2)}) copy-start(bf16[3,256,1024]{2,1,0:T(8,128)(2,1)S(1)} %collective-permute-done.2.refs_4_.refs_6_) | copy-start | bytes 4718596
  77.7 39.9 %collective-permute-start.6 = (bf16[3,256,1024]{2,1,0:T(8,128)(2,1)S(1)}, bf16[3,256,1024]{2,1,0:T(8,128)(2,1)}, u32[]{:S(2)}, u32[]{:S(2)}) collective-permute-start(bf16[3,256,1024]{2,1,0:T(8,128)(2,1)S(1)} %collective-permute-done.2.refs_4_.refs_6_), channel_id=1, source_target_pairs={{0,16},{8,24},{16,0},{24,8},{1,17},{9,25},{17,1},{25,9},{2,18},{10... | collective-permute-start | bytes 4718600 | tf_op jit(solution)/shard_map/ppermute | solution.py:27
  78.9 7.3 %copy-start.8 = (bf16[3,256,1024]{2,1,0:T(8,128)(2,1)}, bf16[3,256,1024]{2,1,0:T(8,128)(2,1)S(1)}, u32[]{:S(2)}) copy-start(bf16[3,256,1024]{2,1,0:T(8,128)(2,1)S(1)} %collective-permute-done.3.refs_5_.refs_8_.refs_7_) | copy-start | bytes 4718596
  84.0 19.0 %copy-start.9 = (bf16[3,256,1024]{2,1,0:T(8,128)(2,1)}, bf16[3,256,1024]{2,1,0:T(8,128)(2,1)S(1)}, u32[]{:S(2)}) copy-start(bf16[3,256,1024]{2,1,0:T(8,128)(2,1)S(1)} %collective-permute-done.5.refs_7_.refs_11_) | copy-start | bytes 4718596
  84.0 35.6 %collective-permute-start.7 = (bf16[3,256,1024]{2,1,0:T(8,128)(2,1)S(1)}, bf16[3,256,1024]{2,1,0:T(8,128)(2,1)S(1)}, u32[]{:S(2)}, u32[]{:S(2)}) collective-permute-start(bf16[3,256,1024]{2,1,0:T(8,128)(2,1)S(1)} %collective-permute-done.5.refs_7_.refs_11_), channel_id=1, source_target_pairs={{0,8},{8,0},{16,24},{24,16},{1,9},{9,1},{17,25},{25,17},{2,10},{10... | collective-permute-start | bytes 4718600 | tf_op jit(solution)/shard_map/ppermute | solution.py:27
  85.0 36.1 %collective-permute-start.11 = (bf16[3,256,1024]{2,1,0:T(8,128)(2,1)S(1)}, bf16[3,256,1024]{2,1,0:T(8,128)(2,1)}, u32[]{:S(2)}, u32[]{:S(2)}) collective-permute-start(bf16[3,256,1024]{2,1,0:T(8,128)(2,1)S(1)} %get-tuple-element.38), channel_id=1, source_target_pairs={{0,1},{1,0},{2,3},{3,2},{4,5},{5,4},{6,7},{7,6},{8,9},{9,8},{10,11... | collective-permute-start | bytes 4718600 | tf_op jit(solution)/shard_map/ppermute | solution.py:27
  91.8 30.7 %collective-permute-start.4 = (bf16[3,256,1024]{2,1,0:T(8,128)(2,1)S(1)}, bf16[3,256,1024]{2,1,0:T(8,128)(2,1)S(1)}, u32[]{:S(2)}, u32[]{:S(2)}) collective-permute-start(bf16[3,256,1024]{2,1,0:T(8,128)(2,1)S(1)} %collective-permute-done.2.refs_4_.refs_6_), channel_id=1, source_target_pairs={{0,8},{8,0},{16,24},{24,16},{1,9},{9,1},{17,25},{25,17},{2,10},{10... | collective-permute-start | bytes 4718600 | tf_op jit(solution)/shard_map/ppermute | solution.py:27
  94.8 102.2 %collective-permute-start.15 = (bf16[1024,2048]{1,0:T(8,128)(2,1)}, bf16[1024,2048]{1,0:T(8,128)(2,1)}, u32[]{:S(2)}, u32[]{:S(2)}) collective-permute-start(bf16[1024,2048]{1,0:T(8,128)(2,1)} %collective-permute-done.14.refs_2_), channel_id=1, source_target_pairs={{2,0},{4,6},{3,1},{5,7},{10,8},{12,14},{11,9},{13,15},{18,16},{20,... | collective-permute-start | bytes 12582920 | tf_op jit(solution)/shard_map/ppermute | solution.py:485
  117.7 48.6 %collective-permute-start.18 = (bf16[512,2048]{1,0:T(8,128)(2,1)}, bf16[512,2048]{1,0:T(8,128)(2,1)}, u32[]{:S(2)}, u32[]{:S(2)}) collective-permute-start(bf16[512,2048]{1,0:T(8,128)(2,1)} %get-tuple-element.71), channel_id=1, source_target_pairs={{2,4},{4,2},{3,5},{5,3},{10,12},{12,10},{11,13},{13,11},{18,20},{2... | collective-permute-start | bytes 6291464 | tf_op jit(solution)/shard_map/ppermute | solution.py:487
  119.6 2.8 copy-start.10
  119.6 5.8 %collective-permute-start.8 = (bf16[3,256,1024]{2,1,0:T(8,128)(2,1)}, bf16[3,256,1024]{2,1,0:T(8,128)(2,1)S(1)}, u32[]{:S(2)}, u32[]{:S(2)}) collective-permute-start(bf16[3,256,1024]{2,1,0:T(8,128)(2,1)} %collective-permute-done.6.refs_8_.refs_12_), channel_id=1, source_target_pairs={{0,8},{8,0},{16,24},{24,16},{1,9},{9,1},{17,25},{25,17},{2,10},{10... | collective-permute-start | bytes 4718600 | tf_op jit(solution)/shard_map/ppermute | solution.py:27
  121.2 35.5 %collective-permute-start.12 = (bf16[3,256,1024]{2,1,0:T(8,128)(2,1)}, bf16[3,256,1024]{2,1,0:T(8,128)(2,1)}, u32[]{:S(2)}, u32[]{:S(2)}) collective-permute-start(bf16[3,256,1024]{2,1,0:T(8,128)(2,1)} %get-tuple-element.40), channel_id=1, source_target_pairs={{0,1},{1,0},{2,3},{3,2},{4,5},{5,4},{6,7},{7,6},{8,9},{9,8},{10,11... | collective-permute-start | bytes 4718600 | tf_op jit(solution)/shard_map/ppermute | solution.py:27
  123.6 45.6 %collective-permute-start.16 = (bf16[3,256,1024]{2,1,0:T(8,128)(2,1)}, bf16[3,256,1024]{2,1,0:T(8,128)(2,1)}, u32[]{:S(2)}, u32[]{:S(2)}) collective-permute-start(bf16[3,256,1024]{2,1,0:T(8,128)(2,1)} %collective-permute-done.11.refs_7_.refs_5_), channel_id=1, source_target_pairs={{0,16},{8,24},{16,0},{24,8},{1,17},{9,25},{17,1},{25,9},{2,18},{10... | collective-permute-start | bytes 4718600 | tf_op jit(solution)/shard_map/ppermute | solution.py:27
  147.6 78.8 %collective-permute-start.9 = (bf16[512,2048]{1,0:T(8,128)(2,1)}, bf16[512,2048]{1,0:T(8,128)(2,1)S(1)}, u32[]{:S(2)}, u32[]{:S(2)}) collective-permute-start(bf16[512,2048]{1,0:T(8,128)(2,1)} %get-tuple-element.37), channel_id=1, source_target_pairs={{2,4},{4,2},{3,5},{5,3},{10,12},{12,10},{11,13},{13,11},{18,20},{2... | collective-permute-start | bytes 6291464 | tf_op jit(solution)/shard_map/ppermute | solution.py:559
  156.6 35.7 %collective-permute-start.20 = (bf16[3,256,1024]{2,1,0:T(8,128)(2,1)}, bf16[3,256,1024]{2,1,0:T(8,128)(2,1)S(1)}, u32[]{:S(2)}, u32[]{:S(2)}) collective-permute-start(bf16[3,256,1024]{2,1,0:T(8,128)(2,1)} %collective-permute-done.12.refs_5_.refs_6_), channel_id=1, source_target_pairs={{0,16},{8,24},{16,0},{24,8},{1,17},{9,25},{17,1},{25,9},{2,18},{10... | collective-permute-start | bytes 4718600 | tf_op jit(solution)/shard_map/ppermute | solution.py:27
  166.3 28.4 %collective-permute-start.13 = (bf16[3,256,1024]{2,1,0:T(8,128)(2,1)}, bf16[3,256,1024]{2,1,0:T(8,128)(2,1)S(1)}, u32[]{:S(2)}, u32[]{:S(2)}) collective-permute-start(bf16[3,256,1024]{2,1,0:T(8,128)(2,1)} %collective-permute-done.11.refs_7_.refs_5_), channel_id=1, source_target_pairs={{0,8},{8,0},{16,24},{24,16},{1,9},{9,1},{17,25},{25,17},{2,10},{10... | collective-permute-start | bytes 4718600 | tf_op jit(solution)/shard_map/ppermute | solution.py:27
  169.2 27.7 %collective-permute-start.17 = (bf16[3,256,1024]{2,1,0:T(8,128)(2,1)}, bf16[3,256,1024]{2,1,0:T(8,128)(2,1)S(1)}, u32[]{:S(2)}, u32[]{:S(2)}) collective-permute-start(bf16[3,256,1024]{2,1,0:T(8,128)(2,1)} %collective-permute-done.16.refs_13_), channel_id=1, source_target_pairs={{0,8},{8,0},{16,24},{24,16},{1,9},{9,1},{17,25},{25,17},{2,10},{10... | collective-permute-start | bytes 4718600 | tf_op jit(solution)/shard_map/ppermute | solution.py:27
  192.4 33.9 %copy-start.13 = (bf16[3,256,1024]{2,1,0:T(8,128)(2,1)}, bf16[3,256,1024]{2,1,0:T(8,128)(2,1)S(1)}, u32[]{:S(2)}) copy-start(bf16[3,256,1024]{2,1,0:T(8,128)(2,1)S(1)} %collective-permute-done.20.refs_7_.refs_14_) | copy-start | bytes 4718596
  192.4 38.3 %collective-permute-start.27 = (bf16[256,2048]{1,0:T(8,128)(2,1)}, bf16[256,2048]{1,0:T(8,128)(2,1)}, u32[]{:S(2)}, u32[]{:S(2)}) collective-permute-start(bf16[256,2048]{1,0:T(8,128)(2,1)} %get-tuple-element.73), channel_id=1, source_target_pairs={{2,0},{4,6},{3,1},{5,7},{10,8},{12,14},{11,9},{13,15},{18,16},{20,... | collective-permute-start | bytes 3145736 | tf_op jit(solution)/shard_map/ppermute | solution.py:592
  194.6 2.3 copy-start.14
  194.6 69.4 %collective-permute-start.25 = (bf16[256,2048]{1,0:T(8,128)(2,1)}, bf16[256,2048]{1,0:T(8,128)(2,1)}, u32[]{:S(2)}, u32[]{:S(2)}) collective-permute-start(bf16[256,2048]{1,0:T(8,128)(2,1)} %get-tuple-element.74), channel_id=1, source_target_pairs={{2,0},{4,6},{3,1},{5,7},{10,8},{12,14},{11,9},{13,15},{18,16},{20,... | collective-permute-start | bytes 3145736 | tf_op jit(solution)/shard_map/ppermute | solution.py:592
  224.1 8.8 %copy-start.17 = (f32[512,16]{0,1:T(8,128)S(1)}, f32[512,16]{0,1:T(8,128)}, u32[]{:S(2)}) copy-start(f32[512,16]{0,1:T(8,128)} %param.8) | copy-start | bytes 98308
  224.1 11.8 %collective-permute-start.19 = (bf16[3,256,1024]{2,1,0:T(8,128)(2,1)}, bf16[3,256,1024]{2,1,0:T(8,128)(2,1)}, u32[]{:S(2)}, u32[]{:S(2)}) collective-permute-start(bf16[3,256,1024]{2,1,0:T(8,128)(2,1)} %collective-permute-done.12.refs_5_.refs_6_), channel_id=1, source_target_pairs={{0,8},{8,0},{16,24},{24,16},{1,9},{9,1},{17,25},{25,17},{2,10},{10... | collective-permute-start | bytes 4718600 | tf_op jit(solution)/shard_map/ppermute | solution.py:27
  226.3 9.7 %collective-permute-start.21 = (bf16[3,256,1024]{2,1,0:T(8,128)(2,1)S(1)}, bf16[3,256,1024]{2,1,0:T(8,128)(2,1)}, u32[]{:S(2)}, u32[]{:S(2)}) collective-permute-start(bf16[3,256,1024]{2,1,0:T(8,128)(2,1)S(1)} %collective-permute-done.20.refs_7_.refs_14_), channel_id=1, source_target_pairs={{0,8},{8,0},{16,24},{24,16},{1,9},{9,1},{17,25},{25,17},{2,10},{10... | collective-permute-start | bytes 4718600 | tf_op jit(solution)/shard_map/ppermute | solution.py:27
  228.4 45.5 %collective-permute-start.23 = (bf16[256,2048]{1,0:T(8,128)(2,1)}, bf16[256,2048]{1,0:T(8,128)(2,1)}, u32[]{:S(2)}, u32[]{:S(2)}) collective-permute-start(bf16[256,2048]{1,0:T(8,128)(2,1)} %get-tuple-element.75), channel_id=1, source_target_pairs={{2,0},{4,6},{3,1},{5,7},{10,8},{12,14},{11,9},{13,15},{18,16},{20,... | collective-permute-start | bytes 3145736 | tf_op jit(solution)/shard_map/ppermute | solution.py:592
  230.6 52.7 %collective-permute-start.10 = (bf16[256,2048]{1,0:T(8,128)(2,1)}, bf16[256,2048]{1,0:T(8,128)(2,1)}, u32[]{:S(2)}, u32[]{:S(2)}) collective-permute-start(bf16[256,2048]{1,0:T(8,128)(2,1)} %get-tuple-element.76), channel_id=1, source_target_pairs={{2,0},{4,6},{3,1},{5,7},{10,8},{12,14},{11,9},{13,15},{18,16},{20,... | collective-permute-start | bytes 3145736 | tf_op jit(solution)/shard_map/ppermute | solution.py:592
  263.4 29.9 %collective-permute-start.28 = (bf16[2,256,512]{2,1,0:T(8,128)(2,1)}, bf16[2,256,512]{2,1,0:T(8,128)(2,1)S(1)}, u32[]{:S(2)}, u32[]{:S(2)}) collective-permute-start(bf16[2,256,512]{2,1,0:T(8,128)(2,1)} %get-tuple-element.58), channel_id=1, source_target_pairs={{0,1},{1,0},{2,3},{3,2},{4,5},{5,4},{6,7},{7,6},{8,9},{9,8},{10,11... | collective-permute-start | bytes 1572872 | tf_op jit(solution)/shard_map/ppermute | solution.py:27
  272.8 23.5 %collective-permute-start.26 = (bf16[2,256,512]{2,1,0:T(8,128)(2,1)}, bf16[2,256,512]{2,1,0:T(8,128)(2,1)S(1)}, u32[]{:S(2)}, u32[]{:S(2)}) collective-permute-start(bf16[2,256,512]{2,1,0:T(8,128)(2,1)} %get-tuple-element.55), channel_id=1, source_target_pairs={{0,1},{1,0},{2,3},{3,2},{4,5},{5,4},{6,7},{7,6},{8,9},{9,8},{10,11... | collective-permute-start | bytes 1572872 | tf_op jit(solution)/shard_map/ppermute | solution.py:27
  282.7 10.5 %copy-start.18 = (f32[512,16]{0,1:T(8,128)S(1)}, f32[512,16]{0,1:T(8,128)}, u32[]{:S(2)}) copy-start(f32[512,16]{0,1:T(8,128)} %param.9) | copy-start | bytes 98308
  282.7 10.5 %copy-start.19 = (f32[512]{0:T(512)S(1)}, f32[512]{0:T(512)}, u32[]{:S(2)}) copy-start(f32[512]{0:T(512)} %param.10) | copy-start | bytes 6148
  282.7 10.6 %copy-start = (bf16[3,256,512]{2,1,0:T(8,128)(2,1)S(1)}, bf16[3,256,512]{2,1,0:T(8,128)(2,1)}, u32[]{:S(2)}) copy-start(bf16[3,256,512]{2,1,0:T(8,128)(2,1)} %get-tuple-element.57.kept.refs_10_) | copy-start | bytes 2359300
  282.7 16.8 %collective-permute-start.24 = (bf16[2,256,512]{2,1,0:T(8,128)(2,1)}, bf16[2,256,512]{2,1,0:T(8,128)(2,1)S(1)}, u32[]{:S(2)}, u32[]{:S(2)}) collective-permute-start(bf16[2,256,512]{2,1,0:T(8,128)(2,1)} %get-tuple-element.53), channel_id=1, source_target_pairs={{0,1},{1,0},{2,3},{3,2},{4,5},{5,4},{6,7},{7,6},{8,9},{9,8},{10,11... | collective-permute-start | bytes 1572872 | tf_op jit(solution)/shard_map/ppermute | solution.py:27
  292.2 4.2 %copy-start.1 = (bf16[3,256,512]{2,1,0:T(8,128)(2,1)S(1)}, bf16[3,256,512]{2,1,0:T(8,128)(2,1)}, u32[]{:S(2)}) copy-start(bf16[3,256,512]{2,1,0:T(8,128)(2,1)} %get-tuple-element.54.kept.refs_11_) | copy-start | bytes 2359300
  292.2 18.4 %collective-permute-start.22 = (bf16[2,256,512]{2,1,0:T(8,128)(2,1)}, bf16[2,256,512]{2,1,0:T(8,128)(2,1)}, u32[]{:S(2)}, u32[]{:S(2)}) collective-permute-start(bf16[2,256,512]{2,1,0:T(8,128)(2,1)} %get-tuple-element.51), channel_id=1, source_target_pairs={{0,1},{1,0},{2,3},{3,2},{4,5},{5,4},{6,7},{7,6},{8,9},{9,8},{10,11... | collective-permute-start | bytes 1572872 | tf_op jit(solution)/shard_map/ppermute | solution.py:27
  293.3 6.2 %copy-start.2 = (bf16[3,256,512]{2,1,0:T(8,128)(2,1)S(1)}, bf16[3,256,512]{2,1,0:T(8,128)(2,1)}, u32[]{:S(2)}) copy-start(bf16[3,256,512]{2,1,0:T(8,128)(2,1)} %get-tuple-element.52.kept.refs_12_) | copy-start | bytes 2359300
  296.4 14.2 %copy-start.3 = (bf16[3,256,512]{2,1,0:T(8,128)(2,1)S(1)}, bf16[3,256,512]{2,1,0:T(8,128)(2,1)}, u32[]{:S(2)}) copy-start(bf16[3,256,512]{2,1,0:T(8,128)(2,1)} %get-tuple-element.50.kept.refs_13_) | copy-start | bytes 2359300
  299.5 21.8 %copy-start.4 = (f32[4,2,16,8,128]{4,3,2,1,0:T(8,128)S(1)}, f32[4,2,16,8,128]{4,3,2,1,0:T(8,128)}, u32[]{:S(2)}) copy-start(f32[4,2,16,8,128]{4,3,2,1,0:T(8,128)} %carry.1.refs_4_) | copy-start | bytes 1572868
  299.5 21.8 %copy-start.5 = (s32[3]{0:T(128)S(1)}, s32[3]{0:T(128)}, u32[]{:S(2)}) copy-start(s32[3]{0:T(128)} %pad_add_fusion.place) | copy-start | bytes 40
  314.7 3.1 collective-permute-start.29
  316.0 3.7 %collective-permute-start.30 = (f32[16,8,128]{2,1,0:T(8,128)S(1)}, f32[16,8,128]{2,1,0:T(8,128)S(1)}, u32[]{:S(2)}, u32[]{:S(2)}) collective-permute-start(f32[16,8,128]{2,1,0:T(8,128)S(1)} %get-tuple-element.62.refs_0_), channel_id=1, source_target_pairs={{0,16},{8,24},{16,0},{24,8},{1,17},{9,25},{17,1},{25,9},{2,18},{10... | collective-permute-start | bytes 196616 | tf_op jit(solution)/shard_map/ppermute | solution.py:27
  317.2 4.0 %collective-permute-start.31 = (f32[16,8,128]{2,1,0:T(8,128)S(1)}, f32[16,8,128]{2,1,0:T(8,128)S(1)}, u32[]{:S(2)}, u32[]{:S(2)}) collective-permute-start(f32[16,8,128]{2,1,0:T(8,128)S(1)} %get-tuple-element.62.refs_0_), channel_id=1, source_target_pairs={{0,24},{8,16},{16,8},{24,0},{1,25},{9,17},{17,9},{25,1},{2,26},{10... | collective-permute-start | bytes 196616 | tf_op jit(solution)/shard_map/ppermute | solution.py:27
  (4 other events, 5.5 us)
where the time goes:
time: 333 us; the launch traced here: 332 us
  waiting for transfers between devices  135 us (41%)
  Pallas kernels  127 us (38%)
  starting transfers between devices  49.4 us (15%)
  local copies, waits for them, and re-layouts  18.3 us (5%)
    ppermute x23, waiting for transfers between devices, exchanged(): return lax.ppermute(block, axis, [(i, i ^ mask) for i in range(count)])  120 us
    pallas_call x7, Pallas kernels, project(): pl.pallas_call(functools.partial(project_kernel, plan, len(inputs), len(p...  101 us
    ppermute x23, starting transfers between devices, exchanged(): return lax.ppermute(block, axis, [(i, i ^ mask) for i in range(count)])  27.5 us
    pallas_call x4, Pallas kernels, scan(): pl.pallas_call(scan_kernel, in_specs=[local] * 6, out_specs=[local] * 2,...  13.3 us
    pallas_call x1, Pallas kernels, finish(): pl.pallas_call(functools.partial(finish_kernel, len(ends), n_chunks, seg_...  10.7 us
    ppermute x4, starting transfers between devices, per_device(): last = lax.ppermute(block, 'tp', [(1, 0), (2, 3)])  9.09 us
    ppermute x1, waiting for transfers between devices, per_device(): far_middle = [lax.ppermute(block, 'tp', [(1, 2), (2, 1)])]  8.42 us
  transfers between devices with their start and end apart: 32, of which 13 were waited for; matrix products, arithmetic and copies ran while one was open for 5% of the time, Pallas kernels for 34%

commit v1 on v0

--- a/solution.py
+++ b/solution.py
@@ -50,7 +50,7 @@
         choose(middle, high, number, act)
 
 
-def fetch_weights(plan, place, p, block, own, pieces, first, target, sem):
+def fetch_weights(plan, place, p, block, own, pieces, first, lanes, target, sem):
     pair, ctx = place[0], place[1]
     local = lax.rem(block, plan.half_blocks)
     here = lax.div(block, plan.half_blocks) == pair
@@ -58,7 +58,7 @@
     @pl.when(here)
     def _():
         row = pl.multiple_of(local * DEPTH, DEPTH)
-        pltpu.make_async_copy(own.at[p, pl.ds(row, DEPTH), :], target, sem).start()
+        pltpu.make_async_copy(own.at[p, pl.ds(row, DEPTH), lanes], target, sem).start()
 
     @pl.when(jnp.logical_not(here))
     def _():
@@ -67,18 +67,19 @@
         number = number + lax.rem(local, plan.part_blocks) - first
 
         def act(n):
-            pltpu.make_async_copy(pieces[n].at[p], target, sem).start()
+            pltpu.make_async_copy(pieces[n].at[p, :, lanes], target, sem).start()
 
         choose(0, len(pieces), number, act)
 
 
-def project_kernel(plan, n_inputs, n_pieces, first, base, final, blocks, x_plan, place, *refs):
+def project_kernel(plan, n_inputs, n_pieces, first, base, sides, blocks, x_plan, place, *refs):
     refs = list(refs)
     inputs = [refs.pop(0) for _ in range(n_inputs)]
     own = refs.pop(0)
     pieces = [refs.pop(0) for _ in range(n_pieces)]
     init = refs.pop(0) if base is not None else None
-    outs = [refs.pop(0) for _ in range(2 if final else 1)]
+    final = len(sides) > 0
+    outs = [refs.pop(0) for _ in range(max(1, len(sides)))]
     x_buf, w_buf, x_sem, w_sem = refs[:4]
     refs = refs[4:]
     if final:
@@ -88,12 +89,16 @@
         i_buf = o_buf
     pair, tp = place[0], place[2]
     rows, depth = x_buf.shape
+    width = w_buf.shape[2]
+    taken = pl.ds(0, width)
+    if len(sides) == 1:
+        taken = pl.ds(pl.multiple_of((pair if sides[0] == 0 else 1 - pair) * width, 128), width)
     spans = (slice(0, depth // 2), slice(depth // 2, depth))
 
     def fetch(p):
         if init is not None:
             pltpu.make_async_copy(
-                init.at[p, pl.ds(base, rows), :], i_buf.at[p], i_sem.at[p]
+                init.at[p, pl.ds(base, rows), taken], i_buf.at[p], i_sem.at[p]
             ).start()
         for part in (0, 1):
 
@@ -102,7 +107,7 @@
                 block = x_plan(tp, step, inputs, x_buf.at[:, where], x_sem.at[part], p == 0)
                 target = w_buf.at[p, where, :]
                 fetch_weights(
-                    plan, place, p, block, own, pieces, first, target, w_sem.at[p, part]
+                    plan, place, p, block, own, pieces, first, taken, target, w_sem.at[p, part]
                 )
                 return carry
 
@@ -146,9 +151,10 @@
                 lax.fori_loop(0, rows // chunk, functools.partial(multiply, whole, False), 0)
             pltpu.make_async_copy(o_buf.at[p], outs[0].at[p], o_sem.at[p]).start()
             continue
-        kept, given = outs
-        half = kept.shape[2]
+        half = outs[0].shape[2]
         lanes = [pl.ds(pl.multiple_of(x * half, 128), half) for x in (pair, 1 - pair)]
+        if len(sides) == 1:
+            lanes = [pl.ds(0, half)]
 
         def product(span, n):
             return jnp.dot(
@@ -156,36 +162,42 @@
             )
 
         if p == 0:
-            early = [product(spans[0], n) for n in (0, 1)]
+            early = [product(spans[0], n) for n in range(len(sides))]
             await_part(0, 1)
             fetch(2)
-            sums = [early[n] + product(spans[1], n) for n in (0, 1)]
+            sums = [early[n] + product(spans[1], n) for n in range(len(sides))]
         else:
-            sums = [product(slice(0, depth), n) for n in (0, 1)]
-        for n in (0, 1):
-            new = sums[n]
+            sums = [product(slice(0, depth), n) for n in range(len(sides))]
+        for n, side in enumerate(sides):
+            new, out = sums[n], outs[n]
             if init is not None:
                 new = i_buf[p, :, lanes[n]] + new
             new = new.astype(jnp.bfloat16)
-            if n == 0 or p == 0:
-                outs[n][p] = new
+            if side == 0 or p == 0:
+                out[p] = new
             elif p == 1:
-                given[1] = new
+                out[1] = new
             else:
-                both = given[1].astype(jnp.float32) * new.astype(jnp.float32)
-                given[1] = both.astype(jnp.bfloat16)
+                both = out[1].astype(jnp.float32) * new.astype(jnp.float32)
+                out[1] = both.astype(jnp.bfloat16)
     if not final:
         for p in range(3):
             pltpu.make_async_copy(o_buf.at[p], outs[0].at[p], o_sem.at[p]).wait()
 
 
-def project(plan, place, inputs, own, pieces, first, init, base, rows, blocks, x_plan, name):
+def project(
+    plan, place, inputs, own, pieces, first, init, base, rows, blocks, x_plan, name, sides=(0, 1)
+):
     final = name == "project"
+    sides = sides if final else ()
     width = own.shape[2]
     anywhere = pl.BlockSpec(memory_space=pl.ANY)
     local = pl.BlockSpec(memory_space=pltpu.VMEM)
     operands = list(inputs) + [own] + list(pieces) + ([] if init is None else [init])
     depth = blocks * DEPTH
+    half = width // 2
+    if len(sides) == 1:
+        width = half
     total = (3, rows, width)
     scratch = [
         pltpu.VMEM((rows, depth), jnp.bfloat16),
@@ -197,7 +209,7 @@
         if init is not None:
             scratch += [pltpu.VMEM(total, jnp.float32), pltpu.SemaphoreType.DMA((3,))]
         out_shape = [
-            jax.ShapeDtypeStruct((n, rows, width // 2), jnp.bfloat16) for n in (3, 2)
+            jax.ShapeDtypeStruct((3 - side, rows, half), jnp.bfloat16) for side in sides
         ]
     else:
         scratch += [pltpu.VMEM(total, jnp.float32)] + [pltpu.SemaphoreType.DMA((3,))] * 2
@@ -205,13 +217,13 @@
     return pl.pallas_call(
         functools.partial(
             project_kernel, plan, len(inputs), len(pieces), first,
-            None if init is None else base, final, blocks, x_plan,
+            None if init is None else base, sides, blocks, x_plan,
         ),
         grid_spec=pltpu.PrefetchScalarGridSpec(
             num_scalar_prefetch=1,
             grid=(),
             in_specs=[anywhere] * len(operands),
-            out_specs=[local, local] if final else anywhere,
+            out_specs=[local] * len(sides) if final else anywhere,
             scratch_shapes=scratch,
         ),
         out_shape=out_shape,
@@ -437,7 +449,7 @@
                 lanes = slice(g * 128, (g + 1) * 128)
                 query = ref[0, :, lanes].astype(jnp.float32)
                 gated = query * conv[:rows, side * groups + g, :]
-                out[lanes, pl.ds(column, rows)] = gated.astype(jnp.bfloat16).T
+                out[lanes, pl.ds(column, rows)] = gated.T.astype(jnp.bfloat16)
         base += rows
 
 
@@ -594,10 +606,18 @@
                 last = after(last, weights)
             if k in T["S"]:
                 last = after(last, states[T["S"][k]])
-            keep, give = project(
-                plan, place, [far_middle[n], last], own, ordered, 0, most, base, rows,
-                per_quarter, last_plan(per_quarter, row, rows), "project",
-            )
+
+            def last_part(x, sides):
+                return project(
+                    plan, place, [far_middle[n], x], own, ordered, 0, most, base, rows,
+                    per_quarter, last_plan(per_quarter, row, rows), "project", sides,
+                )
+
+            if k < len(CHUNKS) - 1:
+                keep, give = last_part(last, (0, 1))
+            else:
+                (give,) = last_part(last, (1,))
+                (keep,) = last_part(after(last, give), (0,))
         else:
             block = lax.slice_in_dim(tokens, base, base + rows, axis=0)
             whole = lax.all_gather(block, "tp", axis=0, tiled=False)

time: 333 us -> 330 us (level)
  waiting for transfers between devices: 135 us -> 131 us
    pallas_call x7 -> x8, Pallas kernels: 101 us -> 105 us  [project(): pl.pallas_call(functools.partial(project_kernel, plan, len(inputs), len(p...]
    ppermute x23, waiting for transfers between devices: 120 us -> 116 us  [exchanged(): return lax.ppermute(block, axis, [(i, i ^ mask) for i in range(count)])]
  transfers between devices with their start and end apart: 32 -> 32, of which waited for: 13 -> 13; matrix products, arithmetic and copies ran while one was open for 5% -> 5% of each run, Pallas kernels for 34% -> 35%
where the time goes in v1:
time: 330 us; the launch traced here: 329 us
  waiting for transfers between devices  131 us (40%)
  Pallas kernels  129 us (39%)
  starting transfers between devices  48.4 us (15%)
  local copies, waits for them, and re-layouts  18.3 us (6%)
    ppermute x23, waiting for transfers between devices, exchanged(): return lax.ppermute(block, axis, [(i, i ^ mask) for i in range(count)])  116 us
    pallas_call x8, Pallas kernels, project(): pl.pallas_call(functools.partial(project_kernel, plan, len(inputs), len(p...  105 us
    ppermute x23, starting transfers between devices, exchanged(): return lax.ppermute(block, axis, [(i, i ^ mask) for i in range(count)])  27.4 us
    pallas_call x4, Pallas kernels, scan(): pl.pallas_call(scan_kernel, in_specs=[local] * 6, out_specs=[local] * 2,...  12.2 us
    pallas_call x1, Pallas kernels, finish(): pl.pallas_call(functools.partial(finish_kernel, len(ends), n_chunks, seg_...  9.71 us
    ppermute x1, waiting for transfers between devices, per_device(): far_middle = [lax.ppermute(block, 'tp', [(1, 2), (2, 1)])]  8.42 us
    ppermute x4, starting transfers between devices, per_device(): last = lax.ppermute(block, 'tp', [(1, 0), (2, 3)])  8.18 us
  transfers between devices with their start and end apart: 32, of which 13 were waited for; matrix products, arithmetic and copies ran while one was open for 5% of the time, Pallas kernels for 35%

profile of v1, /device:TPU:9, one launch (start us, length us, event | category | flops | bytes accessed | tf_op | source)
XLA Modules:
  0.0 329.0 jit_solution(4792379892573096398)
XLA Ops:
  0.0 4.5 %collective-permute-start.14 = (bf16[1024,2048]{1,0:T(8,128)(2,1)}, bf16[1024,2048]{1,0:T(8,128)(2,1)}, u32[]{:S(2)}, u32[]{:S(2)}) collective-permute-start(bf16[1024,2048]{1,0:T(8,128)(2,1)} %refs_0_.5), channel_id=1, source_target_pairs={{2,4},{4,2},{3,5},{5,3},{10,12},{12,10},{11,13},{13,11},{18,20},{2... | collective-permute-start | bytes 12582920 | tf_op jit(solution)/shard_map/ppermute | solution.py:496
  4.5 4.8 %dynamic-slice_bitcast_fusion = (bf16[3,256,1024]{2,1,0:T(8,128)(2,1)}, bf16[3,256,1024]{2,1,0:T(8,128)(2,1)S(1)}, bf16[3,256,1024]{2,1,0:T(8,128)(2,1)S(1)}, bf16[3,256,1024]{2,1,0:T(8,128)(2,1)S(1)}) fusion(bf16[4096,3,1024]{2,0,1:T(8,128)(2,1)} %param.7, s32[]{:T(128)S(6)} %select_n.15, s32[]{:T(128)S(6)} %select_n.13, s32[]{:T(128)S(6)} %select_n.12, ...), kind=kLoop, calls=%fused_computation | loop fusion | bytes 12582928 | tf_op jit(solution)/shard_map/dynamic_slice | solution.py:527
  9.3 1.2 collective-permute-start.1
  10.7 33.3 %collective-permute-done.1.refs_3_.refs_5_ = bf16[3,256,1024]{2,1,0:T(8,128)(2,1)S(1)} collective-permute-done((bf16[3,256,1024]{2,1,0:T(8,128)(2,1)S(1)}, bf16[3,256,1024]{2,1,0:T(8,128)(2,1)S(1)}, u32[]{:S(2)}, u32[]{:S(2)}) %collective-permute-start.1) | collective-permute-done | bytes 1572896 | tf_op jit(solution)/shard_map/ppermute | solution.py:27
  44.0 3.8 %collective-permute-start.3 = (bf16[3,256,1024]{2,1,0:T(8,128)(2,1)S(1)}, bf16[3,256,1024]{2,1,0:T(8,128)(2,1)S(1)}, u32[]{:S(2)}, u32[]{:S(2)}) collective-permute-start(bf16[3,256,1024]{2,1,0:T(8,128)(2,1)S(1)} %collective-permute-done.1.refs_3_.refs_5_), channel_id=1, source_target_pairs={{0,8},{8,0},{16,24},{24,16},{1,9},{9,1},{17,25},{25,17},{2,10},{10... | collective-permute-start | bytes 4718600 | tf_op jit(solution)/shard_map/ppermute | solution.py:27
  47.8 1.2 collective-permute-start.5
  49.1 28.7 %collective-permute-done.2.refs_4_.refs_6_ = bf16[3,256,1024]{2,1,0:T(8,128)(2,1)S(1)} collective-permute-done((bf16[3,256,1024]{2,1,0:T(8,128)(2,1)S(1)}, bf16[3,256,1024]{2,1,0:T(8,128)(2,1)S(1)}, u32[]{:S(2)}, u32[]{:S(2)}) %collective-permute-start.2) | collective-permute-done | bytes 1572896 | tf_op jit(solution)/shard_map/ppermute | solution.py:27
  79.0 5.0 %collective-permute-done.5.refs_7_.refs_11_ = bf16[3,256,1024]{2,1,0:T(8,128)(2,1)S(1)} collective-permute-done((bf16[3,256,1024]{2,1,0:T(8,128)(2,1)S(1)}, bf16[3,256,1024]{2,1,0:T(8,128)(2,1)S(1)}, u32[]{:S(2)}, u32[]{:S(2)}) %collective-permute-start.5) | collective-permute-done | bytes 1572896 | tf_op jit(solution)/shard_map/ppermute | solution.py:27
  85.0 1.2 collective-permute-start.11
  86.3 5.5 %collective-permute-done.refs_1_ = bf16[1024,2048]{1,0:T(8,128)(2,1)} collective-permute-done((bf16[1024,2048]{1,0:T(8,128)(2,1)}, bf16[1024,2048]{1,0:T(8,128)(2,1)}, u32[]{:S(2)}, u32[]{:S(2)}) %collective-permute-start) | collective-permute-done | bytes 4194336 | tf_op jit(solution)/shard_map/ppermute | solution.py:495
  91.8 1.5 collective-permute-start.4
  93.3 1.5 collective-permute-done.14.refs_2_
  94.8 3.4 %collective-permute-start.15 = (bf16[1024,2048]{1,0:T(8,128)(2,1)}, bf16[1024,2048]{1,0:T(8,128)(2,1)}, u32[]{:S(2)}, u32[]{:S(2)}) collective-permute-start(bf16[1024,2048]{1,0:T(8,128)(2,1)} %collective-permute-done.14.refs_2_), channel_id=1, source_target_pairs={{2,0},{4,6},{3,1},{5,7},{10,8},{12,14},{11,9},{13,15},{18,16},{20,... | collective-permute-start | bytes 12582920 | tf_op jit(solution)/shard_map/ppermute | solution.py:497
  98.1 4.8 %fusion = (bf16[512,2048]{1,0:T(8,128)(2,1)}, bf16[512,2048]{1,0:T(8,128)(2,1)}) fusion(bf16[1024,2048]{1,0:T(8,128)(2,1)} %collective-permute-done.refs_1_), kind=kLoop, calls=%fused_computation.10 | loop fusion | bytes 8388608 | tf_op jit(solution)/shard_map/slice | solution.py:498
  103.0 14.7 %collective-permute-done.6.refs_8_.refs_12_ = bf16[3,256,1024]{2,1,0:T(8,128)(2,1)} collective-permute-done((bf16[3,256,1024]{2,1,0:T(8,128)(2,1)S(1)}, bf16[3,256,1024]{2,1,0:T(8,128)(2,1)}, u32[]{:S(2)}, u32[]{:S(2)}) %collective-permute-start.6) | collective-permute-done | bytes 1572896 | tf_op jit(solution)/shard_map/ppermute | solution.py:27
  117.7 1.9 collective-permute-start.18
  121.2 1.2 collective-permute-start.12
  126.5 20.9 %part_a.1.refs_17_ = f32[3,1024,1024]{2,1,0:T(8,128)} custom-call(s32[3]{0:T(128)} %pad_add_fusion.place, bf16[1024,2048]{1,0:T(8,128)(2,1)} %refs_0_.5, bf16[1024,2048]{1,0:T(8,128)(2,1)} %collective-permute-done.refs_1_, bf16[3,4096,1024]{2,1,0:T(8,128)(2,1)} %bitcast.18, bf16[3,256,1024]{2,1,0:T(8,128)(2,1)} %copy-done.6, ...), custom_call_target="tpu_custom_call" | custom-call | tf_op jit(solution)/shard_map/part_a/pallas_call | solution.py:217
  147.5 3.1 collective-permute-start.9
  150.6 6.0 %collective-permute-done.12.refs_5_.refs_6_ = bf16[3,256,1024]{2,1,0:T(8,128)(2,1)} collective-permute-done((bf16[3,256,1024]{2,1,0:T(8,128)(2,1)}, bf16[3,256,1024]{2,1,0:T(8,128)(2,1)}, u32[]{:S(2)}, u32[]{:S(2)}) %collective-permute-start.12) | collective-permute-done | bytes 1572896 | tf_op jit(solution)/shard_map/ppermute | solution.py:27
  157.8 8.4 %collective-permute-done.18.refs_0_ = bf16[512,2048]{1,0:T(8,128)(2,1)} collective-permute-done((bf16[512,2048]{1,0:T(8,128)(2,1)}, bf16[512,2048]{1,0:T(8,128)(2,1)}, u32[]{:S(2)}, u32[]{:S(2)}) %collective-permute-start.18) | collective-permute-done | bytes 2097184 | tf_op jit(solution)/shard_map/ppermute | solution.py:499
  166.3 2.9 collective-permute-start.13
  169.2 3.1 fusion.1
  172.3 20.0 %collective-permute-done.20.refs_7_.refs_14_ = bf16[3,256,1024]{2,1,0:T(8,128)(2,1)S(1)} collective-permute-done((bf16[3,256,1024]{2,1,0:T(8,128)(2,1)}, bf16[3,256,1024]{2,1,0:T(8,128)(2,1)S(1)}, u32[]{:S(2)}, u32[]{:S(2)}) %collective-permute-start.20) | collective-permute-done | bytes 1572896 | tf_op jit(solution)/shard_map/ppermute | solution.py:27
  192.4 1.3 collective-permute-start.27
  193.7 2.3 collective-permute-start.25
  197.2 26.0 %part_b.1.refs_9_ = f32[3,1024,1024]{2,1,0:T(8,128)} custom-call(s32[3]{0:T(128)} %pad_add_fusion.place, bf16[1024,2048]{1,0:T(8,128)(2,1)} %refs_0_.5, bf16[1024,2048]{1,0:T(8,128)(2,1)} %collective-permute-done.refs_1_, bf16[1024,2048]{1,0:T(8,128)(2,1)} %collective-permute-done.14.refs_2_, bf16[1024,2048]{1,0:T(8,128)(2,1)} %collective-permute-done.15.refs_3_, ...), custom_call_target="tpu_custom_call" | custom-call | tf_op jit(solution)/shard_map/part_b/pallas_call | solution.py:217
  223.3 2.1 collective-permute-start.19
  225.5 1.8 fusion.2
  227.5 2.3 collective-permute-start.23
  229.8 2.3 collective-permute-start.10
  232.7 2.4 carry.1.refs_4_
  235.1 18.6 %part_c.1.refs_19_ = f32[3,1024,1024]{2,1,0:T(8,128)} custom-call(s32[3]{0:T(128)} %pad_add_fusion.place, bf16[1024,2048]{1,0:T(8,128)(2,1)} %refs_0_.5, bf16[1024,2048]{1,0:T(8,128)(2,1)} %collective-permute-done.refs_1_, bf16[1024,2048]{1,0:T(8,128)(2,1)} %collective-permute-done.14.refs_2_, bf16[1024,2048]{1,0:T(8,128)(2,1)} %collective-permute-done.15.refs_3_, ...), custom_call_target="tpu_custom_call" | custom-call | tf_op jit(solution)/shard_map/part_c/pallas_call | solution.py:217
  253.7 8.8 %project.9 = (bf16[3,256,512]{2,1,0:T(8,128)(2,1)}, bf16[2,256,512]{2,1,0:T(8,128)(2,1)}) custom-call(s32[3]{0:T(128)} %pad_add_fusion.place, bf16[512,2048]{1,0:T(8,128)(2,1)} %collective-permute-done.18.refs_0_, bf16[256,2048]{1,0:T(8,128)(2,1)} %copy-done.17, bf16[3,4096,1024]{2,1,0:T(8,128)(2,1)} %bitcast.21, bf16[3,256,1024]{2,1,0:T(8,128)(2,1)} %copy-done.6, ...), custom_call_target="tpu_custom_call" | custom-call | tf_op jit(solution)/shard_map/project/pallas_call | solution.py:217
  263.2 8.8 %project.8 = (bf16[3,256,512]{2,1,0:T(8,128)(2,1)}, bf16[2,256,512]{2,1,0:T(8,128)(2,1)}) custom-call(s32[3]{0:T(128)} %pad_add_fusion.place, bf16[512,2048]{1,0:T(8,128)(2,1)} %collective-permute-done.18.refs_0_, bf16[256,2048]{1,0:T(8,128)(2,1)} %collective-permute-done.25.refs_1_, bf16[3,4096,1024]{2,1,0:T(8,128)(2,1)} %bitcast.22, ...), custom_call_target="tpu_custom_call" | custom-call | tf_op jit(solution)/shard_map/project/pallas_call | solution.py:217
  273.0 8.8 %project.7 = (bf16[3,256,512]{2,1,0:T(8,128)(2,1)}, bf16[2,256,512]{2,1,0:T(8,128)(2,1)}) custom-call(s32[3]{0:T(128)} %pad_add_fusion.place, bf16[512,2048]{1,0:T(8,128)(2,1)} %copy-done.16, bf16[256,2048]{1,0:T(8,128)(2,1)} %collective-permute-done.23.refs_1_, bf16[3,4096,1024]{2,1,0:T(8,128)(2,1)} %bitcast.23, bf16[3,256,1024]{2,1,0:T(8,128)(2,1)} %copy-done.6, ...), custom_call_target="tpu_custom_call" | custom-call | tf_op jit(solution)/shard_map/project/pallas_call | solution.py:217
  282.5 6.2 %project.5 = bf16[2,256,512]{2,1,0:T(8,128)(2,1)} custom-call(s32[3]{0:T(128)} %pad_add_fusion.place, bf16[512,2048]{1,0:T(8,128)(2,1)} %copy-done.16, bf16[256,2048]{1,0:T(8,128)(2,1)} %collective-permute-done.10.refs_1_, bf16[3,4096,1024]{2,1,0:T(8,128)(2,1)} %bitcast.24, bf16[3,256,1024]{2,1,0:T(8,128)(2,1)} %copy-done.6, ...), custom_call_target="tpu_custom_call" | custom-call | tf_op jit(solution)/shard_map/project/pallas_call | solution.py:217
  289.7 6.5 %project.6.kept.refs_13_ = bf16[3,256,512]{2,1,0:T(8,128)(2,1)} custom-call(s32[3]{0:T(128)} %pad_add_fusion.place, bf16[512,2048]{1,0:T(8,128)(2,1)} %copy-done.16, bf16[256,2048]{1,0:T(8,128)(2,1)} %collective-permute-done.10.refs_1_, bf16[3,4096,1024]{2,1,0:T(8,128)(2,1)} %bitcast.25, bf16[3,256,1024]{2,1,0:T(8,128)(2,1)} %copy-done.6, ...), custom_call_target="tpu_custom_call" | custom-call | tf_op jit(solution)/shard_map/project/pallas_call | solution.py:217
  296.3 3.1 scan.4
  299.4 3.1 scan.5
  302.5 3.1 scan.6
  305.5 4.1 %collective-permute-done.22.given.refs_17_ = bf16[2,256,512]{2,1,0:T(8,128)(2,1)S(1)} collective-permute-done((bf16[2,256,512]{2,1,0:T(8,128)(2,1)}, bf16[2,256,512]{2,1,0:T(8,128)(2,1)S(1)}, u32[]{:S(2)}, u32[]{:S(2)}) %collective-permute-start.22) | collective-permute-done | bytes 524320 | tf_op jit(solution)/shard_map/ppermute | solution.py:27
  309.6 3.1 scan.7
  312.7 1.3 collective-permute-start.29
  314.0 1.2 collective-permute-start.30
  315.7 2.0 collective-permute-done.30.refs_2_
  317.7 1.6 collective-permute-done.31.refs_3_
  319.3 9.7 %finish.1 = bf16[512,2048]{1,0:T(8,128)(2,1)} custom-call(s32[3]{0:T(128)S(1)} %copy-done.5, f32[16,8,128]{2,1,0:T(8,128)S(1)} %get-tuple-element.60.refs_0_, f32[16,8,128]{2,1,0:T(8,128)S(1)} %collective-permute-done.29.refs_1_, f32[16,8,128]{2,1,0:T(8,128)S(1)} %collective-permute-done.30.refs_2_, f32[16,8,128]{2,1,0:T(8,128)S(1)} %collective-permute-done.31.refs_3_, ...), custom_call_target="tpu_custom_call" | custom-call | flops 33554432 | bytes 8388608 | tf_op jit(solution)/shard_map/finish/pallas_call | solution.py:463
  (84 shorter events, 15.3 us)
Async XLA Ops:
  0.0 91.8 %collective-permute-start = (bf16[1024,2048]{1,0:T(8,128)(2,1)}, bf16[1024,2048]{1,0:T(8,128)(2,1)}, u32[]{:S(2)}, u32[]{:S(2)}) collective-permute-start(bf16[1024,2048]{1,0:T(8,128)(2,1)} %refs_0_.5), channel_id=1, source_target_pairs={{0,2},{2,0},{4,6},{6,4},{1,3},{3,1},{5,7},{7,5},{8,10},{10,8},{12,... | collective-permute-start | bytes 12582920 | tf_op jit(solution)/shard_map/ppermute | solution.py:495
  0.0 94.8 %collective-permute-start.14 = (bf16[1024,2048]{1,0:T(8,128)(2,1)}, bf16[1024,2048]{1,0:T(8,128)(2,1)}, u32[]{:S(2)}, u32[]{:S(2)}) collective-permute-start(bf16[1024,2048]{1,0:T(8,128)(2,1)} %refs_0_.5), channel_id=1, source_target_pairs={{2,4},{4,2},{3,5},{5,3},{10,12},{12,10},{11,13},{13,11},{18,20},{2... | collective-permute-start | bytes 12582920 | tf_op jit(solution)/shard_map/ppermute | solution.py:496
  9.3 34.8 %collective-permute-start.1 = (bf16[3,256,1024]{2,1,0:T(8,128)(2,1)S(1)}, bf16[3,256,1024]{2,1,0:T(8,128)(2,1)S(1)}, u32[]{:S(2)}, u32[]{:S(2)}) collective-permute-start(bf16[3,256,1024]{2,1,0:T(8,128)(2,1)S(1)} %get-tuple-element.67), channel_id=1, source_target_pairs={{0,1},{1,0},{2,3},{3,2},{4,5},{5,4},{6,7},{7,6},{8,9},{9,8},{10,11... | collective-permute-start | bytes 4718600 | tf_op jit(solution)/shard_map/ppermute | solution.py:27
  10.5 67.2 %collective-permute-start.2 = (bf16[3,256,1024]{2,1,0:T(8,128)(2,1)S(1)}, bf16[3,256,1024]{2,1,0:T(8,128)(2,1)S(1)}, u32[]{:S(2)}, u32[]{:S(2)}) collective-permute-start(bf16[3,256,1024]{2,1,0:T(8,128)(2,1)S(1)} %get-tuple-element.66), channel_id=1, source_target_pairs={{0,1},{1,0},{2,3},{3,2},{4,5},{5,4},{6,7},{7,6},{8,9},{9,8},{10,11... | collective-permute-start | bytes 4718600 | tf_op jit(solution)/shard_map/ppermute | solution.py:27
  44.0 59.0 %copy-start.6 = (bf16[3,256,1024]{2,1,0:T(8,128)(2,1)}, bf16[3,256,1024]{2,1,0:T(8,128)(2,1)S(1)}, u32[]{:S(2)}) copy-start(bf16[3,256,1024]{2,1,0:T(8,128)(2,1)S(1)} %collective-permute-done.1.refs_3_.refs_5_) | copy-start | bytes 4718596
  44.0 34.9 %collective-permute-start.3 = (bf16[3,256,1024]{2,1,0:T(8,128)(2,1)S(1)}, bf16[3,256,1024]{2,1,0:T(8,128)(2,1)S(1)}, u32[]{:S(2)}, u32[]{:S(2)}) collective-permute-start(bf16[3,256,1024]{2,1,0:T(8,128)(2,1)S(1)} %collective-permute-done.1.refs_3_.refs_5_), channel_id=1, source_target_pairs={{0,8},{8,0},{16,24},{24,16},{1,9},{9,1},{17,25},{25,17},{2,10},{10... | collective-permute-start | bytes 4718600 | tf_op jit(solution)/shard_map/ppermute | solution.py:27
  47.8 36.1 %collective-permute-start.5 = (bf16[3,256,1024]{2,1,0:T(8,128)(2,1)S(1)}, bf16[3,256,1024]{2,1,0:T(8,128)(2,1)S(1)}, u32[]{:S(2)}, u32[]{:S(2)}) collective-permute-start(bf16[3,256,1024]{2,1,0:T(8,128)(2,1)S(1)} %collective-permute-done.1.refs_3_.refs_5_), channel_id=1, source_target_pairs={{0,16},{8,24},{16,0},{24,8},{1,17},{9,25},{17,1},{25,9},{2,18},{10... | collective-permute-start | bytes 4718600 | tf_op jit(solution)/shard_map/ppermute | solution.py:27
  77.7 25.3 %copy-start.7 = (bf16[3,256,1024]{2,1,0:T(8,128)(2,1)}, bf16[3,256,1024]{2,1,0:T(8,128)(2,1)S(1)}, u32[]{:S(2)}) copy-start(bf16[3,256,1024]{2,1,0:T(8,128)(2,1)S(1)} %collective-permute-done.2.refs_4_.refs_6_) | copy-start | bytes 4718596
  77.7 39.9 %collective-permute-start.6 = (bf16[3,256,1024]{2,1,0:T(8,128)(2,1)S(1)}, bf16[3,256,1024]{2,1,0:T(8,128)(2,1)}, u32[]{:S(2)}, u32[]{:S(2)}) collective-permute-start(bf16[3,256,1024]{2,1,0:T(8,128)(2,1)S(1)} %collective-permute-done.2.refs_4_.refs_6_), channel_id=1, source_target_pairs={{0,16},{8,24},{16,0},{24,8},{1,17},{9,25},{17,1},{25,9},{2,18},{10... | collective-permute-start | bytes 4718600 | tf_op jit(solution)/shard_map/ppermute | solution.py:27
  78.9 7.3 %copy-start.8 = (bf16[3,256,1024]{2,1,0:T(8,128)(2,1)}, bf16[3,256,1024]{2,1,0:T(8,128)(2,1)S(1)}, u32[]{:S(2)}) copy-start(bf16[3,256,1024]{2,1,0:T(8,128)(2,1)S(1)} %collective-permute-done.3.refs_5_.refs_8_.refs_7_) | copy-start | bytes 4718596
  84.0 19.0 %copy-start.9 = (bf16[3,256,1024]{2,1,0:T(8,128)(2,1)}, bf16[3,256,1024]{2,1,0:T(8,128)(2,1)S(1)}, u32[]{:S(2)}) copy-start(bf16[3,256,1024]{2,1,0:T(8,128)(2,1)S(1)} %collective-permute-done.5.refs_7_.refs_11_) | copy-start | bytes 4718596
  84.0 35.6 %collective-permute-start.7 = (bf16[3,256,1024]{2,1,0:T(8,128)(2,1)S(1)}, bf16[3,256,1024]{2,1,0:T(8,128)(2,1)S(1)}, u32[]{:S(2)}, u32[]{:S(2)}) collective-permute-start(bf16[3,256,1024]{2,1,0:T(8,128)(2,1)S(1)} %collective-permute-done.5.refs_7_.refs_11_), channel_id=1, source_target_pairs={{0,8},{8,0},{16,24},{24,16},{1,9},{9,1},{17,25},{25,17},{2,10},{10... | collective-permute-start | bytes 4718600 | tf_op jit(solution)/shard_map/ppermute | solution.py:27
  85.0 36.1 %collective-permute-start.11 = (bf16[3,256,1024]{2,1,0:T(8,128)(2,1)S(1)}, bf16[3,256,1024]{2,1,0:T(8,128)(2,1)}, u32[]{:S(2)}, u32[]{:S(2)}) collective-permute-start(bf16[3,256,1024]{2,1,0:T(8,128)(2,1)S(1)} %get-tuple-element.37), channel_id=1, source_target_pairs={{0,1},{1,0},{2,3},{3,2},{4,5},{5,4},{6,7},{7,6},{8,9},{9,8},{10,11... | collective-permute-start | bytes 4718600 | tf_op jit(solution)/shard_map/ppermute | solution.py:27
  91.8 30.7 %collective-permute-start.4 = (bf16[3,256,1024]{2,1,0:T(8,128)(2,1)S(1)}, bf16[3,256,1024]{2,1,0:T(8,128)(2,1)S(1)}, u32[]{:S(2)}, u32[]{:S(2)}) collective-permute-start(bf16[3,256,1024]{2,1,0:T(8,128)(2,1)S(1)} %collective-permute-done.2.refs_4_.refs_6_), channel_id=1, source_target_pairs={{0,8},{8,0},{16,24},{24,16},{1,9},{9,1},{17,25},{25,17},{2,10},{10... | collective-permute-start | bytes 4718600 | tf_op jit(solution)/shard_map/ppermute | solution.py:27
  94.8 101.3 %collective-permute-start.15 = (bf16[1024,2048]{1,0:T(8,128)(2,1)}, bf16[1024,2048]{1,0:T(8,128)(2,1)}, u32[]{:S(2)}, u32[]{:S(2)}) collective-permute-start(bf16[1024,2048]{1,0:T(8,128)(2,1)} %collective-permute-done.14.refs_2_), channel_id=1, source_target_pairs={{2,0},{4,6},{3,1},{5,7},{10,8},{12,14},{11,9},{13,15},{18,16},{20,... | collective-permute-start | bytes 12582920 | tf_op jit(solution)/shard_map/ppermute | solution.py:497
  117.7 48.6 %collective-permute-start.18 = (bf16[512,2048]{1,0:T(8,128)(2,1)}, bf16[512,2048]{1,0:T(8,128)(2,1)}, u32[]{:S(2)}, u32[]{:S(2)}) collective-permute-start(bf16[512,2048]{1,0:T(8,128)(2,1)} %get-tuple-element.69), channel_id=1, source_target_pairs={{2,4},{4,2},{3,5},{5,3},{10,12},{12,10},{11,13},{13,11},{18,20},{2... | collective-permute-start | bytes 6291464 | tf_op jit(solution)/shard_map/ppermute | solution.py:499
  119.6 2.8 copy-start.10
  119.6 5.8 %collective-permute-start.8 = (bf16[3,256,1024]{2,1,0:T(8,128)(2,1)}, bf16[3,256,1024]{2,1,0:T(8,128)(2,1)S(1)}, u32[]{:S(2)}, u32[]{:S(2)}) collective-permute-start(bf16[3,256,1024]{2,1,0:T(8,128)(2,1)} %collective-permute-done.6.refs_8_.refs_12_), channel_id=1, source_target_pairs={{0,8},{8,0},{16,24},{24,16},{1,9},{9,1},{17,25},{25,17},{2,10},{10... | collective-permute-start | bytes 4718600 | tf_op jit(solution)/shard_map/ppermute | solution.py:27
  121.2 35.5 %collective-permute-start.12 = (bf16[3,256,1024]{2,1,0:T(8,128)(2,1)}, bf16[3,256,1024]{2,1,0:T(8,128)(2,1)}, u32[]{:S(2)}, u32[]{:S(2)}) collective-permute-start(bf16[3,256,1024]{2,1,0:T(8,128)(2,1)} %get-tuple-element.39), channel_id=1, source_target_pairs={{0,1},{1,0},{2,3},{3,2},{4,5},{5,4},{6,7},{7,6},{8,9},{9,8},{10,11... | collective-permute-start | bytes 4718600 | tf_op jit(solution)/shard_map/ppermute | solution.py:27
  123.6 45.6 %collective-permute-start.16 = (bf16[3,256,1024]{2,1,0:T(8,128)(2,1)}, bf16[3,256,1024]{2,1,0:T(8,128)(2,1)}, u32[]{:S(2)}, u32[]{:S(2)}) collective-permute-start(bf16[3,256,1024]{2,1,0:T(8,128)(2,1)} %collective-permute-done.11.refs_7_.refs_5_), channel_id=1, source_target_pairs={{0,16},{8,24},{16,0},{24,8},{1,17},{9,25},{17,1},{25,9},{2,18},{10... | collective-permute-start | bytes 4718600 | tf_op jit(solution)/shard_map/ppermute | solution.py:27
  147.5 78.0 %collective-permute-start.9 = (bf16[512,2048]{1,0:T(8,128)(2,1)}, bf16[512,2048]{1,0:T(8,128)(2,1)S(1)}, u32[]{:S(2)}, u32[]{:S(2)}) collective-permute-start(bf16[512,2048]{1,0:T(8,128)(2,1)} %get-tuple-element.36), channel_id=1, source_target_pairs={{2,4},{4,2},{3,5},{5,3},{10,12},{12,10},{11,13},{13,11},{18,20},{2... | collective-permute-start | bytes 6291464 | tf_op jit(solution)/shard_map/ppermute | solution.py:571
  156.6 35.7 %collective-permute-start.20 = (bf16[3,256,1024]{2,1,0:T(8,128)(2,1)}, bf16[3,256,1024]{2,1,0:T(8,128)(2,1)S(1)}, u32[]{:S(2)}, u32[]{:S(2)}) collective-permute-start(bf16[3,256,1024]{2,1,0:T(8,128)(2,1)} %collective-permute-done.12.refs_5_.refs_6_), channel_id=1, source_target_pairs={{0,16},{8,24},{16,0},{24,8},{1,17},{9,25},{17,1},{25,9},{2,18},{10... | collective-permute-start | bytes 4718600 | tf_op jit(solution)/shard_map/ppermute | solution.py:27
  166.3 27.5 %collective-permute-start.13 = (bf16[3,256,1024]{2,1,0:T(8,128)(2,1)}, bf16[3,256,1024]{2,1,0:T(8,128)(2,1)S(1)}, u32[]{:S(2)}, u32[]{:S(2)}) collective-permute-start(bf16[3,256,1024]{2,1,0:T(8,128)(2,1)} %collective-permute-done.11.refs_7_.refs_5_), channel_id=1, source_target_pairs={{0,8},{8,0},{16,24},{24,16},{1,9},{9,1},{17,25},{25,17},{2,10},{10... | collective-permute-start | bytes 4718600 | tf_op jit(solution)/shard_map/ppermute | solution.py:27
  169.2 26.9 %collective-permute-start.17 = (bf16[3,256,1024]{2,1,0:T(8,128)(2,1)}, bf16[3,256,1024]{2,1,0:T(8,128)(2,1)S(1)}, u32[]{:S(2)}, u32[]{:S(2)}) collective-permute-start(bf16[3,256,1024]{2,1,0:T(8,128)(2,1)} %collective-permute-done.16.refs_13_), channel_id=1, source_target_pairs={{0,8},{8,0},{16,24},{24,16},{1,9},{9,1},{17,25},{25,17},{2,10},{10... | collective-permute-start | bytes 4718600 | tf_op jit(solution)/shard_map/ppermute | solution.py:27
  192.4 33.0 %copy-start.13 = (bf16[3,256,1024]{2,1,0:T(8,128)(2,1)}, bf16[3,256,1024]{2,1,0:T(8,128)(2,1)S(1)}, u32[]{:S(2)}) copy-start(bf16[3,256,1024]{2,1,0:T(8,128)(2,1)S(1)} %collective-permute-done.20.refs_7_.refs_14_) | copy-start | bytes 4718596
  192.4 37.4 %collective-permute-start.27 = (bf16[256,2048]{1,0:T(8,128)(2,1)}, bf16[256,2048]{1,0:T(8,128)(2,1)S(1)}, u32[]{:S(2)}, u32[]{:S(2)}) collective-permute-start(bf16[256,2048]{1,0:T(8,128)(2,1)} %get-tuple-element.71), channel_id=1, source_target_pairs={{2,0},{4,6},{3,1},{5,7},{10,8},{12,14},{11,9},{13,15},{18,16},{20,... | collective-permute-start | bytes 3145736 | tf_op jit(solution)/shard_map/ppermute | solution.py:604
  193.7 69.4 %collective-permute-start.25 = (bf16[256,2048]{1,0:T(8,128)(2,1)}, bf16[256,2048]{1,0:T(8,128)(2,1)}, u32[]{:S(2)}, u32[]{:S(2)}) collective-permute-start(bf16[256,2048]{1,0:T(8,128)(2,1)} %get-tuple-element.72), channel_id=1, source_target_pairs={{2,0},{4,6},{3,1},{5,7},{10,8},{12,14},{11,9},{13,15},{18,16},{20,... | collective-permute-start | bytes 3145736 | tf_op jit(solution)/shard_map/ppermute | solution.py:604
  223.2 8.8 %copy-start.18 = (f32[512,16]{0,1:T(8,128)S(1)}, f32[512,16]{0,1:T(8,128)}, u32[]{:S(2)}) copy-start(f32[512,16]{0,1:T(8,128)} %param.8) | copy-start | bytes 98308
  223.3 11.8 %collective-permute-start.19 = (bf16[3,256,1024]{2,1,0:T(8,128)(2,1)}, bf16[3,256,1024]{2,1,0:T(8,128)(2,1)}, u32[]{:S(2)}, u32[]{:S(2)}) collective-permute-start(bf16[3,256,1024]{2,1,0:T(8,128)(2,1)} %collective-permute-done.12.refs_5_.refs_6_), channel_id=1, source_target_pairs={{0,8},{8,0},{16,24},{24,16},{1,9},{9,1},{17,25},{25,17},{2,10},{10... | collective-permute-start | bytes 4718600 | tf_op jit(solution)/shard_map/ppermute | solution.py:27
  225.4 9.7 %collective-permute-start.21 = (bf16[3,256,1024]{2,1,0:T(8,128)(2,1)S(1)}, bf16[3,256,1024]{2,1,0:T(8,128)(2,1)}, u32[]{:S(2)}, u32[]{:S(2)}) collective-permute-start(bf16[3,256,1024]{2,1,0:T(8,128)(2,1)S(1)} %collective-permute-done.20.refs_7_.refs_14_), channel_id=1, source_target_pairs={{0,8},{8,0},{16,24},{24,16},{1,9},{9,1},{17,25},{25,17},{2,10},{10... | collective-permute-start | bytes 4718600 | tf_op jit(solution)/shard_map/ppermute | solution.py:27
  227.5 45.5 %collective-permute-start.23 = (bf16[256,2048]{1,0:T(8,128)(2,1)}, bf16[256,2048]{1,0:T(8,128)(2,1)}, u32[]{:S(2)}, u32[]{:S(2)}) collective-permute-start(bf16[256,2048]{1,0:T(8,128)(2,1)} %get-tuple-element.73), channel_id=1, source_target_pairs={{2,0},{4,6},{3,1},{5,7},{10,8},{12,14},{11,9},{13,15},{18,16},{20,... | collective-permute-start | bytes 3145736 | tf_op jit(solution)/shard_map/ppermute | solution.py:604
  229.7 23.9 %copy-start.17 = (bf16[256,2048]{1,0:T(8,128)(2,1)}, bf16[256,2048]{1,0:T(8,128)(2,1)S(1)}, u32[]{:S(2)}) copy-start(bf16[256,2048]{1,0:T(8,128)(2,1)S(1)} %collective-permute-done.27.refs_1_) | copy-start | bytes 3145732
  229.8 52.7 %collective-permute-start.10 = (bf16[256,2048]{1,0:T(8,128)(2,1)}, bf16[256,2048]{1,0:T(8,128)(2,1)}, u32[]{:S(2)}, u32[]{:S(2)}) collective-permute-start(bf16[256,2048]{1,0:T(8,128)(2,1)} %get-tuple-element.74), channel_id=1, source_target_pairs={{2,0},{4,6},{3,1},{5,7},{10,8},{12,14},{11,9},{13,15},{18,16},{20,... | collective-permute-start | bytes 3145736 | tf_op jit(solution)/shard_map/ppermute | solution.py:604
  262.5 33.7 %collective-permute-start.28 = (bf16[2,256,512]{2,1,0:T(8,128)(2,1)}, bf16[2,256,512]{2,1,0:T(8,128)(2,1)S(1)}, u32[]{:S(2)}, u32[]{:S(2)}) collective-permute-start(bf16[2,256,512]{2,1,0:T(8,128)(2,1)} %get-tuple-element.56), channel_id=1, source_target_pairs={{0,1},{1,0},{2,3},{3,2},{4,5},{5,4},{6,7},{7,6},{8,9},{9,8},{10,11... | collective-permute-start | bytes 1572872 | tf_op jit(solution)/shard_map/ppermute | solution.py:27
  272.0 27.3 %collective-permute-start.26 = (bf16[2,256,512]{2,1,0:T(8,128)(2,1)}, bf16[2,256,512]{2,1,0:T(8,128)(2,1)S(1)}, u32[]{:S(2)}, u32[]{:S(2)}) collective-permute-start(bf16[2,256,512]{2,1,0:T(8,128)(2,1)} %get-tuple-element.53), channel_id=1, source_target_pairs={{0,1},{1,0},{2,3},{3,2},{4,5},{5,4},{6,7},{7,6},{8,9},{9,8},{10,11... | collective-permute-start | bytes 1572872 | tf_op jit(solution)/shard_map/ppermute | solution.py:27
  281.8 7.8 %copy-start.19 = (f32[512,16]{0,1:T(8,128)S(1)}, f32[512,16]{0,1:T(8,128)}, u32[]{:S(2)}) copy-start(f32[512,16]{0,1:T(8,128)} %param.9) | copy-start | bytes 98308
  281.8 7.8 %copy-start.20 = (f32[512]{0:T(512)S(1)}, f32[512]{0:T(512)}, u32[]{:S(2)}) copy-start(f32[512]{0:T(512)} %param.10) | copy-start | bytes 6148
  281.9 20.6 %collective-permute-start.24 = (bf16[2,256,512]{2,1,0:T(8,128)(2,1)}, bf16[2,256,512]{2,1,0:T(8,128)(2,1)S(1)}, u32[]{:S(2)}, u32[]{:S(2)}) collective-permute-start(bf16[2,256,512]{2,1,0:T(8,128)(2,1)} %get-tuple-element.51), channel_id=1, source_target_pairs={{0,1},{1,0},{2,3},{3,2},{4,5},{5,4},{6,7},{7,6},{8,9},{9,8},{10,11... | collective-permute-start | bytes 1572872 | tf_op jit(solution)/shard_map/ppermute | solution.py:27
  288.7 20.9 %collective-permute-start.22 = (bf16[2,256,512]{2,1,0:T(8,128)(2,1)}, bf16[2,256,512]{2,1,0:T(8,128)(2,1)S(1)}, u32[]{:S(2)}, u32[]{:S(2)}) collective-permute-start(bf16[2,256,512]{2,1,0:T(8,128)(2,1)} %project.5), channel_id=1, source_target_pairs={{0,1},{1,0},{2,3},{3,2},{4,5},{5,4},{6,7},{7,6},{8,9},{9,8},{10,11... | collective-permute-start | bytes 1572872 | tf_op jit(solution)/shard_map/ppermute | solution.py:27
  289.7 6.5 %copy-start.1 = (bf16[3,256,512]{2,1,0:T(8,128)(2,1)S(1)}, bf16[3,256,512]{2,1,0:T(8,128)(2,1)}, u32[]{:S(2)}) copy-start(bf16[3,256,512]{2,1,0:T(8,128)(2,1)} %get-tuple-element.55.kept.refs_10_) | copy-start | bytes 2359300
  296.2 3.1 copy-start.2
  296.2 6.2 %copy-start.3 = (bf16[3,256,512]{2,1,0:T(8,128)(2,1)S(1)}, bf16[3,256,512]{2,1,0:T(8,128)(2,1)}, u32[]{:S(2)}) copy-start(bf16[3,256,512]{2,1,0:T(8,128)(2,1)} %get-tuple-element.50.kept.refs_12_) | copy-start | bytes 2359300
  299.3 10.3 %copy-start = (bf16[3,256,512]{2,1,0:T(8,128)(2,1)S(1)}, bf16[3,256,512]{2,1,0:T(8,128)(2,1)}, u32[]{:S(2)}) copy-start(bf16[3,256,512]{2,1,0:T(8,128)(2,1)} %project.6.kept.refs_13_) | copy-start | bytes 2359300
  302.4 16.8 %copy-start.4 = (f32[4,2,16,8,128]{4,3,2,1,0:T(8,128)S(1)}, f32[4,2,16,8,128]{4,3,2,1,0:T(8,128)}, u32[]{:S(2)}) copy-start(f32[4,2,16,8,128]{4,3,2,1,0:T(8,128)} %carry.1.refs_4_) | copy-start | bytes 1572868
  302.4 16.8 %copy-start.5 = (s32[3]{0:T(128)S(1)}, s32[3]{0:T(128)}, u32[]{:S(2)}) copy-start(s32[3]{0:T(128)} %pad_add_fusion.place) | copy-start | bytes 40
  312.7 3.0 collective-permute-start.29
  314.0 3.7 %collective-permute-start.30 = (f32[16,8,128]{2,1,0:T(8,128)S(1)}, f32[16,8,128]{2,1,0:T(8,128)S(1)}, u32[]{:S(2)}, u32[]{:S(2)}) collective-permute-start(f32[16,8,128]{2,1,0:T(8,128)S(1)} %get-tuple-element.60.refs_0_), channel_id=1, source_target_pairs={{0,16},{8,24},{16,0},{24,8},{1,17},{9,25},{17,1},{25,9},{2,18},{10... | collective-permute-start | bytes 196616 | tf_op jit(solution)/shard_map/ppermute | solution.py:27
  315.2 4.0 %collective-permute-start.31 = (f32[16,8,128]{2,1,0:T(8,128)S(1)}, f32[16,8,128]{2,1,0:T(8,128)S(1)}, u32[]{:S(2)}, u32[]{:S(2)}) collective-permute-start(f32[16,8,128]{2,1,0:T(8,128)S(1)} %get-tuple-element.60.refs_0_), channel_id=1, source_target_pairs={{0,24},{8,16},{16,8},{24,0},{1,25},{9,17},{17,9},{25,1},{2,26},{10... | collective-permute-start | bytes 196616 | tf_op jit(solution)/shard_map/ppermute | solution.py:27
  (5 other events, 7.8 us)

commit v2 on v1

--- a/solution.py
+++ b/solution.py
@@ -416,8 +416,7 @@
     locals_ = [refs.pop(0) for _ in range(n_chunks)]
     kept = [refs.pop(0) for _ in range(n_chunks)]
     given = [refs.pop(0) for _ in range(n_chunks)]
-    out = refs.pop(0)
-    conv = refs.pop(0)
+    out, conv, queries = refs
     poles, sublanes, _ = decay.shape
     groups = sublanes // 2
     pair = place[0]
@@ -429,28 +428,41 @@
             states[r] = states[r] + weights[mask, 0, r] * end + weights[mask, 1, r] * turned
     factors = [decay[r] for r in range(poles)]
     states = tuple(states)
-    base = 0
-    for k in range(n_chunks):
-        rows = locals_[k].shape[0]
-
-        def step(t, states):
-            new = [factors[r] * states[r] for r in range(poles)]
-            total = list(new)
-            while len(total) > 1:
-                total = [a + b for a, b in zip(total[::2], total[1::2])]
-            conv[t] = total[0] + locals_[k][t]
-            return tuple(new)
-
-        states = lax.fori_loop(0, rows, step, states, unroll=8)
-        for side, ref in enumerate((kept[k], given[k])):
-            segment = pair if side == 0 else 1 - pair
-            column = pl.multiple_of(segment * seg_len + base, 128)
-            for g in range(groups):
-                lanes = slice(g * 128, (g + 1) * 128)
-                query = ref[0, :, lanes].astype(jnp.float32)
-                gated = query * conv[:rows, side * groups + g, :]
-                out[lanes, pl.ds(column, rows)] = gated.T.astype(jnp.bfloat16)
-        base += rows
+    rows = locals_[0].shape[0]
+    per_lane = rows // 128
+    tiles = sublanes * per_lane
+    span = rows // tiles
+    for k in range(n_chunks + 1):
+        now, before = k % 2, (k + 1) % 2
+        if k < n_chunks:
+            queries[now, 0] = kept[k][0]
+            queries[now, 1] = given[k][0]
+
+        def body(tile, states):
+            if k > 0:
+                lane, part = lax.div(tile, per_lane), lax.rem(tile, per_lane)
+                side, group = lax.div(lane, groups), lax.rem(lane, groups)
+                first = pl.multiple_of(lane * rows + part * 128, 128)
+                value = conv[before, pl.ds(first, 128), :]
+                channels = pl.ds(pl.multiple_of(group * 128, 128), 128)
+                times = pl.ds(pl.multiple_of(part * 128, 128), 128)
+                query = queries[before, side, times, channels].astype(jnp.float32)
+                segment = jnp.where(side == 0, pair, 1 - pair)
+                column = segment * seg_len + (k - 1) * rows + part * 128
+                out[channels, pl.ds(pl.multiple_of(column, 128), 128)] = (
+                    (query * value).T.astype(jnp.bfloat16)
+                )
+            if k < n_chunks:
+                for j in range(span):
+                    t = tile * span + j
+                    states = tuple(factors[r] * states[r] for r in range(poles))
+                    total = list(states)
+                    while len(total) > 1:
+                        total = [a + b for a, b in zip(total[::2], total[1::2])]
+                    conv[now, pl.ds(t, sublanes, stride=rows), :] = total[0] + locals_[k][t]
+            return states
+
+        states = lax.fori_loop(0, tiles, body, states)
 
 
 def finish(place, ends, weights, decay, locals_, kept, given, seg_len):
@@ -459,7 +471,7 @@
     operands = list(ends) + [weights, decay] + list(locals_) + list(kept) + list(given)
     lanes = decay.shape[1:]
     channels = kept[0].shape[2]
-    longest = max(k.shape[1] for k in kept)
+    rows = kept[0].shape[1]
     return pl.pallas_call(
         functools.partial(finish_kernel, len(ends), n_chunks, seg_len),
         grid_spec=pltpu.PrefetchScalarGridSpec(
@@ -467,7 +479,10 @@
             grid=(),
             in_specs=[local] * len(operands),
             out_specs=local,
-            scratch_shapes=[pltpu.VMEM((longest,) + lanes, jnp.float32)],
+            scratch_shapes=[
+                pltpu.VMEM((2, lanes[0] * rows, 128), jnp.float32),
+                pltpu.VMEM((2, 2, rows, channels), jnp.bfloat16),
+            ],
         ),
         out_shape=jax.ShapeDtypeStruct((channels, 2 * seg_len), jnp.bfloat16),
         compiler_params=pltpu.CompilerParams(vmem_limit_bytes=40 * MIB),

time: 330 us -> 333 us (level)
  Pallas kernels: 129 us -> 133 us
    pallas_call x1, Pallas kernels: 9.71 us -> 13.4 us  [finish(): pl.pallas_call(functools.partial(finish_kernel, len(ends), n_chunks, seg_...]
where the time goes in v2:
time: 333 us
  Pallas kernels  133 us (40%)
  waiting for transfers between devices  131 us (39%)
  starting transfers between devices  48.4 us (15%)
  local copies, waits for them, and re-layouts  18.3 us (5%)
    ppermute x23, waiting for transfers between devices, exchanged(): return lax.ppermute(block, axis, [(i, i ^ mask) for i in range(count)])  116 us
    pallas_call x8, Pallas kernels, project(): pl.pallas_call(functools.partial(project_kernel, plan, len(inputs), len(p...  105 us
    ppermute x23, starting transfers between devices, exchanged(): return lax.ppermute(block, axis, [(i, i ^ mask) for i in range(count)])  27.4 us
    pallas_call x1, Pallas kernels, finish(): pl.pallas_call(functools.partial(finish_kernel, len(ends), n_chunks, seg_...  13.4 us
    pallas_call x4, Pallas kernels, scan(): pl.pallas_call(scan_kernel, in_specs=[local] * 6, out_specs=[local] * 2,...  12.2 us
    ppermute x1, waiting for transfers between devices, per_device(): far_middle = [lax.ppermute(block, 'tp', [(1, 2), (2, 1)])]  8.42 us
    ppermute x4, starting transfers between devices, per_device(): last = lax.ppermute(block, 'tp', [(1, 0), (2, 3)])  8.18 us
  transfers between devices with their start and end apart: 32, of which 13 were waited for; matrix products, arithmetic and copies ran while one was open for 5% of the time, Pallas kernels for 35%

profile of v2, /device:TPU:9, one launch (start us, length us, event | category | flops | bytes accessed | tf_op | source)
XLA Modules:
  0.0 332.7 jit_solution(9412390840455785182)
XLA Ops:
  0.0 4.5 %collective-permute-start.14 = (bf16[1024,2048]{1,0:T(8,128)(2,1)}, bf16[1024,2048]{1,0:T(8,128)(2,1)}, u32[]{:S(2)}, u32[]{:S(2)}) collective-permute-start(bf16[1024,2048]{1,0:T(8,128)(2,1)} %refs_0_.5), channel_id=1, source_target_pairs={{2,4},{4,2},{3,5},{5,3},{10,12},{12,10},{11,13},{13,11},{18,20},{2... | collective-permute-start | bytes 12582920 | tf_op jit(solution)/shard_map/ppermute | solution.py:511
  4.5 4.8 %dynamic-slice_bitcast_fusion = (bf16[3,256,1024]{2,1,0:T(8,128)(2,1)}, bf16[3,256,1024]{2,1,0:T(8,128)(2,1)S(1)}, bf16[3,256,1024]{2,1,0:T(8,128)(2,1)S(1)}, bf16[3,256,1024]{2,1,0:T(8,128)(2,1)S(1)}) fusion(bf16[4096,3,1024]{2,0,1:T(8,128)(2,1)} %param.7, s32[]{:T(128)S(6)} %select_n.15, s32[]{:T(128)S(6)} %select_n.13, s32[]{:T(128)S(6)} %select_n.12, ...), kind=kLoop, calls=%fused_computation | loop fusion | bytes 12582928 | tf_op jit(solution)/shard_map/dynamic_slice | solution.py:542
  9.3 1.2 collective-permute-start.1
  10.7 33.3 %collective-permute-done.1.refs_3_.refs_5_ = bf16[3,256,1024]{2,1,0:T(8,128)(2,1)S(1)} collective-permute-done((bf16[3,256,1024]{2,1,0:T(8,128)(2,1)S(1)}, bf16[3,256,1024]{2,1,0:T(8,128)(2,1)S(1)}, u32[]{:S(2)}, u32[]{:S(2)}) %collective-permute-start.1) | collective-permute-done | bytes 1572896 | tf_op jit(solution)/shard_map/ppermute | solution.py:27
  44.0 3.8 %collective-permute-start.3 = (bf16[3,256,1024]{2,1,0:T(8,128)(2,1)S(1)}, bf16[3,256,1024]{2,1,0:T(8,128)(2,1)S(1)}, u32[]{:S(2)}, u32[]{:S(2)}) collective-permute-start(bf16[3,256,1024]{2,1,0:T(8,128)(2,1)S(1)} %collective-permute-done.1.refs_3_.refs_5_), channel_id=1, source_target_pairs={{0,8},{8,0},{16,24},{24,16},{1,9},{9,1},{17,25},{25,17},{2,10},{10... | collective-permute-start | bytes 4718600 | tf_op jit(solution)/shard_map/ppermute | solution.py:27
  47.8 1.2 collective-permute-start.5
  49.1 28.7 %collective-permute-done.2.refs_4_.refs_6_ = bf16[3,256,1024]{2,1,0:T(8,128)(2,1)S(1)} collective-permute-done((bf16[3,256,1024]{2,1,0:T(8,128)(2,1)S(1)}, bf16[3,256,1024]{2,1,0:T(8,128)(2,1)S(1)}, u32[]{:S(2)}, u32[]{:S(2)}) %collective-permute-start.2) | collective-permute-done | bytes 1572896 | tf_op jit(solution)/shard_map/ppermute | solution.py:27
  79.0 5.0 %collective-permute-done.5.refs_7_.refs_11_ = bf16[3,256,1024]{2,1,0:T(8,128)(2,1)S(1)} collective-permute-done((bf16[3,256,1024]{2,1,0:T(8,128)(2,1)S(1)}, bf16[3,256,1024]{2,1,0:T(8,128)(2,1)S(1)}, u32[]{:S(2)}, u32[]{:S(2)}) %collective-permute-start.5) | collective-permute-done | bytes 1572896 | tf_op jit(solution)/shard_map/ppermute | solution.py:27
  85.0 1.2 collective-permute-start.11
  86.3 5.5 %collective-permute-done.refs_1_ = bf16[1024,2048]{1,0:T(8,128)(2,1)} collective-permute-done((bf16[1024,2048]{1,0:T(8,128)(2,1)}, bf16[1024,2048]{1,0:T(8,128)(2,1)}, u32[]{:S(2)}, u32[]{:S(2)}) %collective-permute-start) | collective-permute-done | bytes 4194336 | tf_op jit(solution)/shard_map/ppermute | solution.py:510
  91.8 1.5 collective-permute-start.4
  93.3 1.5 collective-permute-done.14.refs_2_
  94.8 3.4 %collective-permute-start.15 = (bf16[1024,2048]{1,0:T(8,128)(2,1)}, bf16[1024,2048]{1,0:T(8,128)(2,1)}, u32[]{:S(2)}, u32[]{:S(2)}) collective-permute-start(bf16[1024,2048]{1,0:T(8,128)(2,1)} %collective-permute-done.14.refs_2_), channel_id=1, source_target_pairs={{2,0},{4,6},{3,1},{5,7},{10,8},{12,14},{11,9},{13,15},{18,16},{20,... | collective-permute-start | bytes 12582920 | tf_op jit(solution)/shard_map/ppermute | solution.py:512
  98.1 4.8 %fusion = (bf16[512,2048]{1,0:T(8,128)(2,1)}, bf16[512,2048]{1,0:T(8,128)(2,1)}) fusion(bf16[1024,2048]{1,0:T(8,128)(2,1)} %collective-permute-done.refs_1_), kind=kLoop, calls=%fused_computation.10 | loop fusion | bytes 8388608 | tf_op jit(solution)/shard_map/slice | solution.py:513
  103.0 14.7 %collective-permute-done.6.refs_8_.refs_12_ = bf16[3,256,1024]{2,1,0:T(8,128)(2,1)} collective-permute-done((bf16[3,256,1024]{2,1,0:T(8,128)(2,1)S(1)}, bf16[3,256,1024]{2,1,0:T(8,128)(2,1)}, u32[]{:S(2)}, u32[]{:S(2)}) %collective-permute-start.6) | collective-permute-done | bytes 1572896 | tf_op jit(solution)/shard_map/ppermute | solution.py:27
  117.7 1.9 collective-permute-start.18
  121.2 1.2 collective-permute-start.12
  126.5 20.9 %part_a.1.refs_17_ = f32[3,1024,1024]{2,1,0:T(8,128)} custom-call(s32[3]{0:T(128)} %pad_add_fusion.place, bf16[1024,2048]{1,0:T(8,128)(2,1)} %refs_0_.5, bf16[1024,2048]{1,0:T(8,128)(2,1)} %collective-permute-done.refs_1_, bf16[3,4096,1024]{2,1,0:T(8,128)(2,1)} %bitcast.18, bf16[3,256,1024]{2,1,0:T(8,128)(2,1)} %copy-done.6, ...), custom_call_target="tpu_custom_call" | custom-call | tf_op jit(solution)/shard_map/part_a/pallas_call | solution.py:217
  147.5 3.1 collective-permute-start.9
  150.6 6.0 %collective-permute-done.12.refs_5_.refs_6_ = bf16[3,256,1024]{2,1,0:T(8,128)(2,1)} collective-permute-done((bf16[3,256,1024]{2,1,0:T(8,128)(2,1)}, bf16[3,256,1024]{2,1,0:T(8,128)(2,1)}, u32[]{:S(2)}, u32[]{:S(2)}) %collective-permute-start.12) | collective-permute-done | bytes 1572896 | tf_op jit(solution)/shard_map/ppermute | solution.py:27
  157.8 8.4 %collective-permute-done.18.refs_0_ = bf16[512,2048]{1,0:T(8,128)(2,1)} collective-permute-done((bf16[512,2048]{1,0:T(8,128)(2,1)}, bf16[512,2048]{1,0:T(8,128)(2,1)}, u32[]{:S(2)}, u32[]{:S(2)}) %collective-permute-start.18) | collective-permute-done | bytes 2097184 | tf_op jit(solution)/shard_map/ppermute | solution.py:514
  166.3 2.9 collective-permute-start.13
  169.2 3.1 fusion.1
  172.3 20.0 %collective-permute-done.20.refs_7_.refs_14_ = bf16[3,256,1024]{2,1,0:T(8,128)(2,1)S(1)} collective-permute-done((bf16[3,256,1024]{2,1,0:T(8,128)(2,1)}, bf16[3,256,1024]{2,1,0:T(8,128)(2,1)S(1)}, u32[]{:S(2)}, u32[]{:S(2)}) %collective-permute-start.20) | collective-permute-done | bytes 1572896 | tf_op jit(solution)/shard_map/ppermute | solution.py:27
  192.4 1.3 collective-permute-start.27
  193.7 2.3 collective-permute-start.25
  197.2 26.0 %part_b.1.refs_9_ = f32[3,1024,1024]{2,1,0:T(8,128)} custom-call(s32[3]{0:T(128)} %pad_add_fusion.place, bf16[1024,2048]{1,0:T(8,128)(2,1)} %refs_0_.5, bf16[1024,2048]{1,0:T(8,128)(2,1)} %collective-permute-done.refs_1_, bf16[1024,2048]{1,0:T(8,128)(2,1)} %collective-permute-done.14.refs_2_, bf16[1024,2048]{1,0:T(8,128)(2,1)} %collective-permute-done.15.refs_3_, ...), custom_call_target="tpu_custom_call" | custom-call | tf_op jit(solution)/shard_map/part_b/pallas_call | solution.py:217
  223.3 2.1 collective-permute-start.19
  225.5 1.8 fusion.2
  227.5 2.3 collective-permute-start.23
  229.8 2.3 collective-permute-start.10
  232.7 2.4 carry.1.refs_4_
  235.1 18.6 %part_c.1.refs_19_ = f32[3,1024,1024]{2,1,0:T(8,128)} custom-call(s32[3]{0:T(128)} %pad_add_fusion.place, bf16[1024,2048]{1,0:T(8,128)(2,1)} %refs_0_.5, bf16[1024,2048]{1,0:T(8,128)(2,1)} %collective-permute-done.refs_1_, bf16[1024,2048]{1,0:T(8,128)(2,1)} %collective-permute-done.14.refs_2_, bf16[1024,2048]{1,0:T(8,128)(2,1)} %collective-permute-done.15.refs_3_, ...), custom_call_target="tpu_custom_call" | custom-call | tf_op jit(solution)/shard_map/part_c/pallas_call | solution.py:217
  253.7 8.8 %project.9 = (bf16[3,256,512]{2,1,0:T(8,128)(2,1)}, bf16[2,256,512]{2,1,0:T(8,128)(2,1)}) custom-call(s32[3]{0:T(128)} %pad_add_fusion.place, bf16[512,2048]{1,0:T(8,128)(2,1)} %collective-permute-done.18.refs_0_, bf16[256,2048]{1,0:T(8,128)(2,1)} %copy-done.17, bf16[3,4096,1024]{2,1,0:T(8,128)(2,1)} %bitcast.21, bf16[3,256,1024]{2,1,0:T(8,128)(2,1)} %copy-done.6, ...), custom_call_target="tpu_custom_call" | custom-call | tf_op jit(solution)/shard_map/project/pallas_call | solution.py:217
  263.2 8.8 %project.8 = (bf16[3,256,512]{2,1,0:T(8,128)(2,1)}, bf16[2,256,512]{2,1,0:T(8,128)(2,1)}) custom-call(s32[3]{0:T(128)} %pad_add_fusion.place, bf16[512,2048]{1,0:T(8,128)(2,1)} %collective-permute-done.18.refs_0_, bf16[256,2048]{1,0:T(8,128)(2,1)} %collective-permute-done.25.refs_1_, bf16[3,4096,1024]{2,1,0:T(8,128)(2,1)} %bitcast.22, ...), custom_call_target="tpu_custom_call" | custom-call | tf_op jit(solution)/shard_map/project/pallas_call | solution.py:217
  273.0 8.8 %project.7 = (bf16[3,256,512]{2,1,0:T(8,128)(2,1)}, bf16[2,256,512]{2,1,0:T(8,128)(2,1)}) custom-call(s32[3]{0:T(128)} %pad_add_fusion.place, bf16[512,2048]{1,0:T(8,128)(2,1)} %copy-done.16, bf16[256,2048]{1,0:T(8,128)(2,1)} %collective-permute-done.23.refs_1_, bf16[3,4096,1024]{2,1,0:T(8,128)(2,1)} %bitcast.23, bf16[3,256,1024]{2,1,0:T(8,128)(2,1)} %copy-done.6, ...), custom_call_target="tpu_custom_call" | custom-call | tf_op jit(solution)/shard_map/project/pallas_call | solution.py:217
  282.5 6.2 %project.5 = bf16[2,256,512]{2,1,0:T(8,128)(2,1)} custom-call(s32[3]{0:T(128)} %pad_add_fusion.place, bf16[512,2048]{1,0:T(8,128)(2,1)} %copy-done.16, bf16[256,2048]{1,0:T(8,128)(2,1)} %collective-permute-done.10.refs_1_, bf16[3,4096,1024]{2,1,0:T(8,128)(2,1)} %bitcast.24, bf16[3,256,1024]{2,1,0:T(8,128)(2,1)} %copy-done.6, ...), custom_call_target="tpu_custom_call" | custom-call | tf_op jit(solution)/shard_map/project/pallas_call | solution.py:217
  289.7 6.5 %project.6.kept.refs_13_ = bf16[3,256,512]{2,1,0:T(8,128)(2,1)} custom-call(s32[3]{0:T(128)} %pad_add_fusion.place, bf16[512,2048]{1,0:T(8,128)(2,1)} %copy-done.16, bf16[256,2048]{1,0:T(8,128)(2,1)} %collective-permute-done.10.refs_1_, bf16[3,4096,1024]{2,1,0:T(8,128)(2,1)} %bitcast.25, bf16[3,256,1024]{2,1,0:T(8,128)(2,1)} %copy-done.6, ...), custom_call_target="tpu_custom_call" | custom-call | tf_op jit(solution)/shard_map/project/pallas_call | solution.py:217
  296.3 3.1 scan.4
  299.4 3.1 scan.5
  302.5 3.1 scan.6
  305.5 4.1 %collective-permute-done.22.given.refs_17_ = bf16[2,256,512]{2,1,0:T(8,128)(2,1)S(1)} collective-permute-done((bf16[2,256,512]{2,1,0:T(8,128)(2,1)}, bf16[2,256,512]{2,1,0:T(8,128)(2,1)S(1)}, u32[]{:S(2)}, u32[]{:S(2)}) %collective-permute-start.22) | collective-permute-done | bytes 524320 | tf_op jit(solution)/shard_map/ppermute | solution.py:27
  309.6 3.1 scan.7
  312.7 1.3 collective-permute-start.29
  314.0 1.2 collective-permute-start.30
  315.7 2.0 collective-permute-done.30.refs_2_
  317.7 1.6 collective-permute-done.31.refs_3_
  319.3 13.4 %finish.1 = bf16[512,2048]{1,0:T(8,128)(2,1)} custom-call(s32[3]{0:T(128)S(1)} %copy-done.5, f32[16,8,128]{2,1,0:T(8,128)S(1)} %get-tuple-element.60.refs_0_, f32[16,8,128]{2,1,0:T(8,128)S(1)} %collective-permute-done.29.refs_1_, f32[16,8,128]{2,1,0:T(8,128)S(1)} %collective-permute-done.30.refs_2_, f32[16,8,128]{2,1,0:T(8,128)S(1)} %collective-permute-done.31.refs_3_, ...), custom_call_target="tpu_custom_call" | custom-call | flops 33554432 | bytes 8388608 | tf_op jit(solution)/shard_map/finish/pallas_call | solution.py:475
  (84 shorter events, 15.3 us)
Async XLA Ops:
  0.0 91.8 %collective-permute-start = (bf16[1024,2048]{1,0:T(8,128)(2,1)}, bf16[1024,2048]{1,0:T(8,128)(2,1)}, u32[]{:S(2)}, u32[]{:S(2)}) collective-permute-start(bf16[1024,2048]{1,0:T(8,128)(2,1)} %refs_0_.5), channel_id=1, source_target_pairs={{0,2},{2,0},{4,6},{6,4},{1,3},{3,1},{5,7},{7,5},{8,10},{10,8},{12,... | collective-permute-start | bytes 12582920 | tf_op jit(solution)/shard_map/ppermute | solution.py:510
  0.0 94.8 %collective-permute-start.14 = (bf16[1024,2048]{1,0:T(8,128)(2,1)}, bf16[1024,2048]{1,0:T(8,128)(2,1)}, u32[]{:S(2)}, u32[]{:S(2)}) collective-permute-start(bf16[1024,2048]{1,0:T(8,128)(2,1)} %refs_0_.5), channel_id=1, source_target_pairs={{2,4},{4,2},{3,5},{5,3},{10,12},{12,10},{11,13},{13,11},{18,20},{2... | collective-permute-start | bytes 12582920 | tf_op jit(solution)/shard_map/ppermute | solution.py:511
  9.3 34.8 %collective-permute-start.1 = (bf16[3,256,1024]{2,1,0:T(8,128)(2,1)S(1)}, bf16[3,256,1024]{2,1,0:T(8,128)(2,1)S(1)}, u32[]{:S(2)}, u32[]{:S(2)}) collective-permute-start(bf16[3,256,1024]{2,1,0:T(8,128)(2,1)S(1)} %get-tuple-element.67), channel_id=1, source_target_pairs={{0,1},{1,0},{2,3},{3,2},{4,5},{5,4},{6,7},{7,6},{8,9},{9,8},{10,11... | collective-permute-start | bytes 4718600 | tf_op jit(solution)/shard_map/ppermute | solution.py:27
  10.5 67.2 %collective-permute-start.2 = (bf16[3,256,1024]{2,1,0:T(8,128)(2,1)S(1)}, bf16[3,256,1024]{2,1,0:T(8,128)(2,1)S(1)}, u32[]{:S(2)}, u32[]{:S(2)}) collective-permute-start(bf16[3,256,1024]{2,1,0:T(8,128)(2,1)S(1)} %get-tuple-element.66), channel_id=1, source_target_pairs={{0,1},{1,0},{2,3},{3,2},{4,5},{5,4},{6,7},{7,6},{8,9},{9,8},{10,11... | collective-permute-start | bytes 4718600 | tf_op jit(solution)/shard_map/ppermute | solution.py:27
  44.0 59.0 %copy-start.6 = (bf16[3,256,1024]{2,1,0:T(8,128)(2,1)}, bf16[3,256,1024]{2,1,0:T(8,128)(2,1)S(1)}, u32[]{:S(2)}) copy-start(bf16[3,256,1024]{2,1,0:T(8,128)(2,1)S(1)} %collective-permute-done.1.refs_3_.refs_5_) | copy-start | bytes 4718596
  44.0 34.9 %collective-permute-start.3 = (bf16[3,256,1024]{2,1,0:T(8,128)(2,1)S(1)}, bf16[3,256,1024]{2,1,0:T(8,128)(2,1)S(1)}, u32[]{:S(2)}, u32[]{:S(2)}) collective-permute-start(bf16[3,256,1024]{2,1,0:T(8,128)(2,1)S(1)} %collective-permute-done.1.refs_3_.refs_5_), channel_id=1, source_target_pairs={{0,8},{8,0},{16,24},{24,16},{1,9},{9,1},{17,25},{25,17},{2,10},{10... | collective-permute-start | bytes 4718600 | tf_op jit(solution)/shard_map/ppermute | solution.py:27
  47.8 36.1 %collective-permute-start.5 = (bf16[3,256,1024]{2,1,0:T(8,128)(2,1)S(1)}, bf16[3,256,1024]{2,1,0:T(8,128)(2,1)S(1)}, u32[]{:S(2)}, u32[]{:S(2)}) collective-permute-start(bf16[3,256,1024]{2,1,0:T(8,128)(2,1)S(1)} %collective-permute-done.1.refs_3_.refs_5_), channel_id=1, source_target_pairs={{0,16},{8,24},{16,0},{24,8},{1,17},{9,25},{17,1},{25,9},{2,18},{10... | collective-permute-start | bytes 4718600 | tf_op jit(solution)/shard_map/ppermute | solution.py:27
  77.7 25.3 %copy-start.7 = (bf16[3,256,1024]{2,1,0:T(8,128)(2,1)}, bf16[3,256,1024]{2,1,0:T(8,128)(2,1)S(1)}, u32[]{:S(2)}) copy-start(bf16[3,256,1024]{2,1,0:T(8,128)(2,1)S(1)} %collective-permute-done.2.refs_4_.refs_6_) | copy-start | bytes 4718596
  77.7 39.9 %collective-permute-start.6 = (bf16[3,256,1024]{2,1,0:T(8,128)(2,1)S(1)}, bf16[3,256,1024]{2,1,0:T(8,128)(2,1)}, u32[]{:S(2)}, u32[]{:S(2)}) collective-permute-start(bf16[3,256,1024]{2,1,0:T(8,128)(2,1)S(1)} %collective-permute-done.2.refs_4_.refs_6_), channel_id=1, source_target_pairs={{0,16},{8,24},{16,0},{24,8},{1,17},{9,25},{17,1},{25,9},{2,18},{10... | collective-permute-start | bytes 4718600 | tf_op jit(solution)/shard_map/ppermute | solution.py:27
  78.9 7.3 %copy-start.8 = (bf16[3,256,1024]{2,1,0:T(8,128)(2,1)}, bf16[3,256,1024]{2,1,0:T(8,128)(2,1)S(1)}, u32[]{:S(2)}) copy-start(bf16[3,256,1024]{2,1,0:T(8,128)(2,1)S(1)} %collective-permute-done.3.refs_5_.refs_8_.refs_7_) | copy-start | bytes 4718596
  84.0 19.0 %copy-start.9 = (bf16[3,256,1024]{2,1,0:T(8,128)(2,1)}, bf16[3,256,1024]{2,1,0:T(8,128)(2,1)S(1)}, u32[]{:S(2)}) copy-start(bf16[3,256,1024]{2,1,0:T(8,128)(2,1)S(1)} %collective-permute-done.5.refs_7_.refs_11_) | copy-start | bytes 4718596
  84.0 35.6 %collective-permute-start.7 = (bf16[3,256,1024]{2,1,0:T(8,128)(2,1)S(1)}, bf16[3,256,1024]{2,1,0:T(8,128)(2,1)S(1)}, u32[]{:S(2)}, u32[]{:S(2)}) collective-permute-start(bf16[3,256,1024]{2,1,0:T(8,128)(2,1)S(1)} %collective-permute-done.5.refs_7_.refs_11_), channel_id=1, source_target_pairs={{0,8},{8,0},{16,24},{24,16},{1,9},{9,1},{17,25},{25,17},{2,10},{10... | collective-permute-start | bytes 4718600 | tf_op jit(solution)/shard_map/ppermute | solution.py:27
  85.0 36.1 %collective-permute-start.11 = (bf16[3,256,1024]{2,1,0:T(8,128)(2,1)S(1)}, bf16[3,256,1024]{2,1,0:T(8,128)(2,1)}, u32[]{:S(2)}, u32[]{:S(2)}) collective-permute-start(bf16[3,256,1024]{2,1,0:T(8,128)(2,1)S(1)} %get-tuple-element.37), channel_id=1, source_target_pairs={{0,1},{1,0},{2,3},{3,2},{4,5},{5,4},{6,7},{7,6},{8,9},{9,8},{10,11... | collective-permute-start | bytes 4718600 | tf_op jit(solution)/shard_map/ppermute | solution.py:27
  91.8 30.7 %collective-permute-start.4 = (bf16[3,256,1024]{2,1,0:T(8,128)(2,1)S(1)}, bf16[3,256,1024]{2,1,0:T(8,128)(2,1)S(1)}, u32[]{:S(2)}, u32[]{:S(2)}) collective-permute-start(bf16[3,256,1024]{2,1,0:T(8,128)(2,1)S(1)} %collective-permute-done.2.refs_4_.refs_6_), channel_id=1, source_target_pairs={{0,8},{8,0},{16,24},{24,16},{1,9},{9,1},{17,25},{25,17},{2,10},{10... | collective-permute-start | bytes 4718600 | tf_op jit(solution)/shard_map/ppermute | solution.py:27
  94.8 101.3 %collective-permute-start.15 = (bf16[1024,2048]{1,0:T(8,128)(2,1)}, bf16[1024,2048]{1,0:T(8,128)(2,1)}, u32[]{:S(2)}, u32[]{:S(2)}) collective-permute-start(bf16[1024,2048]{1,0:T(8,128)(2,1)} %collective-permute-done.14.refs_2_), channel_id=1, source_target_pairs={{2,0},{4,6},{3,1},{5,7},{10,8},{12,14},{11,9},{13,15},{18,16},{20,... | collective-permute-start | bytes 12582920 | tf_op jit(solution)/shard_map/ppermute | solution.py:512
  117.7 48.6 %collective-permute-start.18 = (bf16[512,2048]{1,0:T(8,128)(2,1)}, bf16[512,2048]{1,0:T(8,128)(2,1)}, u32[]{:S(2)}, u32[]{:S(2)}) collective-permute-start(bf16[512,2048]{1,0:T(8,128)(2,1)} %get-tuple-element.69), channel_id=1, source_target_pairs={{2,4},{4,2},{3,5},{5,3},{10,12},{12,10},{11,13},{13,11},{18,20},{2... | collective-permute-start | bytes 6291464 | tf_op jit(solution)/shard_map/ppermute | solution.py:514
  119.6 2.8 copy-start.10
  119.6 5.8 %collective-permute-start.8 = (bf16[3,256,1024]{2,1,0:T(8,128)(2,1)}, bf16[3,256,1024]{2,1,0:T(8,128)(2,1)S(1)}, u32[]{:S(2)}, u32[]{:S(2)}) collective-permute-start(bf16[3,256,1024]{2,1,0:T(8,128)(2,1)} %collective-permute-done.6.refs_8_.refs_12_), channel_id=1, source_target_pairs={{0,8},{8,0},{16,24},{24,16},{1,9},{9,1},{17,25},{25,17},{2,10},{10... | collective-permute-start | bytes 4718600 | tf_op jit(solution)/shard_map/ppermute | solution.py:27
  121.2 35.5 %collective-permute-start.12 = (bf16[3,256,1024]{2,1,0:T(8,128)(2,1)}, bf16[3,256,1024]{2,1,0:T(8,128)(2,1)}, u32[]{:S(2)}, u32[]{:S(2)}) collective-permute-start(bf16[3,256,1024]{2,1,0:T(8,128)(2,1)} %get-tuple-element.39), channel_id=1, source_target_pairs={{0,1},{1,0},{2,3},{3,2},{4,5},{5,4},{6,7},{7,6},{8,9},{9,8},{10,11... | collective-permute-start | bytes 4718600 | tf_op jit(solution)/shard_map/ppermute | solution.py:27
  123.6 45.6 %collective-permute-start.16 = (bf16[3,256,1024]{2,1,0:T(8,128)(2,1)}, bf16[3,256,1024]{2,1,0:T(8,128)(2,1)}, u32[]{:S(2)}, u32[]{:S(2)}) collective-permute-start(bf16[3,256,1024]{2,1,0:T(8,128)(2,1)} %collective-permute-done.11.refs_7_.refs_5_), channel_id=1, source_target_pairs={{0,16},{8,24},{16,0},{24,8},{1,17},{9,25},{17,1},{25,9},{2,18},{10... | collective-permute-start | bytes 4718600 | tf_op jit(solution)/shard_map/ppermute | solution.py:27
  147.5 78.0 %collective-permute-start.9 = (bf16[512,2048]{1,0:T(8,128)(2,1)}, bf16[512,2048]{1,0:T(8,128)(2,1)S(1)}, u32[]{:S(2)}, u32[]{:S(2)}) collective-permute-start(bf16[512,2048]{1,0:T(8,128)(2,1)} %get-tuple-element.36), channel_id=1, source_target_pairs={{2,4},{4,2},{3,5},{5,3},{10,12},{12,10},{11,13},{13,11},{18,20},{2... | collective-permute-start | bytes 6291464 | tf_op jit(solution)/shard_map/ppermute | solution.py:586
  156.6 35.7 %collective-permute-start.20 = (bf16[3,256,1024]{2,1,0:T(8,128)(2,1)}, bf16[3,256,1024]{2,1,0:T(8,128)(2,1)S(1)}, u32[]{:S(2)}, u32[]{:S(2)}) collective-permute-start(bf16[3,256,1024]{2,1,0:T(8,128)(2,1)} %collective-permute-done.12.refs_5_.refs_6_), channel_id=1, source_target_pairs={{0,16},{8,24},{16,0},{24,8},{1,17},{9,25},{17,1},{25,9},{2,18},{10... | collective-permute-start | bytes 4718600 | tf_op jit(solution)/shard_map/ppermute | solution.py:27
  166.3 27.5 %collective-permute-start.13 = (bf16[3,256,1024]{2,1,0:T(8,128)(2,1)}, bf16[3,256,1024]{2,1,0:T(8,128)(2,1)S(1)}, u32[]{:S(2)}, u32[]{:S(2)}) collective-permute-start(bf16[3,256,1024]{2,1,0:T(8,128)(2,1)} %collective-permute-done.11.refs_7_.refs_5_), channel_id=1, source_target_pairs={{0,8},{8,0},{16,24},{24,16},{1,9},{9,1},{17,25},{25,17},{2,10},{10... | collective-permute-start | bytes 4718600 | tf_op jit(solution)/shard_map/ppermute | solution.py:27
  169.2 26.9 %collective-permute-start.17 = (bf16[3,256,1024]{2,1,0:T(8,128)(2,1)}, bf16[3,256,1024]{2,1,0:T(8,128)(2,1)S(1)}, u32[]{:S(2)}, u32[]{:S(2)}) collective-permute-start(bf16[3,256,1024]{2,1,0:T(8,128)(2,1)} %collective-permute-done.16.refs_13_), channel_id=1, source_target_pairs={{0,8},{8,0},{16,24},{24,16},{1,9},{9,1},{17,25},{25,17},{2,10},{10... | collective-permute-start | bytes 4718600 | tf_op jit(solution)/shard_map/ppermute | solution.py:27
  192.4 33.0 %copy-start.13 = (bf16[3,256,1024]{2,1,0:T(8,128)(2,1)}, bf16[3,256,1024]{2,1,0:T(8,128)(2,1)S(1)}, u32[]{:S(2)}) copy-start(bf16[3,256,1024]{2,1,0:T(8,128)(2,1)S(1)} %collective-permute-done.20.refs_7_.refs_14_) | copy-start | bytes 4718596
  192.4 37.4 %collective-permute-start.27 = (bf16[256,2048]{1,0:T(8,128)(2,1)}, bf16[256,2048]{1,0:T(8,128)(2,1)S(1)}, u32[]{:S(2)}, u32[]{:S(2)}) collective-permute-start(bf16[256,2048]{1,0:T(8,128)(2,1)} %get-tuple-element.71), channel_id=1, source_target_pairs={{2,0},{4,6},{3,1},{5,7},{10,8},{12,14},{11,9},{13,15},{18,16},{20,... | collective-permute-start | bytes 3145736 | tf_op jit(solution)/shard_map/ppermute | solution.py:619
  193.7 69.4 %collective-permute-start.25 = (bf16[256,2048]{1,0:T(8,128)(2,1)}, bf16[256,2048]{1,0:T(8,128)(2,1)}, u32[]{:S(2)}, u32[]{:S(2)}) collective-permute-start(bf16[256,2048]{1,0:T(8,128)(2,1)} %get-tuple-element.72), channel_id=1, source_target_pairs={{2,0},{4,6},{3,1},{5,7},{10,8},{12,14},{11,9},{13,15},{18,16},{20,... | collective-permute-start | bytes 3145736 | tf_op jit(solution)/shard_map/ppermute | solution.py:619
  223.2 8.8 %copy-start.18 = (f32[512,16]{0,1:T(8,128)S(1)}, f32[512,16]{0,1:T(8,128)}, u32[]{:S(2)}) copy-start(f32[512,16]{0,1:T(8,128)} %param.8) | copy-start | bytes 98308
  223.3 11.8 %collective-permute-start.19 = (bf16[3,256,1024]{2,1,0:T(8,128)(2,1)}, bf16[3,256,1024]{2,1,0:T(8,128)(2,1)}, u32[]{:S(2)}, u32[]{:S(2)}) collective-permute-start(bf16[3,256,1024]{2,1,0:T(8,128)(2,1)} %collective-permute-done.12.refs_5_.refs_6_), channel_id=1, source_target_pairs={{0,8},{8,0},{16,24},{24,16},{1,9},{9,1},{17,25},{25,17},{2,10},{10... | collective-permute-start | bytes 4718600 | tf_op jit(solution)/shard_map/ppermute | solution.py:27
  225.4 9.7 %collective-permute-start.21 = (bf16[3,256,1024]{2,1,0:T(8,128)(2,1)S(1)}, bf16[3,256,1024]{2,1,0:T(8,128)(2,1)}, u32[]{:S(2)}, u32[]{:S(2)}) collective-permute-start(bf16[3,256,1024]{2,1,0:T(8,128)(2,1)S(1)} %collective-permute-done.20.refs_7_.refs_14_), channel_id=1, source_target_pairs={{0,8},{8,0},{16,24},{24,16},{1,9},{9,1},{17,25},{25,17},{2,10},{10... | collective-permute-start | bytes 4718600 | tf_op jit(solution)/shard_map/ppermute | solution.py:27
  227.5 45.5 %collective-permute-start.23 = (bf16[256,2048]{1,0:T(8,128)(2,1)}, bf16[256,2048]{1,0:T(8,128)(2,1)}, u32[]{:S(2)}, u32[]{:S(2)}) collective-permute-start(bf16[256,2048]{1,0:T(8,128)(2,1)} %get-tuple-element.73), channel_id=1, source_target_pairs={{2,0},{4,6},{3,1},{5,7},{10,8},{12,14},{11,9},{13,15},{18,16},{20,... | collective-permute-start | bytes 3145736 | tf_op jit(solution)/shard_map/ppermute | solution.py:619
  229.7 23.9 %copy-start.17 = (bf16[256,2048]{1,0:T(8,128)(2,1)}, bf16[256,2048]{1,0:T(8,128)(2,1)S(1)}, u32[]{:S(2)}) copy-start(bf16[256,2048]{1,0:T(8,128)(2,1)S(1)} %collective-permute-done.27.refs_1_) | copy-start | bytes 3145732
  229.8 52.7 %collective-permute-start.10 = (bf16[256,2048]{1,0:T(8,128)(2,1)}, bf16[256,2048]{1,0:T(8,128)(2,1)}, u32[]{:S(2)}, u32[]{:S(2)}) collective-permute-start(bf16[256,2048]{1,0:T(8,128)(2,1)} %get-tuple-element.74), channel_id=1, source_target_pairs={{2,0},{4,6},{3,1},{5,7},{10,8},{12,14},{11,9},{13,15},{18,16},{20,... | collective-permute-start | bytes 3145736 | tf_op jit(solution)/shard_map/ppermute | solution.py:619
  262.5 33.7 %collective-permute-start.28 = (bf16[2,256,512]{2,1,0:T(8,128)(2,1)}, bf16[2,256,512]{2,1,0:T(8,128)(2,1)S(1)}, u32[]{:S(2)}, u32[]{:S(2)}) collective-permute-start(bf16[2,256,512]{2,1,0:T(8,128)(2,1)} %get-tuple-element.56), channel_id=1, source_target_pairs={{0,1},{1,0},{2,3},{3,2},{4,5},{5,4},{6,7},{7,6},{8,9},{9,8},{10,11... | collective-permute-start | bytes 1572872 | tf_op jit(solution)/shard_map/ppermute | solution.py:27
  272.0 27.3 %collective-permute-start.26 = (bf16[2,256,512]{2,1,0:T(8,128)(2,1)}, bf16[2,256,512]{2,1,0:T(8,128)(2,1)S(1)}, u32[]{:S(2)}, u32[]{:S(2)}) collective-permute-start(bf16[2,256,512]{2,1,0:T(8,128)(2,1)} %get-tuple-element.53), channel_id=1, source_target_pairs={{0,1},{1,0},{2,3},{3,2},{4,5},{5,4},{6,7},{7,6},{8,9},{9,8},{10,11... | collective-permute-start | bytes 1572872 | tf_op jit(solution)/shard_map/ppermute | solution.py:27
  281.8 7.8 %copy-start.19 = (f32[512,16]{0,1:T(8,128)S(1)}, f32[512,16]{0,1:T(8,128)}, u32[]{:S(2)}) copy-start(f32[512,16]{0,1:T(8,128)} %param.9) | copy-start | bytes 98308
  281.8 7.8 %copy-start.20 = (f32[512]{0:T(512)S(1)}, f32[512]{0:T(512)}, u32[]{:S(2)}) copy-start(f32[512]{0:T(512)} %param.10) | copy-start | bytes 6148
  281.9 20.6 %collective-permute-start.24 = (bf16[2,256,512]{2,1,0:T(8,128)(2,1)}, bf16[2,256,512]{2,1,0:T(8,128)(2,1)S(1)}, u32[]{:S(2)}, u32[]{:S(2)}) collective-permute-start(bf16[2,256,512]{2,1,0:T(8,128)(2,1)} %get-tuple-element.51), channel_id=1, source_target_pairs={{0,1},{1,0},{2,3},{3,2},{4,5},{5,4},{6,7},{7,6},{8,9},{9,8},{10,11... | collective-permute-start | bytes 1572872 | tf_op jit(solution)/shard_map/ppermute | solution.py:27
  288.7 20.9 %collective-permute-start.22 = (bf16[2,256,512]{2,1,0:T(8,128)(2,1)}, bf16[2,256,512]{2,1,0:T(8,128)(2,1)S(1)}, u32[]{:S(2)}, u32[]{:S(2)}) collective-permute-start(bf16[2,256,512]{2,1,0:T(8,128)(2,1)} %project.5), channel_id=1, source_target_pairs={{0,1},{1,0},{2,3},{3,2},{4,5},{5,4},{6,7},{7,6},{8,9},{9,8},{10,11... | collective-permute-start | bytes 1572872 | tf_op jit(solution)/shard_map/ppermute | solution.py:27
  289.7 6.5 %copy-start.1 = (bf16[3,256,512]{2,1,0:T(8,128)(2,1)S(1)}, bf16[3,256,512]{2,1,0:T(8,128)(2,1)}, u32[]{:S(2)}) copy-start(bf16[3,256,512]{2,1,0:T(8,128)(2,1)} %get-tuple-element.55.kept.refs_10_) | copy-start | bytes 2359300
  296.2 3.1 copy-start.2
  296.2 6.2 %copy-start.3 = (bf16[3,256,512]{2,1,0:T(8,128)(2,1)S(1)}, bf16[3,256,512]{2,1,0:T(8,128)(2,1)}, u32[]{:S(2)}) copy-start(bf16[3,256,512]{2,1,0:T(8,128)(2,1)} %get-tuple-element.50.kept.refs_12_) | copy-start | bytes 2359300
  299.3 10.3 %copy-start = (bf16[3,256,512]{2,1,0:T(8,128)(2,1)S(1)}, bf16[3,256,512]{2,1,0:T(8,128)(2,1)}, u32[]{:S(2)}) copy-start(bf16[3,256,512]{2,1,0:T(8,128)(2,1)} %project.6.kept.refs_13_) | copy-start | bytes 2359300
  302.4 16.8 %copy-start.4 = (f32[4,2,16,8,128]{4,3,2,1,0:T(8,128)S(1)}, f32[4,2,16,8,128]{4,3,2,1,0:T(8,128)}, u32[]{:S(2)}) copy-start(f32[4,2,16,8,128]{4,3,2,1,0:T(8,128)} %carry.1.refs_4_) | copy-start | bytes 1572868
  302.4 16.8 %copy-start.5 = (s32[3]{0:T(128)S(1)}, s32[3]{0:T(128)}, u32[]{:S(2)}) copy-start(s32[3]{0:T(128)} %pad_add_fusion.place) | copy-start | bytes 40
  312.7 3.0 collective-permute-start.29
  314.0 3.7 %collective-permute-start.30 = (f32[16,8,128]{2,1,0:T(8,128)S(1)}, f32[16,8,128]{2,1,0:T(8,128)S(1)}, u32[]{:S(2)}, u32[]{:S(2)}) collective-permute-start(f32[16,8,128]{2,1,0:T(8,128)S(1)} %get-tuple-element.60.refs_0_), channel_id=1, source_target_pairs={{0,16},{8,24},{16,0},{24,8},{1,17},{9,25},{17,1},{25,9},{2,18},{10... | collective-permute-start | bytes 196616 | tf_op jit(solution)/shard_map/ppermute | solution.py:27
  315.2 4.0 %collective-permute-start.31 = (f32[16,8,128]{2,1,0:T(8,128)S(1)}, f32[16,8,128]{2,1,0:T(8,128)S(1)}, u32[]{:S(2)}, u32[]{:S(2)}) collective-permute-start(f32[16,8,128]{2,1,0:T(8,128)S(1)} %get-tuple-element.60.refs_0_), channel_id=1, source_target_pairs={{0,24},{8,16},{16,8},{24,0},{1,25},{9,17},{17,9},{25,1},{2,26},{10... | collective-permute-start | bytes 196616 | tf_op jit(solution)/shard_map/ppermute | solution.py:27
  (5 other events, 7.8 us)

commit v3 on v1

--- a/solution.py
+++ b/solution.py
@@ -355,7 +355,7 @@
         local_ref[t] = total[0] + direct * p
         return tuple(new)
 
-    states = lax.fori_loop(0, rows, step, tuple(state_in[r] for r in range(poles)), unroll=8)
+    states = lax.fori_loop(0, rows, step, tuple(state_in[r] for r in range(poles)), unroll=16)
     for r in range(poles):
         state_out[r] = states[r]
 
@@ -441,7 +441,7 @@
             conv[t] = total[0] + locals_[k][t]
             return tuple(new)
 
-        states = lax.fori_loop(0, rows, step, states, unroll=8)
+        states = lax.fori_loop(0, rows, step, states, unroll=16)
         for side, ref in enumerate((kept[k], given[k])):
             segment = pair if side == 0 else 1 - pair
             column = pl.multiple_of(segment * seg_len + base, 128)

time: 330 us -> 329 us (level)
  no operation moved by 1% of the time
where the time goes in v3:
time: 329 us; the launch traced here: 328 us
  waiting for transfers between devices  132 us (40%)
  Pallas kernels  128 us (39%)
  starting transfers between devices  48.4 us (15%)
  local copies, waits for them, and re-layouts  18.3 us (6%)
    ppermute x23, waiting for transfers between devices, exchanged(): return lax.ppermute(block, axis, [(i, i ^ mask) for i in range(count)])  116 us
    pallas_call x8, Pallas kernels, project(): pl.pallas_call(functools.partial(project_kernel, plan, len(inputs), len(p...  105 us
    ppermute x23, starting transfers between devices, exchanged(): return lax.ppermute(block, axis, [(i, i ^ mask) for i in range(count)])  27.4 us
    pallas_call x4, Pallas kernels, scan(): pl.pallas_call(scan_kernel, in_specs=[local] * 6, out_specs=[local] * 2,...  11.8 us
    pallas_call x1, Pallas kernels, finish(): pl.pallas_call(functools.partial(finish_kernel, len(ends), n_chunks, seg_...  9.28 us
    ppermute x1, waiting for transfers between devices, per_device(): far_middle = [lax.ppermute(block, 'tp', [(1, 2), (2, 1)])]  8.42 us
    ppermute x4, starting transfers between devices, per_device(): last = lax.ppermute(block, 'tp', [(1, 0), (2, 3)])  8.18 us
  transfers between devices with their start and end apart: 32, of which 13 were waited for; matrix products, arithmetic and copies ran while one was open for 5% of the time, Pallas kernels for 35%

profile of v3, /device:TPU:9, one launch (start us, length us, event | category | flops | bytes accessed | tf_op | source)
XLA Modules:
  0.0 328.4 jit_solution(12051379902780368533)
XLA Ops:
  0.0 4.5 %collective-permute-start.14 = (bf16[1024,2048]{1,0:T(8,128)(2,1)}, bf16[1024,2048]{1,0:T(8,128)(2,1)}, u32[]{:S(2)}, u32[]{:S(2)}) collective-permute-start(bf16[1024,2048]{1,0:T(8,128)(2,1)} %refs_0_.5), channel_id=1, source_target_pairs={{2,4},{4,2},{3,5},{5,3},{10,12},{12,10},{11,13},{13,11},{18,20},{2... | collective-permute-start | bytes 12582920 | tf_op jit(solution)/shard_map/ppermute | solution.py:496
  4.5 4.8 %dynamic-slice_bitcast_fusion = (bf16[3,256,1024]{2,1,0:T(8,128)(2,1)}, bf16[3,256,1024]{2,1,0:T(8,128)(2,1)S(1)}, bf16[3,256,1024]{2,1,0:T(8,128)(2,1)S(1)}, bf16[3,256,1024]{2,1,0:T(8,128)(2,1)S(1)}) fusion(bf16[4096,3,1024]{2,0,1:T(8,128)(2,1)} %param.7, s32[]{:T(128)S(6)} %select_n.15, s32[]{:T(128)S(6)} %select_n.13, s32[]{:T(128)S(6)} %select_n.12, ...), kind=kLoop, calls=%fused_computation | loop fusion | bytes 12582928 | tf_op jit(solution)/shard_map/dynamic_slice | solution.py:527
  9.3 1.2 collective-permute-start.1
  10.7 33.3 %collective-permute-done.1.refs_3_.refs_5_ = bf16[3,256,1024]{2,1,0:T(8,128)(2,1)S(1)} collective-permute-done((bf16[3,256,1024]{2,1,0:T(8,128)(2,1)S(1)}, bf16[3,256,1024]{2,1,0:T(8,128)(2,1)S(1)}, u32[]{:S(2)}, u32[]{:S(2)}) %collective-permute-start.1) | collective-permute-done | bytes 1572896 | tf_op jit(solution)/shard_map/ppermute | solution.py:27
  44.0 3.8 %collective-permute-start.3 = (bf16[3,256,1024]{2,1,0:T(8,128)(2,1)S(1)}, bf16[3,256,1024]{2,1,0:T(8,128)(2,1)S(1)}, u32[]{:S(2)}, u32[]{:S(2)}) collective-permute-start(bf16[3,256,1024]{2,1,0:T(8,128)(2,1)S(1)} %collective-permute-done.1.refs_3_.refs_5_), channel_id=1, source_target_pairs={{0,8},{8,0},{16,24},{24,16},{1,9},{9,1},{17,25},{25,17},{2,10},{10... | collective-permute-start | bytes 4718600 | tf_op jit(solution)/shard_map/ppermute | solution.py:27
  47.8 1.2 collective-permute-start.5
  49.1 28.7 %collective-permute-done.2.refs_4_.refs_6_ = bf16[3,256,1024]{2,1,0:T(8,128)(2,1)S(1)} collective-permute-done((bf16[3,256,1024]{2,1,0:T(8,128)(2,1)S(1)}, bf16[3,256,1024]{2,1,0:T(8,128)(2,1)S(1)}, u32[]{:S(2)}, u32[]{:S(2)}) %collective-permute-start.2) | collective-permute-done | bytes 1572896 | tf_op jit(solution)/shard_map/ppermute | solution.py:27
  79.0 5.0 %collective-permute-done.5.refs_7_.refs_11_ = bf16[3,256,1024]{2,1,0:T(8,128)(2,1)S(1)} collective-permute-done((bf16[3,256,1024]{2,1,0:T(8,128)(2,1)S(1)}, bf16[3,256,1024]{2,1,0:T(8,128)(2,1)S(1)}, u32[]{:S(2)}, u32[]{:S(2)}) %collective-permute-start.5) | collective-permute-done | bytes 1572896 | tf_op jit(solution)/shard_map/ppermute | solution.py:27
  85.0 1.2 collective-permute-start.11
  86.3 5.5 %collective-permute-done.refs_1_ = bf16[1024,2048]{1,0:T(8,128)(2,1)} collective-permute-done((bf16[1024,2048]{1,0:T(8,128)(2,1)}, bf16[1024,2048]{1,0:T(8,128)(2,1)}, u32[]{:S(2)}, u32[]{:S(2)}) %collective-permute-start) | collective-permute-done | bytes 4194336 | tf_op jit(solution)/shard_map/ppermute | solution.py:495
  91.8 1.5 collective-permute-start.4
  93.3 1.5 collective-permute-done.14.refs_2_
  94.8 3.4 %collective-permute-start.15 = (bf16[1024,2048]{1,0:T(8,128)(2,1)}, bf16[1024,2048]{1,0:T(8,128)(2,1)}, u32[]{:S(2)}, u32[]{:S(2)}) collective-permute-start(bf16[1024,2048]{1,0:T(8,128)(2,1)} %collective-permute-done.14.refs_2_), channel_id=1, source_target_pairs={{2,0},{4,6},{3,1},{5,7},{10,8},{12,14},{11,9},{13,15},{18,16},{20,... | collective-permute-start | bytes 12582920 | tf_op jit(solution)/shard_map/ppermute | solution.py:497
  98.1 4.8 %fusion = (bf16[512,2048]{1,0:T(8,128)(2,1)}, bf16[512,2048]{1,0:T(8,128)(2,1)}) fusion(bf16[1024,2048]{1,0:T(8,128)(2,1)} %collective-permute-done.refs_1_), kind=kLoop, calls=%fused_computation.10 | loop fusion | bytes 8388608 | tf_op jit(solution)/shard_map/slice | solution.py:498
  103.0 14.7 %collective-permute-done.6.refs_8_.refs_12_ = bf16[3,256,1024]{2,1,0:T(8,128)(2,1)} collective-permute-done((bf16[3,256,1024]{2,1,0:T(8,128)(2,1)S(1)}, bf16[3,256,1024]{2,1,0:T(8,128)(2,1)}, u32[]{:S(2)}, u32[]{:S(2)}) %collective-permute-start.6) | collective-permute-done | bytes 1572896 | tf_op jit(solution)/shard_map/ppermute | solution.py:27
  117.7 1.9 collective-permute-start.18
  121.2 1.2 collective-permute-start.12
  126.5 20.9 %part_a.1.refs_17_ = f32[3,1024,1024]{2,1,0:T(8,128)} custom-call(s32[3]{0:T(128)} %pad_add_fusion.place, bf16[1024,2048]{1,0:T(8,128)(2,1)} %refs_0_.5, bf16[1024,2048]{1,0:T(8,128)(2,1)} %collective-permute-done.refs_1_, bf16[3,4096,1024]{2,1,0:T(8,128)(2,1)} %bitcast.18, bf16[3,256,1024]{2,1,0:T(8,128)(2,1)} %copy-done.6, ...), custom_call_target="tpu_custom_call" | custom-call | tf_op jit(solution)/shard_map/part_a/pallas_call | solution.py:217
  147.5 3.1 collective-permute-start.9
  150.6 6.0 %collective-permute-done.12.refs_5_.refs_6_ = bf16[3,256,1024]{2,1,0:T(8,128)(2,1)} collective-permute-done((bf16[3,256,1024]{2,1,0:T(8,128)(2,1)}, bf16[3,256,1024]{2,1,0:T(8,128)(2,1)}, u32[]{:S(2)}, u32[]{:S(2)}) %collective-permute-start.12) | collective-permute-done | bytes 1572896 | tf_op jit(solution)/shard_map/ppermute | solution.py:27
  157.8 8.4 %collective-permute-done.18.refs_0_ = bf16[512,2048]{1,0:T(8,128)(2,1)} collective-permute-done((bf16[512,2048]{1,0:T(8,128)(2,1)}, bf16[512,2048]{1,0:T(8,128)(2,1)}, u32[]{:S(2)}, u32[]{:S(2)}) %collective-permute-start.18) | collective-permute-done | bytes 2097184 | tf_op jit(solution)/shard_map/ppermute | solution.py:499
  166.3 2.9 collective-permute-start.13
  169.2 3.1 fusion.1
  172.3 20.0 %collective-permute-done.20.refs_7_.refs_14_ = bf16[3,256,1024]{2,1,0:T(8,128)(2,1)S(1)} collective-permute-done((bf16[3,256,1024]{2,1,0:T(8,128)(2,1)}, bf16[3,256,1024]{2,1,0:T(8,128)(2,1)S(1)}, u32[]{:S(2)}, u32[]{:S(2)}) %collective-permute-start.20) | collective-permute-done | bytes 1572896 | tf_op jit(solution)/shard_map/ppermute | solution.py:27
  192.4 1.3 collective-permute-start.27
  193.7 2.3 collective-permute-start.25
  197.2 26.0 %part_b.1.refs_9_ = f32[3,1024,1024]{2,1,0:T(8,128)} custom-call(s32[3]{0:T(128)} %pad_add_fusion.place, bf16[1024,2048]{1,0:T(8,128)(2,1)} %refs_0_.5, bf16[1024,2048]{1,0:T(8,128)(2,1)} %collective-permute-done.refs_1_, bf16[1024,2048]{1,0:T(8,128)(2,1)} %collective-permute-done.14.refs_2_, bf16[1024,2048]{1,0:T(8,128)(2,1)} %collective-permute-done.15.refs_3_, ...), custom_call_target="tpu_custom_call" | custom-call | tf_op jit(solution)/shard_map/part_b/pallas_call | solution.py:217
  223.3 2.1 collective-permute-start.19
  225.5 1.8 fusion.2
  227.5 2.3 collective-permute-start.23
  229.8 2.3 collective-permute-start.10
  232.7 2.4 carry.1.refs_4_
  235.1 18.6 %part_c.1.refs_19_ = f32[3,1024,1024]{2,1,0:T(8,128)} custom-call(s32[3]{0:T(128)} %pad_add_fusion.place, bf16[1024,2048]{1,0:T(8,128)(2,1)} %refs_0_.5, bf16[1024,2048]{1,0:T(8,128)(2,1)} %collective-permute-done.refs_1_, bf16[1024,2048]{1,0:T(8,128)(2,1)} %collective-permute-done.14.refs_2_, bf16[1024,2048]{1,0:T(8,128)(2,1)} %collective-permute-done.15.refs_3_, ...), custom_call_target="tpu_custom_call" | custom-call | tf_op jit(solution)/shard_map/part_c/pallas_call | solution.py:217
  253.7 8.8 %project.9 = (bf16[3,256,512]{2,1,0:T(8,128)(2,1)}, bf16[2,256,512]{2,1,0:T(8,128)(2,1)}) custom-call(s32[3]{0:T(128)} %pad_add_fusion.place, bf16[512,2048]{1,0:T(8,128)(2,1)} %collective-permute-done.18.refs_0_, bf16[256,2048]{1,0:T(8,128)(2,1)} %copy-done.17, bf16[3,4096,1024]{2,1,0:T(8,128)(2,1)} %bitcast.21, bf16[3,256,1024]{2,1,0:T(8,128)(2,1)} %copy-done.6, ...), custom_call_target="tpu_custom_call" | custom-call | tf_op jit(solution)/shard_map/project/pallas_call | solution.py:217
  263.2 8.8 %project.8 = (bf16[3,256,512]{2,1,0:T(8,128)(2,1)}, bf16[2,256,512]{2,1,0:T(8,128)(2,1)}) custom-call(s32[3]{0:T(128)} %pad_add_fusion.place, bf16[512,2048]{1,0:T(8,128)(2,1)} %collective-permute-done.18.refs_0_, bf16[256,2048]{1,0:T(8,128)(2,1)} %collective-permute-done.25.refs_1_, bf16[3,4096,1024]{2,1,0:T(8,128)(2,1)} %bitcast.22, ...), custom_call_target="tpu_custom_call" | custom-call | tf_op jit(solution)/shard_map/project/pallas_call | solution.py:217
  273.0 8.8 %project.7 = (bf16[3,256,512]{2,1,0:T(8,128)(2,1)}, bf16[2,256,512]{2,1,0:T(8,128)(2,1)}) custom-call(s32[3]{0:T(128)} %pad_add_fusion.place, bf16[512,2048]{1,0:T(8,128)(2,1)} %copy-done.16, bf16[256,2048]{1,0:T(8,128)(2,1)} %collective-permute-done.23.refs_1_, bf16[3,4096,1024]{2,1,0:T(8,128)(2,1)} %bitcast.23, bf16[3,256,1024]{2,1,0:T(8,128)(2,1)} %copy-done.6, ...), custom_call_target="tpu_custom_call" | custom-call | tf_op jit(solution)/shard_map/project/pallas_call | solution.py:217
  282.5 6.2 %project.5 = bf16[2,256,512]{2,1,0:T(8,128)(2,1)} custom-call(s32[3]{0:T(128)} %pad_add_fusion.place, bf16[512,2048]{1,0:T(8,128)(2,1)} %copy-done.16, bf16[256,2048]{1,0:T(8,128)(2,1)} %collective-permute-done.10.refs_1_, bf16[3,4096,1024]{2,1,0:T(8,128)(2,1)} %bitcast.24, bf16[3,256,1024]{2,1,0:T(8,128)(2,1)} %copy-done.6, ...), custom_call_target="tpu_custom_call" | custom-call | tf_op jit(solution)/shard_map/project/pallas_call | solution.py:217
  289.7 6.5 %project.6.kept.refs_13_ = bf16[3,256,512]{2,1,0:T(8,128)(2,1)} custom-call(s32[3]{0:T(128)} %pad_add_fusion.place, bf16[512,2048]{1,0:T(8,128)(2,1)} %copy-done.16, bf16[256,2048]{1,0:T(8,128)(2,1)} %collective-permute-done.10.refs_1_, bf16[3,4096,1024]{2,1,0:T(8,128)(2,1)} %bitcast.25, bf16[3,256,1024]{2,1,0:T(8,128)(2,1)} %copy-done.6, ...), custom_call_target="tpu_custom_call" | custom-call | tf_op jit(solution)/shard_map/project/pallas_call | solution.py:217
  296.3 2.9 scan.4
  299.2 2.9 scan.5
  302.2 2.9 scan.6
  305.2 4.4 %collective-permute-done.22.given.refs_17_ = bf16[2,256,512]{2,1,0:T(8,128)(2,1)S(1)} collective-permute-done((bf16[2,256,512]{2,1,0:T(8,128)(2,1)}, bf16[2,256,512]{2,1,0:T(8,128)(2,1)S(1)}, u32[]{:S(2)}, u32[]{:S(2)}) %collective-permute-start.22) | collective-permute-done | bytes 524320 | tf_op jit(solution)/shard_map/ppermute | solution.py:27
  309.6 2.9 scan.7
  312.5 1.3 collective-permute-start.29
  313.9 1.2 collective-permute-start.30
  315.6 2.0 collective-permute-done.30.refs_2_
  317.5 1.6 collective-permute-done.31.refs_3_
  319.2 9.3 %finish.1 = bf16[512,2048]{1,0:T(8,128)(2,1)} custom-call(s32[3]{0:T(128)S(1)} %copy-done.5, f32[16,8,128]{2,1,0:T(8,128)S(1)} %get-tuple-element.60.refs_0_, f32[16,8,128]{2,1,0:T(8,128)S(1)} %collective-permute-done.29.refs_1_, f32[16,8,128]{2,1,0:T(8,128)S(1)} %collective-permute-done.30.refs_2_, f32[16,8,128]{2,1,0:T(8,128)S(1)} %collective-permute-done.31.refs_3_, ...), custom_call_target="tpu_custom_call" | custom-call | flops 33554432 | bytes 8388608 | tf_op jit(solution)/shard_map/finish/pallas_call | solution.py:463
  (84 shorter events, 15.3 us)
Async XLA Ops:
  0.0 91.8 %collective-permute-start = (bf16[1024,2048]{1,0:T(8,128)(2,1)}, bf16[1024,2048]{1,0:T(8,128)(2,1)}, u32[]{:S(2)}, u32[]{:S(2)}) collective-permute-start(bf16[1024,2048]{1,0:T(8,128)(2,1)} %refs_0_.5), channel_id=1, source_target_pairs={{0,2},{2,0},{4,6},{6,4},{1,3},{3,1},{5,7},{7,5},{8,10},{10,8},{12,... | collective-permute-start | bytes 12582920 | tf_op jit(solution)/shard_map/ppermute | solution.py:495
  0.0 94.8 %collective-permute-start.14 = (bf16[1024,2048]{1,0:T(8,128)(2,1)}, bf16[1024,2048]{1,0:T(8,128)(2,1)}, u32[]{:S(2)}, u32[]{:S(2)}) collective-permute-start(bf16[1024,2048]{1,0:T(8,128)(2,1)} %refs_0_.5), channel_id=1, source_target_pairs={{2,4},{4,2},{3,5},{5,3},{10,12},{12,10},{11,13},{13,11},{18,20},{2... | collective-permute-start | bytes 12582920 | tf_op jit(solution)/shard_map/ppermute | solution.py:496
  9.3 34.8 %collective-permute-start.1 = (bf16[3,256,1024]{2,1,0:T(8,128)(2,1)S(1)}, bf16[3,256,1024]{2,1,0:T(8,128)(2,1)S(1)}, u32[]{:S(2)}, u32[]{:S(2)}) collective-permute-start(bf16[3,256,1024]{2,1,0:T(8,128)(2,1)S(1)} %get-tuple-element.67), channel_id=1, source_target_pairs={{0,1},{1,0},{2,3},{3,2},{4,5},{5,4},{6,7},{7,6},{8,9},{9,8},{10,11... | collective-permute-start | bytes 4718600 | tf_op jit(solution)/shard_map/ppermute | solution.py:27
  10.5 67.2 %collective-permute-start.2 = (bf16[3,256,1024]{2,1,0:T(8,128)(2,1)S(1)}, bf16[3,256,1024]{2,1,0:T(8,128)(2,1)S(1)}, u32[]{:S(2)}, u32[]{:S(2)}) collective-permute-start(bf16[3,256,1024]{2,1,0:T(8,128)(2,1)S(1)} %get-tuple-element.66), channel_id=1, source_target_pairs={{0,1},{1,0},{2,3},{3,2},{4,5},{5,4},{6,7},{7,6},{8,9},{9,8},{10,11... | collective-permute-start | bytes 4718600 | tf_op jit(solution)/shard_map/ppermute | solution.py:27
  44.0 59.0 %copy-start.6 = (bf16[3,256,1024]{2,1,0:T(8,128)(2,1)}, bf16[3,256,1024]{2,1,0:T(8,128)(2,1)S(1)}, u32[]{:S(2)}) copy-start(bf16[3,256,1024]{2,1,0:T(8,128)(2,1)S(1)} %collective-permute-done.1.refs_3_.refs_5_) | copy-start | bytes 4718596
  44.0 34.9 %collective-permute-start.3 = (bf16[3,256,1024]{2,1,0:T(8,128)(2,1)S(1)}, bf16[3,256,1024]{2,1,0:T(8,128)(2,1)S(1)}, u32[]{:S(2)}, u32[]{:S(2)}) collective-permute-start(bf16[3,256,1024]{2,1,0:T(8,128)(2,1)S(1)} %collective-permute-done.1.refs_3_.refs_5_), channel_id=1, source_target_pairs={{0,8},{8,0},{16,24},{24,16},{1,9},{9,1},{17,25},{25,17},{2,10},{10... | collective-permute-start | bytes 4718600 | tf_op jit(solution)/shard_map/ppermute | solution.py:27
  47.8 36.1 %collective-permute-start.5 = (bf16[3,256,1024]{2,1,0:T(8,128)(2,1)S(1)}, bf16[3,256,1024]{2,1,0:T(8,128)(2,1)S(1)}, u32[]{:S(2)}, u32[]{:S(2)}) collective-permute-start(bf16[3,256,1024]{2,1,0:T(8,128)(2,1)S(1)} %collective-permute-done.1.refs_3_.refs_5_), channel_id=1, source_target_pairs={{0,16},{8,24},{16,0},{24,8},{1,17},{9,25},{17,1},{25,9},{2,18},{10... | collective-permute-start | bytes 4718600 | tf_op jit(solution)/shard_map/ppermute | solution.py:27
  77.7 25.3 %copy-start.7 = (bf16[3,256,1024]{2,1,0:T(8,128)(2,1)}, bf16[3,256,1024]{2,1,0:T(8,128)(2,1)S(1)}, u32[]{:S(2)}) copy-start(bf16[3,256,1024]{2,1,0:T(8,128)(2,1)S(1)} %collective-permute-done.2.refs_4_.refs_6_) | copy-start | bytes 4718596
  77.7 39.9 %collective-permute-start.6 = (bf16[3,256,1024]{2,1,0:T(8,128)(2,1)S(1)}, bf16[3,256,1024]{2,1,0:T(8,128)(2,1)}, u32[]{:S(2)}, u32[]{:S(2)}) collective-permute-start(bf16[3,256,1024]{2,1,0:T(8,128)(2,1)S(1)} %collective-permute-done.2.refs_4_.refs_6_), channel_id=1, source_target_pairs={{0,16},{8,24},{16,0},{24,8},{1,17},{9,25},{17,1},{25,9},{2,18},{10... | collective-permute-start | bytes 4718600 | tf_op jit(solution)/shard_map/ppermute | solution.py:27
  78.9 7.3 %copy-start.8 = (bf16[3,256,1024]{2,1,0:T(8,128)(2,1)}, bf16[3,256,1024]{2,1,0:T(8,128)(2,1)S(1)}, u32[]{:S(2)}) copy-start(bf16[3,256,1024]{2,1,0:T(8,128)(2,1)S(1)} %collective-permute-done.3.refs_5_.refs_8_.refs_7_) | copy-start | bytes 4718596
  84.0 19.0 %copy-start.9 = (bf16[3,256,1024]{2,1,0:T(8,128)(2,1)}, bf16[3,256,1024]{2,1,0:T(8,128)(2,1)S(1)}, u32[]{:S(2)}) copy-start(bf16[3,256,1024]{2,1,0:T(8,128)(2,1)S(1)} %collective-permute-done.5.refs_7_.refs_11_) | copy-start | bytes 4718596
  84.0 35.6 %collective-permute-start.7 = (bf16[3,256,1024]{2,1,0:T(8,128)(2,1)S(1)}, bf16[3,256,1024]{2,1,0:T(8,128)(2,1)S(1)}, u32[]{:S(2)}, u32[]{:S(2)}) collective-permute-start(bf16[3,256,1024]{2,1,0:T(8,128)(2,1)S(1)} %collective-permute-done.5.refs_7_.refs_11_), channel_id=1, source_target_pairs={{0,8},{8,0},{16,24},{24,16},{1,9},{9,1},{17,25},{25,17},{2,10},{10... | collective-permute-start | bytes 4718600 | tf_op jit(solution)/shard_map/ppermute | solution.py:27
  85.0 36.1 %collective-permute-start.11 = (bf16[3,256,1024]{2,1,0:T(8,128)(2,1)S(1)}, bf16[3,256,1024]{2,1,0:T(8,128)(2,1)}, u32[]{:S(2)}, u32[]{:S(2)}) collective-permute-start(bf16[3,256,1024]{2,1,0:T(8,128)(2,1)S(1)} %get-tuple-element.37), channel_id=1, source_target_pairs={{0,1},{1,0},{2,3},{3,2},{4,5},{5,4},{6,7},{7,6},{8,9},{9,8},{10,11... | collective-permute-start | bytes 4718600 | tf_op jit(solution)/shard_map/ppermute | solution.py:27
  91.8 30.7 %collective-permute-start.4 = (bf16[3,256,1024]{2,1,0:T(8,128)(2,1)S(1)}, bf16[3,256,1024]{2,1,0:T(8,128)(2,1)S(1)}, u32[]{:S(2)}, u32[]{:S(2)}) collective-permute-start(bf16[3,256,1024]{2,1,0:T(8,128)(2,1)S(1)} %collective-permute-done.2.refs_4_.refs_6_), channel_id=1, source_target_pairs={{0,8},{8,0},{16,24},{24,16},{1,9},{9,1},{17,25},{25,17},{2,10},{10... | collective-permute-start | bytes 4718600 | tf_op jit(solution)/shard_map/ppermute | solution.py:27
  94.8 101.3 %collective-permute-start.15 = (bf16[1024,2048]{1,0:T(8,128)(2,1)}, bf16[1024,2048]{1,0:T(8,128)(2,1)}, u32[]{:S(2)}, u32[]{:S(2)}) collective-permute-start(bf16[1024,2048]{1,0:T(8,128)(2,1)} %collective-permute-done.14.refs_2_), channel_id=1, source_target_pairs={{2,0},{4,6},{3,1},{5,7},{10,8},{12,14},{11,9},{13,15},{18,16},{20,... | collective-permute-start | bytes 12582920 | tf_op jit(solution)/shard_map/ppermute | solution.py:497
  117.7 48.6 %collective-permute-start.18 = (bf16[512,2048]{1,0:T(8,128)(2,1)}, bf16[512,2048]{1,0:T(8,128)(2,1)}, u32[]{:S(2)}, u32[]{:S(2)}) collective-permute-start(bf16[512,2048]{1,0:T(8,128)(2,1)} %get-tuple-element.69), channel_id=1, source_target_pairs={{2,4},{4,2},{3,5},{5,3},{10,12},{12,10},{11,13},{13,11},{18,20},{2... | collective-permute-start | bytes 6291464 | tf_op jit(solution)/shard_map/ppermute | solution.py:499
  119.6 2.8 copy-start.10
  119.6 5.8 %collective-permute-start.8 = (bf16[3,256,1024]{2,1,0:T(8,128)(2,1)}, bf16[3,256,1024]{2,1,0:T(8,128)(2,1)S(1)}, u32[]{:S(2)}, u32[]{:S(2)}) collective-permute-start(bf16[3,256,1024]{2,1,0:T(8,128)(2,1)} %collective-permute-done.6.refs_8_.refs_12_), channel_id=1, source_target_pairs={{0,8},{8,0},{16,24},{24,16},{1,9},{9,1},{17,25},{25,17},{2,10},{10... | collective-permute-start | bytes 4718600 | tf_op jit(solution)/shard_map/ppermute | solution.py:27
  121.2 35.5 %collective-permute-start.12 = (bf16[3,256,1024]{2,1,0:T(8,128)(2,1)}, bf16[3,256,1024]{2,1,0:T(8,128)(2,1)}, u32[]{:S(2)}, u32[]{:S(2)}) collective-permute-start(bf16[3,256,1024]{2,1,0:T(8,128)(2,1)} %get-tuple-element.39), channel_id=1, source_target_pairs={{0,1},{1,0},{2,3},{3,2},{4,5},{5,4},{6,7},{7,6},{8,9},{9,8},{10,11... | collective-permute-start | bytes 4718600 | tf_op jit(solution)/shard_map/ppermute | solution.py:27
  123.6 45.6 %collective-permute-start.16 = (bf16[3,256,1024]{2,1,0:T(8,128)(2,1)}, bf16[3,256,1024]{2,1,0:T(8,128)(2,1)}, u32[]{:S(2)}, u32[]{:S(2)}) collective-permute-start(bf16[3,256,1024]{2,1,0:T(8,128)(2,1)} %collective-permute-done.11.refs_7_.refs_5_), channel_id=1, source_target_pairs={{0,16},{8,24},{16,0},{24,8},{1,17},{9,25},{17,1},{25,9},{2,18},{10... | collective-permute-start | bytes 4718600 | tf_op jit(solution)/shard_map/ppermute | solution.py:27
  147.5 78.0 %collective-permute-start.9 = (bf16[512,2048]{1,0:T(8,128)(2,1)}, bf16[512,2048]{1,0:T(8,128)(2,1)S(1)}, u32[]{:S(2)}, u32[]{:S(2)}) collective-permute-start(bf16[512,2048]{1,0:T(8,128)(2,1)} %get-tuple-element.36), channel_id=1, source_target_pairs={{2,4},{4,2},{3,5},{5,3},{10,12},{12,10},{11,13},{13,11},{18,20},{2... | collective-permute-start | bytes 6291464 | tf_op jit(solution)/shard_map/ppermute | solution.py:571
  156.6 35.7 %collective-permute-start.20 = (bf16[3,256,1024]{2,1,0:T(8,128)(2,1)}, bf16[3,256,1024]{2,1,0:T(8,128)(2,1)S(1)}, u32[]{:S(2)}, u32[]{:S(2)}) collective-permute-start(bf16[3,256,1024]{2,1,0:T(8,128)(2,1)} %collective-permute-done.12.refs_5_.refs_6_), channel_id=1, source_target_pairs={{0,16},{8,24},{16,0},{24,8},{1,17},{9,25},{17,1},{25,9},{2,18},{10... | collective-permute-start | bytes 4718600 | tf_op jit(solution)/shard_map/ppermute | solution.py:27
  166.3 27.5 %collective-permute-start.13 = (bf16[3,256,1024]{2,1,0:T(8,128)(2,1)}, bf16[3,256,1024]{2,1,0:T(8,128)(2,1)S(1)}, u32[]{:S(2)}, u32[]{:S(2)}) collective-permute-start(bf16[3,256,1024]{2,1,0:T(8,128)(2,1)} %collective-permute-done.11.refs_7_.refs_5_), channel_id=1, source_target_pairs={{0,8},{8,0},{16,24},{24,16},{1,9},{9,1},{17,25},{25,17},{2,10},{10... | collective-permute-start | bytes 4718600 | tf_op jit(solution)/shard_map/ppermute | solution.py:27
  169.2 26.9 %collective-permute-start.17 = (bf16[3,256,1024]{2,1,0:T(8,128)(2,1)}, bf16[3,256,1024]{2,1,0:T(8,128)(2,1)S(1)}, u32[]{:S(2)}, u32[]{:S(2)}) collective-permute-start(bf16[3,256,1024]{2,1,0:T(8,128)(2,1)} %collective-permute-done.16.refs_13_), channel_id=1, source_target_pairs={{0,8},{8,0},{16,24},{24,16},{1,9},{9,1},{17,25},{25,17},{2,10},{10... | collective-permute-start | bytes 4718600 | tf_op jit(solution)/shard_map/ppermute | solution.py:27
  192.4 33.0 %copy-start.13 = (bf16[3,256,1024]{2,1,0:T(8,128)(2,1)}, bf16[3,256,1024]{2,1,0:T(8,128)(2,1)S(1)}, u32[]{:S(2)}) copy-start(bf16[3,256,1024]{2,1,0:T(8,128)(2,1)S(1)} %collective-permute-done.20.refs_7_.refs_14_) | copy-start | bytes 4718596
  192.4 37.4 %collective-permute-start.27 = (bf16[256,2048]{1,0:T(8,128)(2,1)}, bf16[256,2048]{1,0:T(8,128)(2,1)S(1)}, u32[]{:S(2)}, u32[]{:S(2)}) collective-permute-start(bf16[256,2048]{1,0:T(8,128)(2,1)} %get-tuple-element.71), channel_id=1, source_target_pairs={{2,0},{4,6},{3,1},{5,7},{10,8},{12,14},{11,9},{13,15},{18,16},{20,... | collective-permute-start | bytes 3145736 | tf_op jit(solution)/shard_map/ppermute | solution.py:604
  193.7 69.4 %collective-permute-start.25 = (bf16[256,2048]{1,0:T(8,128)(2,1)}, bf16[256,2048]{1,0:T(8,128)(2,1)}, u32[]{:S(2)}, u32[]{:S(2)}) collective-permute-start(bf16[256,2048]{1,0:T(8,128)(2,1)} %get-tuple-element.72), channel_id=1, source_target_pairs={{2,0},{4,6},{3,1},{5,7},{10,8},{12,14},{11,9},{13,15},{18,16},{20,... | collective-permute-start | bytes 3145736 | tf_op jit(solution)/shard_map/ppermute | solution.py:604
  223.2 8.8 %copy-start.18 = (f32[512,16]{0,1:T(8,128)S(1)}, f32[512,16]{0,1:T(8,128)}, u32[]{:S(2)}) copy-start(f32[512,16]{0,1:T(8,128)} %param.8) | copy-start | bytes 98308
  223.3 11.8 %collective-permute-start.19 = (bf16[3,256,1024]{2,1,0:T(8,128)(2,1)}, bf16[3,256,1024]{2,1,0:T(8,128)(2,1)}, u32[]{:S(2)}, u32[]{:S(2)}) collective-permute-start(bf16[3,256,1024]{2,1,0:T(8,128)(2,1)} %collective-permute-done.12.refs_5_.refs_6_), channel_id=1, source_target_pairs={{0,8},{8,0},{16,24},{24,16},{1,9},{9,1},{17,25},{25,17},{2,10},{10... | collective-permute-start | bytes 4718600 | tf_op jit(solution)/shard_map/ppermute | solution.py:27
  225.4 9.7 %collective-permute-start.21 = (bf16[3,256,1024]{2,1,0:T(8,128)(2,1)S(1)}, bf16[3,256,1024]{2,1,0:T(8,128)(2,1)}, u32[]{:S(2)}, u32[]{:S(2)}) collective-permute-start(bf16[3,256,1024]{2,1,0:T(8,128)(2,1)S(1)} %collective-permute-done.20.refs_7_.refs_14_), channel_id=1, source_target_pairs={{0,8},{8,0},{16,24},{24,16},{1,9},{9,1},{17,25},{25,17},{2,10},{10... | collective-permute-start | bytes 4718600 | tf_op jit(solution)/shard_map/ppermute | solution.py:27
  227.5 45.5 %collective-permute-start.23 = (bf16[256,2048]{1,0:T(8,128)(2,1)}, bf16[256,2048]{1,0:T(8,128)(2,1)}, u32[]{:S(2)}, u32[]{:S(2)}) collective-permute-start(bf16[256,2048]{1,0:T(8,128)(2,1)} %get-tuple-element.73), channel_id=1, source_target_pairs={{2,0},{4,6},{3,1},{5,7},{10,8},{12,14},{11,9},{13,15},{18,16},{20,... | collective-permute-start | bytes 3145736 | tf_op jit(solution)/shard_map/ppermute | solution.py:604
  229.7 23.9 %copy-start.17 = (bf16[256,2048]{1,0:T(8,128)(2,1)}, bf16[256,2048]{1,0:T(8,128)(2,1)S(1)}, u32[]{:S(2)}) copy-start(bf16[256,2048]{1,0:T(8,128)(2,1)S(1)} %collective-permute-done.27.refs_1_) | copy-start | bytes 3145732
  229.8 52.7 %collective-permute-start.10 = (bf16[256,2048]{1,0:T(8,128)(2,1)}, bf16[256,2048]{1,0:T(8,128)(2,1)}, u32[]{:S(2)}, u32[]{:S(2)}) collective-permute-start(bf16[256,2048]{1,0:T(8,128)(2,1)} %get-tuple-element.74), channel_id=1, source_target_pairs={{2,0},{4,6},{3,1},{5,7},{10,8},{12,14},{11,9},{13,15},{18,16},{20,... | collective-permute-start | bytes 3145736 | tf_op jit(solution)/shard_map/ppermute | solution.py:604
  262.5 33.7 %collective-permute-start.28 = (bf16[2,256,512]{2,1,0:T(8,128)(2,1)}, bf16[2,256,512]{2,1,0:T(8,128)(2,1)S(1)}, u32[]{:S(2)}, u32[]{:S(2)}) collective-permute-start(bf16[2,256,512]{2,1,0:T(8,128)(2,1)} %get-tuple-element.56), channel_id=1, source_target_pairs={{0,1},{1,0},{2,3},{3,2},{4,5},{5,4},{6,7},{7,6},{8,9},{9,8},{10,11... | collective-permute-start | bytes 1572872 | tf_op jit(solution)/shard_map/ppermute | solution.py:27
  272.0 27.2 %collective-permute-start.26 = (bf16[2,256,512]{2,1,0:T(8,128)(2,1)}, bf16[2,256,512]{2,1,0:T(8,128)(2,1)S(1)}, u32[]{:S(2)}, u32[]{:S(2)}) collective-permute-start(bf16[2,256,512]{2,1,0:T(8,128)(2,1)} %get-tuple-element.53), channel_id=1, source_target_pairs={{0,1},{1,0},{2,3},{3,2},{4,5},{5,4},{6,7},{7,6},{8,9},{9,8},{10,11... | collective-permute-start | bytes 1572872 | tf_op jit(solution)/shard_map/ppermute | solution.py:27
  281.8 7.8 %copy-start.19 = (f32[512,16]{0,1:T(8,128)S(1)}, f32[512,16]{0,1:T(8,128)}, u32[]{:S(2)}) copy-start(f32[512,16]{0,1:T(8,128)} %param.9) | copy-start | bytes 98308
  281.8 7.8 %copy-start.20 = (f32[512]{0:T(512)S(1)}, f32[512]{0:T(512)}, u32[]{:S(2)}) copy-start(f32[512]{0:T(512)} %param.10) | copy-start | bytes 6148
  281.9 20.4 %collective-permute-start.24 = (bf16[2,256,512]{2,1,0:T(8,128)(2,1)}, bf16[2,256,512]{2,1,0:T(8,128)(2,1)S(1)}, u32[]{:S(2)}, u32[]{:S(2)}) collective-permute-start(bf16[2,256,512]{2,1,0:T(8,128)(2,1)} %get-tuple-element.51), channel_id=1, source_target_pairs={{0,1},{1,0},{2,3},{3,2},{4,5},{5,4},{6,7},{7,6},{8,9},{9,8},{10,11... | collective-permute-start | bytes 1572872 | tf_op jit(solution)/shard_map/ppermute | solution.py:27
  288.7 20.9 %collective-permute-start.22 = (bf16[2,256,512]{2,1,0:T(8,128)(2,1)}, bf16[2,256,512]{2,1,0:T(8,128)(2,1)S(1)}, u32[]{:S(2)}, u32[]{:S(2)}) collective-permute-start(bf16[2,256,512]{2,1,0:T(8,128)(2,1)} %project.5), channel_id=1, source_target_pairs={{0,1},{1,0},{2,3},{3,2},{4,5},{5,4},{6,7},{7,6},{8,9},{9,8},{10,11... | collective-permute-start | bytes 1572872 | tf_op jit(solution)/shard_map/ppermute | solution.py:27
  289.7 6.5 %copy-start.1 = (bf16[3,256,512]{2,1,0:T(8,128)(2,1)S(1)}, bf16[3,256,512]{2,1,0:T(8,128)(2,1)}, u32[]{:S(2)}) copy-start(bf16[3,256,512]{2,1,0:T(8,128)(2,1)} %get-tuple-element.55.kept.refs_10_) | copy-start | bytes 2359300
  296.2 3.0 copy-start.2
  296.2 6.0 %copy-start.3 = (bf16[3,256,512]{2,1,0:T(8,128)(2,1)S(1)}, bf16[3,256,512]{2,1,0:T(8,128)(2,1)}, u32[]{:S(2)}) copy-start(bf16[3,256,512]{2,1,0:T(8,128)(2,1)} %get-tuple-element.50.kept.refs_12_) | copy-start | bytes 2359300
  299.2 10.4 %copy-start = (bf16[3,256,512]{2,1,0:T(8,128)(2,1)S(1)}, bf16[3,256,512]{2,1,0:T(8,128)(2,1)}, u32[]{:S(2)}) copy-start(bf16[3,256,512]{2,1,0:T(8,128)(2,1)} %project.6.kept.refs_13_) | copy-start | bytes 2359300
  302.2 17.0 %copy-start.4 = (f32[4,2,16,8,128]{4,3,2,1,0:T(8,128)S(1)}, f32[4,2,16,8,128]{4,3,2,1,0:T(8,128)}, u32[]{:S(2)}) copy-start(f32[4,2,16,8,128]{4,3,2,1,0:T(8,128)} %carry.1.refs_4_) | copy-start | bytes 1572868
  302.2 17.0 %copy-start.5 = (s32[3]{0:T(128)S(1)}, s32[3]{0:T(128)}, u32[]{:S(2)}) copy-start(s32[3]{0:T(128)} %pad_add_fusion.place) | copy-start | bytes 40
  312.5 3.0 collective-permute-start.29
  313.9 3.7 %collective-permute-start.30 = (f32[16,8,128]{2,1,0:T(8,128)S(1)}, f32[16,8,128]{2,1,0:T(8,128)S(1)}, u32[]{:S(2)}, u32[]{:S(2)}) collective-permute-start(f32[16,8,128]{2,1,0:T(8,128)S(1)} %get-tuple-element.60.refs_0_), channel_id=1, source_target_pairs={{0,16},{8,24},{16,0},{24,8},{1,17},{9,25},{17,1},{25,9},{2,18},{10... | collective-permute-start | bytes 196616 | tf_op jit(solution)/shard_map/ppermute | solution.py:27
  315.1 4.0 %collective-permute-start.31 = (f32[16,8,128]{2,1,0:T(8,128)S(1)}, f32[16,8,128]{2,1,0:T(8,128)S(1)}, u32[]{:S(2)}, u32[]{:S(2)}) collective-permute-start(f32[16,8,128]{2,1,0:T(8,128)S(1)} %get-tuple-element.60.refs_0_), channel_id=1, source_target_pairs={{0,24},{8,16},{16,8},{24,0},{1,25},{9,17},{17,9},{25,1},{2,26},{10... | collective-permute-start | bytes 196616 | tf_op jit(solution)/shard_map/ppermute | solution.py:27
  (5 other events, 7.8 us)
